TPU v7x, 512 devices: a whole 4x4x16 slice. The times are simulated.
512 devices in a mesh: ctx: 64 (over x, z), tp: 8 (over y, core).
Axes of the slice: x: 4, y: 4, z: 16, core: 2. Of those that a mesh axis runs over, the one named last changes fastest.
Arguments:
- x_input: bfloat16 [8192, 8192], P('ctx', 'tp'), may hold values from -6 to 6
- b_input: bfloat16 [8192, 1024], P('ctx', 'tp'), may hold values from -6 to 6
- c_input: bfloat16 [8192, 1024], P('ctx', 'tp'), may hold values from -0.59765625 to 0.59765625
- step: float32 [128, 8192], P('tp', 'ctx'), may hold values from 0.005 to 0.05
- log_decay: float32 [128, 8192], P('tp', 'ctx'), may hold values from -1 to 0, as said below
- skip: float32 [128], P('tp'), may hold values from 0.5 to 2
- gain: float32 [8192], P('tp'), may hold values from 0.1 to 1.9
- out_weight: bfloat16 [8192, 4096], P(('tp', 'ctx')), may hold values from -0.0625 to 0.0625
Outputs:
- mixed: bfloat16 [8192, 4096], P('ctx', 'tp')
Inputs may be any that keep to these rules, and one draw needn't show every extreme that they name: `log_decay`: each entry is the logarithm of a decay factor strictly between 0 and 1.
All inputs are finite; a program needn't handle non-finite values.
Results may differ from a plain program's by a relative error of at most 0.017.
Values may be sent and summed in bfloat16 or wider, within the bound.
No kernel may reach another device: no remote copies, remote signals or barrier semaphores. Data moves between devices by JAX's collectives and lax.ppermute only.
A program may use at most 128 MiB of HBM per device.

v0:
```python
import jax
import jax.numpy as jnp
from jax import lax
from jax.sharding import PartitionSpec as P

P_SIZE = 64
N = 128
SPAN = 128


def entering(array, axis, combine, identity):
    devices, mine = (lax.axis_size(axis), lax.axis_index(axis))
    everything = jax.tree.map(lambda part: lax.all_gather(part, axis), array)
    start = jax.tree.map(
        lambda part, zero: jnp.broadcast_to(jnp.asarray(zero, part.dtype), part.shape),
        array,
        identity,
    )

    def hop(k, before):
        reached = k < mine
        new = combine(before, jax.tree.map(lambda part: part[k], everything))
        return jax.tree.map(lambda a, b: jnp.where(reached, a, b), new, before)

    return lax.fori_loop(0, devices, hop, start)


def final_state(grouped, b_rows, tail):
    weighted = (grouped.astype(jnp.float32) * jnp.transpose(tail, (2, 0, 1))[..., None]).astype(
        jnp.bfloat16
    )
    return jnp.einsum("jgkp,jgn->gkpn", weighted, b_rows, preferred_element_type=jnp.float32)


def span_step(state, block):
    values, b_rows, c_rows, steps, logs = block
    length = values.shape[0]
    width = values.shape[1]
    depth = values.shape[2]
    groups = b_rows.shape[1]
    per_group = width // groups
    cumul = jnp.cumsum(logs, axis=-1)
    within = jnp.tril(jnp.ones((length, length), dtype=bool))
    spread = cumul[:, :, None] - cumul[:, None, :]
    decay_mat = jnp.exp(jnp.where(within[None], spread, -jnp.inf))
    common_region = jnp.einsum("ign,jgn->gij", c_rows, b_rows, preferred_element_type=jnp.float32)
    mixing = (
        common_region[:, None]
        * decay_mat.reshape(groups, per_group, length, length)
        * steps.reshape(groups, per_group, 1, length)
    )
    mixing = mixing.astype(jnp.bfloat16)
    grouped = values.reshape(length, groups, per_group, depth)
    output = jnp.einsum("gkij,jgkp->igkp", mixing, grouped, preferred_element_type=jnp.float32)
    state_grp = state.reshape(groups, per_group, depth, state.shape[2])
    carried = jnp.einsum(
        "ign,gkpn->igkp", c_rows.astype(jnp.float32), state_grp, precision=lax.Precision.HIGHEST
    )
    scales = jnp.exp(cumul).reshape(groups, per_group, length).transpose(2, 0, 1)
    output = output + scales[..., None] * carried
    tail = (jnp.exp(cumul[:, -1:] - cumul) * steps).reshape(groups, per_group, length)
    fresh = final_state(grouped, b_rows, tail)
    updated_state = jnp.exp(cumul[:, -1])[:, None, None] * state + fresh.reshape(state.shape)
    return (updated_state, output.reshape(length, width, depth))


def split_blocks(values, b_rows, c_rows, steps, logs, span):
    total = values.shape[0]
    count = total // span
    width = values.shape[1]
    groups = b_rows.shape[1]
    return (
        values.reshape(count, span, width, values.shape[2]),
        b_rows.reshape(count, span, groups, b_rows.shape[2]),
        c_rows.reshape(count, span, groups, c_rows.shape[2]),
        steps.reshape(width, count, span).transpose(1, 0, 2),
        logs.reshape(width, count, span).transpose(1, 0, 2),
    )


def run_spans(values, b_rows, c_rows, steps, logs, start_state, span):
    blocks = split_blocks(values, b_rows, c_rows, steps, logs, span)
    final, outputs = lax.scan(span_step, start_state, blocks)
    return (final, outputs.reshape(values.shape))


def normalize(ssm, gain, groups):
    total = ssm.shape[0]
    grouped = ssm.reshape(total, groups, -1)
    meansq = jnp.mean(grouped * grouped, axis=-1, keepdims=True)
    normed = grouped * lax.rsqrt(meansq + 1e-05)
    return (normed.reshape(total, -1) * gain[None, :]).astype(jnp.bfloat16)


def combine(earlier, later):
    return (earlier[0] + later[0], jnp.exp(later[0])[:, None, None] * earlier[1] + later[1])


def carry_in(total, carried_digest):
    prefix = entering(
        (total, carried_digest),
        "ctx",
        combine,
        (jnp.zeros_like(total), jnp.zeros_like(carried_digest)),
    )
    return prefix[1]


def shards(x_input, b_input, c_input, step, log_decay, skip, gain, out_weight):
    rows = x_input.shape[0]
    heads = step.shape[0]
    groups = b_input.shape[1] // N
    per_group = heads // groups
    values = x_input.reshape(rows, heads, P_SIZE)
    b_rows = b_input.reshape(rows, groups, N)
    c_rows = c_input.reshape(rows, groups, N)
    empty_state = jnp.zeros((heads, P_SIZE, N), jnp.float32)
    cumul = jnp.cumsum(log_decay, axis=1)
    total = cumul[:, -1]
    carried_digest, ssm = run_spans(values, b_rows, c_rows, step, log_decay, empty_state, SPAN)
    incoming = carry_in(total, carried_digest)
    carried = jnp.einsum(
        "tgn,gkpn->tgkp",
        c_rows.astype(jnp.float32),
        incoming.reshape(groups, per_group, P_SIZE, N),
        precision=lax.Precision.HIGHEST,
    )
    scales = jnp.exp(cumul).reshape(groups, per_group, rows).transpose(2, 0, 1)
    ssm = ssm + (scales[..., None] * carried).reshape(rows, heads, P_SIZE)
    ssm = ssm + skip[None, :, None] * values.astype(jnp.float32)
    hidden = normalize(ssm, gain, groups)
    term = jnp.dot(
        hidden,
        lax.all_gather(out_weight, "ctx", axis=0, tiled=True),
        preferred_element_type=jnp.float32,
    )
    return lax.psum_scatter(term.astype(jnp.bfloat16), "tp", scatter_dimension=1, tiled=True)


def solution(mesh):
    in_specs = (
        P("ctx", "tp"),
        P("ctx", "tp"),
        P("ctx", "tp"),
        P("tp", "ctx"),
        P("tp", "ctx"),
        P("tp"),
        P("tp"),
        P(("tp", "ctx"), None),
    )
    out_specs = P("ctx", "tp")
    return jax.shard_map(shards, mesh=mesh, in_specs=in_specs, out_specs=out_specs, check_vma=False)
```

profile of v0, /device:TPU:1, one launch (start us, length us, event | category | flops | bytes accessed | tf_op | source)
XLA Modules:
  0.0 512.4 jit_solution(13044300048302130583)
XLA Ops:
  9.7 1.8 convolution_add_fusion
  12.4 1.3 dynamic-slice.2
  14.6 123.5 %all-reduce = f32[1024]{0:T(1024)S(1)} all-reduce(f32[1024]{0:T(1024)S(1)} %dynamic-update-slice), channel_id=2, replica_groups=mesh['ctx'=64,'tp'=8] {'ctx'}, use_global_device_ids=true, to_apply=%add | all-reduce | flops 1024 | bytes 8192
  140.2 170.1 %all-gather.7.cloned.1.call-done = f32[1024,64,128]{2,1,0:T(8,128)} async-done(((f32[16,64,128]{2,1,0:T(8,128)}), f32[1024,64,128]{2,1,0:T(8,128)}) %all-gather.7.cloned.1.call-update) | async-done | bytes 33554448 | tf_op jit(solution)/shard_map/all_gather | solution.py:13
  310.3 77.8 %while.9 = (s32[]{:T(128)}, f32[16,64,128]{2,1,0:T(8,128)S(1)}, s32[]{:T(128)}, f32[64,16]{1,0:T(8,128)S(1)}, f32[64,16,64,128]{3,2,1,0:T(8,128)}, /*index=5*/s32[]{:T(128)}, s32[]{:T(128)}) while((s32[]{:T(128)}, f32[16,64,128]{2,1,0:T(8,128)S(1)}, s32[]{:T(128)}, f32[64,16]{1,0:T(8,128)S(1)}, f32[64,16,64,128]{3,2,1,0:T(8,128)}, ...), condition=%wide.region_2.3_spmd.clone, body=%wide.region_1.2_spmd.clone.sunk | while | flops 524292 | bytes 1573161 | solution.py:25
  310.3 1.2 fusion.28
  312.7 1.2 fusion.28
  315.2 1.2 fusion.28
  316.4 1.2 fusion.28
  332.2 1.2 fusion.28
  335.8 1.2 fusion.28
  341.9 1.2 fusion.28
  348.0 1.2 fusion.28
  350.4 1.2 fusion.28
  354.1 1.2 fusion.28
  356.5 1.2 fusion.28
  362.6 1.2 fusion.28
  365.0 1.2 fusion.28
  367.5 1.2 fusion.28
  368.7 1.2 fusion.28
  369.9 1.2 fusion.28
  389.7 69.5 %all-gather.5.cloned.1.call-done = bf16[1024,4096]{1,0:T(8,128)(2,1)} async-done(((bf16[16,4096]{1,0:T(8,128)(2,1)}), bf16[1024,4096]{1,0:T(8,128)(2,1)}) %all-gather.5.cloned.1.call-update) | async-done | bytes 8388624 | tf_op jit(solution)/shard_map/all_gather | solution.py:134
  459.1 5.7 %convolution_convert_fusion = bf16[128,4096]{1,0:T(8,128)(2,1)} fusion(bf16[128,1024]{0,1:T(8,128)(2,1)S(1)} %multiply_convert_fusion.2, bf16[1024,4096]{1,0:T(8,128)(2,1)} %all-gather.5.cloned.1.call-done), kind=kOutput, calls=%fused_computation.3 | convolution fusion | flops 1074266112 | bytes 9699328 | tf_op jit(solution)/shard_map/dot_general | solution.py:132
  464.8 41.0 %reduce-scatter.2.cloned.1.call-done = bf16[128,512]{1,0:T(8,128)(2,1)} async-done(((bf16[128,4096]{1,0:T(8,128)(2,1)}), bf16[128,512]{1,0:T(8,128)(2,1)}) %reduce-scatter.2.cloned.1.call-update) | async-done | bytes 131088 | tf_op jit(solution)/shard_map/reduce_scatter | solution.py:137
  (144 shorter events, 64.9 us)
Async XLA Ops:
  6.5 131.6 %copy-start = (bf16[128,128]{1,0:T(8,128)(2,1)S(1)}, bf16[128,128]{1,0:T(8,128)(2,1)}, u32[]{:S(2)}) copy-start(bf16[128,128]{1,0:T(8,128)(2,1)} %param.12) | copy-start | bytes 98308
  6.5 382.0 %copy-start.1 = (f32[16,128]{1,0:T(8,128)S(1)}, f32[16,128]{1,0:T(8,128)}, u32[]{:S(2)}) copy-start(f32[16,128]{1,0:T(8,128)} %param.13) | copy-start | bytes 24580
  6.5 382.8 %copy-start.2 = (f32[1024]{0:T(1024)S(1)}, f32[1024]{0:T(1024)}, u32[]{:S(2)}) copy-start(f32[1024]{0:T(1024)} %param.16) | copy-start | bytes 12292
  6.5 303.7 %all-gather.7.cloned.1.call-start = ((), (), s32[]{:S(2)}) async-start(), calls=%async_computation.3 | async-start | bytes 34078720 | tf_op jit(solution)/shard_map/all_gather | solution.py:13
  11.5 447.6 %all-gather.5.cloned.1.call-start = ((), (), s32[]{:S(2)}) async-start(), calls=%async_computation.1 | async-start | bytes 8519680 | tf_op jit(solution)/shard_map/all_gather | solution.py:134
  12.3 493.6 %reduce-scatter.2.cloned.1.call-start = ((), (), s32[]{:S(2)}) async-start(), calls=%async_computation.2 | async-start | bytes 1179648 | tf_op jit(solution)/shard_map/reduce_scatter | solution.py:137
Sparse Core Ops, SparseCore 0:
  11.7 298.5 all-gather.6
  313.2 145.8 all-gather.4
  464.9 40.8 reduce-scatter.1
where the time goes:
time: 517 us; the launch traced here: 512 us
  waiting for transfers between devices  281 us (54%)
  blocking collectives  123 us (24%)
  other arithmetic  77.6 us (15%)
  between operations  13.9 us (3%)
  matrix products  9.66 us (2%)
    all_gather x1, waiting for transfers between devices, entering(): everything = jax.tree.map(lambda part: lax.all_gather(part, axis), array)  170 us
    unnamed x1, blocking collectives  123 us
    select_n x64, other arithmetic, hop(): return jax.tree.map(lambda a, b: jnp.where(reached, a, b), new, before)  75.1 us
    all_gather x1, waiting for transfers between devices, shards(): lax.all_gather(out_weight, 'ctx', axis=0, tiled=True)  69.5 us
    reduce_scatter x1, waiting for transfers between devices, shards(): lax.psum_scatter(term.astype(jnp.bfloat16), 'tp', scatter_dimension=1, ti...  41 us
  transfers between devices with their start and end apart: 3, of which 3 were waited for; matrix products, arithmetic and copies ran while one was open for 16% of the time, Pallas kernels for 0%

commit v1 on v0

v1 whole, which is shorter than its diff:
```python
import jax
import jax.numpy as jnp
from jax import lax
from jax.sharding import Mesh, PartitionSpec as P

NX, NZ, NY, NC = 4, 16, 4, 2
TOK = 128
HEADS = 16
P_SIZE = 64
N = 128
EXTRA = 16
f32 = jnp.float32
bf16 = jnp.bfloat16


def split3(value):
    high = lax.reduce_precision(value, 8, 7)
    rest = value - high
    middle = lax.reduce_precision(rest, 8, 7)
    low = lax.reduce_precision(rest - middle, 8, 7)
    return high, middle, low


def gather_x(part):
    return lax.all_to_all(
        jnp.broadcast_to(part[None], (NX,) + part.shape), "x", 0, 0, tiled=True
    )


def entering_states(fresh, total):
    pieces = jnp.stack(split3(total), axis=1)
    rows = jnp.concatenate([pieces, jnp.zeros((HEADS, EXTRA - 3), f32)], axis=1)
    rows = jnp.broadcast_to(rows[:, :, None], (HEADS, EXTRA, N))
    send = jnp.concatenate([fresh, rows], axis=1).astype(bf16)
    got = lax.all_to_all(send, "z", 0, 0, tiled=True).astype(f32)
    blocks = got[:, :P_SIZE]
    decays = got[:, P_SIZE] + got[:, P_SIZE + 1] + got[:, P_SIZE + 2]
    state = jnp.zeros((P_SIZE, N), f32)
    whole = jnp.zeros((1, N), f32)
    for k in range(NZ):
        state = jnp.exp(decays[k])[None] * state + blocks[k]
        whole = whole + decays[k][None]
    row = jnp.concatenate([state, jnp.broadcast_to(whole, (8, N))], axis=0)
    rows_x = gather_x(row)
    me = lax.axis_index("x")
    state = jnp.zeros((P_SIZE, N), f32)
    for k in range(NX):
        new = jnp.exp(rows_x[k, P_SIZE])[None] * state + rows_x[k, :P_SIZE]
        state = jnp.where(k < me, new, state)
    entering = []
    for k in range(NZ):
        entering.append(state.astype(bf16))
        state = jnp.exp(decays[k])[None] * state + blocks[k]
    return lax.all_to_all(jnp.stack(entering), "z", 0, 0, tiled=True)


def project(hidden, weight):
    everyone = gather_x(hidden).reshape(NX * TOK, HEADS * P_SIZE)
    term = jnp.dot(everyone, weight, preferred_element_type=f32)
    half = term.shape[1] // 2
    core = lax.axis_index("c")
    mine = lax.dynamic_slice_in_dim(term, core * half, half, 1)
    other = lax.dynamic_slice_in_dim(term, (1 - core) * half, half, 1).astype(bf16)
    other = lax.ppermute(other, "c", [(0, 1), (1, 0)])
    pair = (mine + other.astype(f32)).astype(bf16).reshape(NX, TOK, half)
    y = lax.axis_index("y")
    axes = ("x", "y")
    total = jnp.zeros((TOK, half), f32)
    for k in range(NX):
        piece = lax.dynamic_index_in_dim(pair, lax.rem(y + k, NX), 0, keepdims=False)
        pairs = [(j * NY + i, ((i + k) % NX) * NY + j) for j in range(NX) for i in range(NY)]
        total = total + lax.ppermute(piece, axes, pairs).astype(f32)
    return total.astype(bf16)


def shards(x_input, b_input, c_input, step, log_decay, skip, gain, out_weight):
    columns = out_weight.shape[1] // NX
    swap = out_weight.reshape(out_weight.shape[0], NX, columns).transpose(1, 0, 2)
    swap = lax.all_to_all(swap, "x", 0, 0, tiled=True)
    weight = lax.all_gather(swap, "z", axis=0)
    weight = weight.transpose(1, 0, 2, 3).reshape(HEADS * P_SIZE, columns)

    values = x_input.reshape(TOK, HEADS, P_SIZE)
    cumul = jnp.cumsum(log_decay, axis=1)
    total = cumul[:, -1]
    tail = jnp.exp(total[:, None] - cumul) * step
    weighted = (values.astype(f32) * tail.T[:, :, None]).astype(bf16)
    fresh = jnp.einsum("shp,sn->hpn", weighted, b_input, preferred_element_type=f32)
    entering = entering_states(fresh, total)

    within = jnp.tril(jnp.ones((TOK, TOK), dtype=bool))
    spread = cumul[:, :, None] - cumul[:, None, :]
    decay = jnp.exp(jnp.where(within[None], spread, -jnp.inf))
    scores = jnp.einsum("tn,sn->ts", c_input, b_input, preferred_element_type=f32)
    mixing = (scores[None] * decay * step[:, None, :]).astype(bf16)
    ssm = jnp.einsum("hts,shp->thp", mixing, values, preferred_element_type=f32)
    carried = jnp.einsum("tn,hpn->thp", c_input, entering, preferred_element_type=f32)
    ssm = ssm + jnp.exp(cumul).T[:, :, None] * carried
    ssm = ssm + skip[None, :, None] * values.astype(f32)
    ssm = ssm.reshape(TOK, HEADS * P_SIZE)
    meansq = jnp.mean(ssm * ssm, axis=1, keepdims=True)
    hidden = (ssm * lax.rsqrt(meansq + 1e-05) * gain[None, :]).astype(bf16)
    return project(hidden, weight)


def solution(mesh):
    fine = Mesh(mesh.devices.reshape(NX, NZ, NY, NC), ("x", "z", "y", "c"))
    ctx, tp = ("x", "z"), ("y", "c")
    in_specs = (
        P(ctx, tp),
        P(ctx, tp),
        P(ctx, tp),
        P(tp, ctx),
        P(tp, ctx),
        P(tp),
        P(tp),
        P(tp + ctx, None),
    )
    return jax.shard_map(
        shards, mesh=fine, in_specs=in_specs, out_specs=P(ctx, tp), check_vma=False
    )
```

time: 517 us -> 182 us (0.35)
  waiting for transfers between devices: 281 us -> 76.5 us
  blocking collectives: 123 us -> 0 us
  starting transfers between devices: 0.08 us -> 64.4 us
  other arithmetic: 77.6 us -> 14.9 us
  matrix products: 9.66 us -> 3.62 us
    all_gather x2 -> x1, waiting for transfers between devices: 240 us -> 27.1 us  [shards(): weight = lax.all_gather(swap, 'z', axis=0)]
    unnamed x1 -> x0, blocking collectives: 123 us -> none
    select_n x64 -> x0, other arithmetic: 75.1 us -> none  [hop(): return jax.tree.map(lambda a, b: jnp.where(reached, a, b), new, before)]
    all_to_all x0 -> x5, waiting for transfers between devices: none -> 41.7 us  [the longest x1 18.6 us: entering_states(): return lax.all_to_all(jnp.stack(entering), 'z', 0, 0, tiled=True)]
    reduce_scatter x1 -> x0, waiting for transfers between devices: 41 us -> none  [shards(): lax.psum_scatter(term.astype(jnp.bfloat16), 'tp', scatter_dimension=1, ti...]
    all_to_all x0 -> x5, starting transfers between devices: none -> 38.9 us  [the longest x1 15.7 us: entering_states(): got = lax.all_to_all(send, 'z', 0, 0, tiled=True).astype(f32)]
    ppermute x0 -> x5, starting transfers between devices: none -> 25.5 us  [the longest x4 15.2 us: project(): total = total + lax.ppermute(piece, axes, pairs).astype(f32)]
    unnamed x1 -> x15, other arithmetic: 0.01 us -> 9.14 us
  transfers between devices with their start and end apart: 3 -> 11, of which waited for: 3 -> 8; matrix products, arithmetic and copies ran while one was open for 16% -> 8% of each run, Pallas kernels for 0% -> 0%
where the time goes in v1:
time: 182 us; the launch traced here: 181 us
  waiting for transfers between devices  76.5 us (42%)
  starting transfers between devices  64.4 us (35%)
  other arithmetic  14.9 us (8%)
  between operations  13.8 us (8%)
  local copies, waits for them, and re-layouts  7.49 us (4%)
  matrix products  3.62 us (2%)
    all_gather x1, waiting for transfers between devices, shards(): weight = lax.all_gather(swap, 'z', axis=0)  27.1 us
    all_to_all x1, waiting for transfers between devices, entering_states(): return lax.all_to_all(jnp.stack(entering), 'z', 0, 0, tiled=True)  18.6 us
    all_to_all x1, starting transfers between devices, entering_states(): got = lax.all_to_all(send, 'z', 0, 0, tiled=True).astype(f32)  15.7 us
    ppermute x4, starting transfers between devices, project(): total = total + lax.ppermute(piece, axes, pairs).astype(f32)  15.2 us
    all_to_all x1, waiting for transfers between devices, entering_states(): got = lax.all_to_all(send, 'z', 0, 0, tiled=True).astype(f32)  14.4 us
    all_to_all x1, starting transfers between devices, entering_states(): return lax.all_to_all(jnp.stack(entering), 'z', 0, 0, tiled=True)  11.6 us
    ppermute x1, starting transfers between devices, project(): other = lax.ppermute(other, 'c', [(0, 1), (1, 0)])  10.3 us
    unnamed x15, other arithmetic  9.14 us
  transfers between devices with their start and end apart: 11, of which 8 were waited for; matrix products, arithmetic and copies ran while one was open for 8% of the time, Pallas kernels for 0%

profile of v1, /device:TPU:1, one launch (start us, length us, event | category | flops | bytes accessed | tf_op | source)
XLA Modules:
  0.0 180.7 jit_solution(1515927975473700735)
XLA Ops:
  6.5 1.0 reduce_window_sum.11
  7.8 1.1 copy.20
  11.0 15.7 %all-to-all-start = ((bf16[16,80,128]{2,1,0:T(8,128)(2,1)}), bf16[16,80,128]{2,1,0:T(8,128)(2,1)S(1)}, u32[]{:S(2)}, u32[]{:S(2)}) async-start(bf16[16,80,128]{2,1,0:T(8,128)(2,1)} %pad_maximum_fusion), calls=%async_computation | async-start | bytes 655360 | tf_op jit(solution)/shard_map/all_to_all | solution.py:35
  27.5 14.4 %all-to-all-done = bf16[16,80,128]{2,1,0:T(8,128)(2,1)S(1)} async-done(((bf16[16,80,128]{2,1,0:T(8,128)(2,1)}), bf16[16,80,128]{2,1,0:T(8,128)(2,1)S(1)}, u32[]{:S(2)}, u32[]{:S(2)}) %all-to-all-start) | async-done | bytes 327712 | tf_op jit(solution)/shard_map/all_to_all | solution.py:35
  41.9 4.0 %all-to-all-start.4 = ((bf16[4,16,1024]{2,1,0:T(8,128)(2,1)}), bf16[4,16,1024]{2,1,0:T(8,128)(2,1)S(1)}, u32[]{:S(2)}, u32[]{:S(2)}) async-start(bf16[4,16,1024]{2,1,0:T(8,128)(2,1)} %copy.22), calls=%async_computation.4 | async-start | bytes 262144 | tf_op jit(solution)/shard_map/all_to_all | solution.py:79
  46.2 4.6 %all-to-all-done.4 = bf16[4,16,1024]{2,1,0:T(8,128)(2,1)S(1)} async-done(((bf16[4,16,1024]{2,1,0:T(8,128)(2,1)}), bf16[4,16,1024]{2,1,0:T(8,128)(2,1)S(1)}, u32[]{:S(2)}, u32[]{:S(2)}) %all-to-all-start.4) | async-done | bytes 131104 | tf_op jit(solution)/shard_map/all_to_all | solution.py:79
  51.5 3.3 %all-to-all-start.1 = ((f32[4,72,128]{2,1,0:T(8,128)}), f32[4,72,128]{2,1,0:T(8,128)S(1)}, u32[]{:S(2)}, u32[]{:S(2)}) async-start(f32[4,72,128]{2,1,0:T(8,128)} %broadcast_in_dim.27), calls=%async_computation.1 | async-start | bytes 294912 | tf_op jit(solution)/shard_map/all_to_all | solution.py:25
  55.6 4.1 %all-to-all-done.1 = f32[4,72,128]{2,1,0:T(8,128)S(1)} async-done(((f32[4,72,128]{2,1,0:T(8,128)}), f32[4,72,128]{2,1,0:T(8,128)S(1)}, u32[]{:S(2)}, u32[]{:S(2)}) %all-to-all-start.1) | async-done | bytes 147488 | tf_op jit(solution)/shard_map/all_to_all | solution.py:25
  69.5 11.6 %all-to-all-start.2 = ((bf16[16,64,128]{2,1,0:T(8,128)(2,1)}), bf16[16,64,128]{2,1,0:T(8,128)(2,1)S(1)}, u32[]{:S(2)}, u32[]{:S(2)}) async-start(bf16[16,64,128]{2,1,0:T(8,128)(2,1)} %constant_dynamic-update-slice_fusion), calls=%async_computation.2 | async-start | bytes 524288 | tf_op jit(solution)/shard_map/all_to_all | solution.py:54
  81.2 18.6 %all-to-all-done.2 = bf16[16,64,128]{2,1,0:T(8,128)(2,1)S(1)} async-done(((bf16[16,64,128]{2,1,0:T(8,128)(2,1)}), bf16[16,64,128]{2,1,0:T(8,128)(2,1)S(1)}, u32[]{:S(2)}, u32[]{:S(2)}) %all-to-all-start.2) | async-done | bytes 262176 | tf_op jit(solution)/shard_map/all_to_all | solution.py:54
  101.0 1.1 broadcast_in_dim.28
  102.1 4.3 %all-to-all-start.3 = ((bf16[4,128,1024]{2,1,0:T(8,128)(2,1)}), bf16[4,128,1024]{2,1,0:T(8,128)(2,1)}, u32[]{:S(2)}, u32[]{:S(2)}) async-start(bf16[4,128,1024]{2,1,0:T(8,128)(2,1)} %broadcast_in_dim.28), calls=%async_computation.3 | async-start | bytes 2097152 | tf_op jit(solution)/shard_map/all_to_all | solution.py:25
  106.4 27.1 %all-gather.3.cloned.1.call-done = bf16[64,16,1024]{2,1,0:T(8,128)(2,1)} async-done(((bf16[4,16,1024]{2,1,0:T(8,128)(2,1)}), bf16[64,16,1024]{2,1,0:T(8,128)(2,1)}) %all-gather.3.cloned.1.call-update) | async-done | bytes 2097168 | tf_op jit(solution)/shard_map/all_gather | solution.py:80
  133.5 1.8 copy.23
  135.3 2.5 %fusion.46 = f32[512,1024]{1,0:T(8,128)S(1)} fusion(bf16[512,1024]{1,0:T(8,128)(2,1)} %bitcast.47, bf16[1024,1024]{1,0:T(8,128)(2,1)S(1)} %bitcast.198), kind=kOutput, calls=%fused_computation.146 | convolution fusion | flops 1073741824 | bytes 5242880 | tf_op jit(solution)/shard_map/dot_general | solution.py:59
  137.8 1.4 copy-done.1
  139.2 10.3 %collective-permute-start = (bf16[512,512]{1,0:T(8,128)(2,1)S(1)}, bf16[512,512]{1,0:T(8,128)(2,1)S(1)}, u32[]{:S(2)}, u32[]{:S(2)}) collective-permute-start(bf16[512,512]{1,0:T(8,128)(2,1)S(1)} %dynamic-slice_convert_fusion), channel_id=1, source_target_pairs={{0,1},{1,0},{2,3},{3,2},{4,5},{5,4},{6,7},{7,6},{8,9},{9,8},{10,11... | collective-permute-start | bytes 1572872 | tf_op jit(solution)/shard_map/ppermute | solution.py:64
  149.5 1.5 collective-permute-done
  151.0 1.4 add_convert_fusion
  153.1 5.6 %collective-permute-start.2 = (bf16[128,512]{1,0:T(8,128)(2,1)S(1)}, bf16[128,512]{1,0:T(8,128)(2,1)S(1)}, u32[]{:S(2)}, u32[]{:S(2)}) collective-permute-start(bf16[128,512]{1,0:T(8,128)(2,1)S(1)} %get-tuple-element.24), channel_id=1, source_target_pairs={{0,128},{2,256},{4,384},{6,0},{128,130},{130,258},{132,386},{134,2... | collective-permute-start | bytes 393224 | tf_op jit(solution)/shard_map/ppermute | solution.py:72
  158.7 4.5 %collective-permute-start.3 = (bf16[128,512]{1,0:T(8,128)(2,1)S(1)}, bf16[128,512]{1,0:T(8,128)(2,1)S(1)}, u32[]{:S(2)}, u32[]{:S(2)}) collective-permute-start(bf16[128,512]{1,0:T(8,128)(2,1)S(1)} %get-tuple-element.23), channel_id=1, source_target_pairs={{0,256},{2,384},{4,0},{6,128},{128,258},{130,386},{132,2},{134,130... | collective-permute-start | bytes 393224 | tf_op jit(solution)/shard_map/ppermute | solution.py:72
  163.2 4.5 %collective-permute-start.4 = (bf16[128,512]{1,0:T(8,128)(2,1)S(1)}, bf16[128,512]{1,0:T(8,128)(2,1)S(1)}, u32[]{:S(2)}, u32[]{:S(2)}) collective-permute-start(bf16[128,512]{1,0:T(8,128)(2,1)S(1)} %get-tuple-element.22), channel_id=1, source_target_pairs={{0,384},{2,0},{4,128},{6,256},{128,386},{130,2},{132,130},{134,258... | collective-permute-start | bytes 393224 | tf_op jit(solution)/shard_map/ppermute | solution.py:72
  167.7 4.5 %collective-permute-done.3 = bf16[128,512]{1,0:T(8,128)(2,1)S(1)} collective-permute-done((bf16[128,512]{1,0:T(8,128)(2,1)S(1)}, bf16[128,512]{1,0:T(8,128)(2,1)S(1)}, u32[]{:S(2)}, u32[]{:S(2)}) %collective-permute-start.3) | collective-permute-done | bytes 131104 | tf_op jit(solution)/shard_map/ppermute | solution.py:72
  172.2 1.0 collective-permute-done.4
  (68 shorter events, 17.2 us)
Async XLA Ops:
  6.5 3.3 %copy-start = (bf16[128,128]{1,0:T(8,128)(2,1)S(1)}, bf16[128,128]{1,0:T(8,128)(2,1)}, u32[]{:S(2)}) copy-start(bf16[128,128]{1,0:T(8,128)(2,1)} %param.9) | copy-start | bytes 98308
  6.5 20.2 %copy-start.3 = (bf16[16,4096]{1,0:T(8,128)(2,1)S(1)}, bf16[16,4096]{1,0:T(8,128)(2,1)}, u32[]{:S(2)}) copy-start(bf16[16,4096]{1,0:T(8,128)(2,1)} %param.15) | copy-start | bytes 393220
  11.0 31.0 %all-to-all-start = ((bf16[16,80,128]{2,1,0:T(8,128)(2,1)}), bf16[16,80,128]{2,1,0:T(8,128)(2,1)S(1)}, u32[]{:S(2)}, u32[]{:S(2)}) async-start(bf16[16,80,128]{2,1,0:T(8,128)(2,1)} %pad_maximum_fusion), calls=%async_computation | async-start | bytes 655360 | tf_op jit(solution)/shard_map/all_to_all | solution.py:35
  41.9 8.8 %all-to-all-start.4 = ((bf16[4,16,1024]{2,1,0:T(8,128)(2,1)}), bf16[4,16,1024]{2,1,0:T(8,128)(2,1)S(1)}, u32[]{:S(2)}, u32[]{:S(2)}) async-start(bf16[4,16,1024]{2,1,0:T(8,128)(2,1)} %copy.22), calls=%async_computation.4 | async-start | bytes 262144 | tf_op jit(solution)/shard_map/all_to_all | solution.py:79
  46.0 35.1 %copy-start.4 = (bf16[128,128]{1,0:T(8,128)(2,1)S(1)}, bf16[128,128]{1,0:T(8,128)(2,1)}, u32[]{:S(2)}) copy-start(bf16[128,128]{1,0:T(8,128)(2,1)} %param.10) | copy-start | bytes 98308
  46.2 53.8 %copy-start.5 = (f32[16,128]{1,0:T(8,128)S(1)}, f32[16,128]{1,0:T(8,128)}, u32[]{:S(2)}) copy-start(f32[16,128]{1,0:T(8,128)} %param.11) | copy-start | bytes 24580
  46.2 53.8 %copy-start.7 = (f32[16]{0:T(128)S(1)}, f32[16]{0:T(128)}, u32[]{:S(2)}) copy-start(f32[16]{0:T(128)} %param.13) | copy-start | bytes 196
  50.8 4.1 %copy-start.2 = (bf16[4,16,1024]{2,1,0:T(8,128)(2,1)}, bf16[4,16,1024]{2,1,0:T(8,128)(2,1)S(1)}, u32[]{:S(2)}) copy-start(bf16[4,16,1024]{2,1,0:T(8,128)(2,1)S(1)} %all-to-all-done.4) | copy-start | bytes 393220
  51.5 8.2 %all-to-all-start.1 = ((f32[4,72,128]{2,1,0:T(8,128)}), f32[4,72,128]{2,1,0:T(8,128)S(1)}, u32[]{:S(2)}, u32[]{:S(2)}) async-start(f32[4,72,128]{2,1,0:T(8,128)} %broadcast_in_dim.27), calls=%async_computation.1 | async-start | bytes 294912 | tf_op jit(solution)/shard_map/all_to_all | solution.py:25
  54.8 78.7 %all-gather.3.cloned.1.call-start = ((), (), s32[]{:S(2)}) async-start(), calls=%async_computation.5 | async-start | bytes 2228224 | tf_op jit(solution)/shard_map/all_gather | solution.py:80
  68.8 31.8 %copy-start.6 = (f32[1024]{0:T(1024)S(1)}, f32[1024]{0:T(1024)}, u32[]{:S(2)}) copy-start(f32[1024]{0:T(1024)} %param.14) | copy-start | bytes 12292
  69.5 30.3 %all-to-all-start.2 = ((bf16[16,64,128]{2,1,0:T(8,128)(2,1)}), bf16[16,64,128]{2,1,0:T(8,128)(2,1)S(1)}, u32[]{:S(2)}, u32[]{:S(2)}) async-start(bf16[16,64,128]{2,1,0:T(8,128)(2,1)} %constant_dynamic-update-slice_fusion), calls=%async_computation.2 | async-start | bytes 524288 | tf_op jit(solution)/shard_map/all_to_all | solution.py:54
  102.1 33.2 %all-to-all-start.3 = ((bf16[4,128,1024]{2,1,0:T(8,128)(2,1)}), bf16[4,128,1024]{2,1,0:T(8,128)(2,1)}, u32[]{:S(2)}, u32[]{:S(2)}) async-start(bf16[4,128,1024]{2,1,0:T(8,128)(2,1)} %broadcast_in_dim.28), calls=%async_computation.3 | async-start | bytes 2097152 | tf_op jit(solution)/shard_map/all_to_all | solution.py:25
  137.8 1.4 copy-start.1
  139.2 11.8 %collective-permute-start = (bf16[512,512]{1,0:T(8,128)(2,1)S(1)}, bf16[512,512]{1,0:T(8,128)(2,1)S(1)}, u32[]{:S(2)}, u32[]{:S(2)}) collective-permute-start(bf16[512,512]{1,0:T(8,128)(2,1)S(1)} %dynamic-slice_convert_fusion), channel_id=1, source_target_pairs={{0,1},{1,0},{2,3},{3,2},{4,5},{5,4},{6,7},{7,6},{8,9},{9,8},{10,11... | collective-permute-start | bytes 1572872 | tf_op jit(solution)/shard_map/ppermute | solution.py:64
  152.4 15.2 %collective-permute-start.1 = (bf16[128,512]{1,0:T(8,128)(2,1)S(1)}, bf16[128,512]{1,0:T(8,128)(2,1)S(1)}, u32[]{:S(2)}, u32[]{:S(2)}) collective-permute-start(bf16[128,512]{1,0:T(8,128)(2,1)S(1)} %get-tuple-element.21), channel_id=1, source_target_pairs={{0,0},{2,128},{4,256},{6,384},{128,2},{130,130},{132,258},{134,386... | collective-permute-start | bytes 393224 | tf_op jit(solution)/shard_map/ppermute | solution.py:72
  153.1 14.6 %collective-permute-start.2 = (bf16[128,512]{1,0:T(8,128)(2,1)S(1)}, bf16[128,512]{1,0:T(8,128)(2,1)S(1)}, u32[]{:S(2)}, u32[]{:S(2)}) collective-permute-start(bf16[128,512]{1,0:T(8,128)(2,1)S(1)} %get-tuple-element.24), channel_id=1, source_target_pairs={{0,128},{2,256},{4,384},{6,0},{128,130},{130,258},{132,386},{134,2... | collective-permute-start | bytes 393224 | tf_op jit(solution)/shard_map/ppermute | solution.py:72
  158.7 13.5 %collective-permute-start.3 = (bf16[128,512]{1,0:T(8,128)(2,1)S(1)}, bf16[128,512]{1,0:T(8,128)(2,1)S(1)}, u32[]{:S(2)}, u32[]{:S(2)}) collective-permute-start(bf16[128,512]{1,0:T(8,128)(2,1)S(1)} %get-tuple-element.23), channel_id=1, source_target_pairs={{0,256},{2,384},{4,0},{6,128},{128,258},{130,386},{132,2},{134,130... | collective-permute-start | bytes 393224 | tf_op jit(solution)/shard_map/ppermute | solution.py:72
  163.2 9.9 %collective-permute-start.4 = (bf16[128,512]{1,0:T(8,128)(2,1)S(1)}, bf16[128,512]{1,0:T(8,128)(2,1)S(1)}, u32[]{:S(2)}, u32[]{:S(2)}) collective-permute-start(bf16[128,512]{1,0:T(8,128)(2,1)S(1)} %get-tuple-element.22), channel_id=1, source_target_pairs={{0,384},{2,0},{4,128},{6,256},{128,386},{130,2},{132,130},{134,258... | collective-permute-start | bytes 393224 | tf_op jit(solution)/shard_map/ppermute | solution.py:72
Sparse Core Ops, SparseCore 0:
  57.7 75.7 all-gather.2

commit v2 on v1

v2 whole, which is shorter than its diff:
```python
import jax
import jax.numpy as jnp
from jax import lax
from jax.experimental import pallas as pl
from jax.experimental.pallas import tpu as pltpu
from jax.sharding import Mesh, PartitionSpec as P

NX, NZ, NY, NC = 4, 16, 4, 2
NTP = NY * NC
TOK = 128
HEADS = 16
P_SIZE = 64
N = 128
WIDTH = HEADS * P_SIZE
EXTRA = 16
ROWS = P_SIZE + EXTRA
SUM_ROWS = P_SIZE + 8
COLS = 128
f32 = jnp.float32
bf16 = jnp.bfloat16
HIGH = lax.Precision.HIGHEST


def call(kernel, out_shape, flops, moved, name):
    return pl.pallas_call(
        kernel,
        out_shape=out_shape,
        name=name,
        compiler_params=pltpu.CompilerParams(vmem_limit_bytes=32 * 2**20),
        cost_estimate=pl.CostEstimate(flops=flops, bytes_accessed=moved, transcendentals=0),
    )


def iota(shape, axis):
    return lax.broadcasted_iota(jnp.int32, shape, axis)


def dot(a, b, ca, cb, precision=None):
    return lax.dot_general(
        a, b, (((ca,), (cb,)), ((), ())), precision=precision, preferred_element_type=f32
    )


def cumulative(logs):
    upto = (iota((TOK, TOK), 0) <= iota((TOK, TOK), 1)).astype(f32)
    return dot(logs, upto, 1, 0, HIGH)


def spread_heads(per_head):
    owner = (iota((HEADS, WIDTH), 1) // P_SIZE == iota((HEADS, WIDTH), 0)).astype(f32)
    return dot(per_head, owner, 0, 0, HIGH)


def fresh_kernel(x_ref, b_ref, step_ref, logs_ref, out_ref):
    logs = logs_ref[...]
    cumul = cumulative(logs)
    total = dot(logs, jnp.ones((TOK, TOK), f32), 1, 0, HIGH)
    tail = jnp.exp(total - cumul) * step_ref[...]
    weighted = (x_ref[...].astype(f32) * spread_heads(tail)).astype(bf16)
    fresh = dot(weighted, b_ref[...], 0, 0).astype(bf16)
    high = total.astype(bf16)
    rest = total - high.astype(f32)
    middle = rest.astype(bf16)
    low = (rest - middle.astype(f32)).astype(bf16)
    row = iota((EXTRA, N), 0)
    for h in range(HEADS):
        out_ref[h, :P_SIZE, :] = fresh[h * P_SIZE : (h + 1) * P_SIZE]
        first, second, third = (
            jnp.broadcast_to(part[h : h + 1].astype(f32), (EXTRA, N)) for part in (high, middle, low)
        )
        pieces = jnp.where(row == 0, first, jnp.where(row == 1, second, third))
        out_ref[h, P_SIZE:, :] = jnp.where(row < 3, pieces, 0.0).astype(bf16)


def block_decay(got_ref, k):
    pieces = got_ref[k, P_SIZE:, :].astype(f32)
    return pieces[0:1] + pieces[1:2] + pieces[2:3]


def row_kernel(got_ref, out_ref):
    state = jnp.zeros((P_SIZE, N), f32)
    whole = jnp.zeros((1, N), f32)
    for k in range(NZ):
        decay = block_decay(got_ref, k)
        state = jnp.exp(decay) * state + got_ref[k, :P_SIZE, :].astype(f32)
        whole = whole + decay
    out_ref[:P_SIZE, :] = state
    out_ref[P_SIZE:, :] = jnp.broadcast_to(whole, (8, N))


def enter_kernel(me_ref, got_ref, rows_ref, out_ref):
    me = me_ref[0]
    state = jnp.zeros((P_SIZE, N), f32)
    for k in range(NX):
        decay = jnp.exp(rows_ref[k, P_SIZE : P_SIZE + 1, :])
        state = jnp.where(k < me, decay * state + rows_ref[k, :P_SIZE, :], state)
    for k in range(NZ):
        out_ref[k, :, :] = state.astype(bf16)
        decay = jnp.exp(block_decay(got_ref, k))
        state = decay * state + got_ref[k, :P_SIZE, :].astype(f32)


def inner_kernel(x_ref, b_ref, c_ref, step_ref, logs_ref, skip_ref, out_ref, scale_ref):
    logs = logs_ref[...]
    cumul = cumulative(logs)
    upto = (iota((TOK, TOK), 1) <= iota((TOK, TOK), 0)).astype(f32)
    cumul_t = dot(upto, logs, 1, 1, HIGH)
    scale_ref[...] = spread_heads(jnp.exp(cumul))
    scores = dot(c_ref[...], b_ref[...], 1, 1)
    within = iota((TOK, TOK), 1) <= iota((TOK, TOK), 0)
    left = iota((TOK, 2 * P_SIZE), 1) < P_SIZE
    for pair in range(HEADS // 2):
        columns = slice(pair * 2 * P_SIZE, (pair + 1) * 2 * P_SIZE)
        values = x_ref[:, columns]
        both = []
        for h in (2 * pair, 2 * pair + 1):
            spread = cumul_t[:, h : h + 1] - cumul[h : h + 1, :]
            decay = jnp.exp(jnp.where(within, spread, -1e30))
            mixing = (scores * decay * step_ref[h : h + 1, :]).astype(bf16)
            both.append(dot(mixing, values, 1, 0))
        own = jnp.where(left, both[0], both[1])
        out_ref[:, columns] = own + skip_ref[:, columns] * values.astype(f32)


def hidden_kernel(inner_ref, scale_ref, c_ref, state_ref, gain_ref, out_ref):
    states = state_ref[...].reshape(WIDTH, N)
    ssm = inner_ref[...] + scale_ref[...] * dot(c_ref[...], states, 1, 1)
    meansq = jnp.mean(ssm * ssm, axis=1, keepdims=True)
    out_ref[...] = (ssm * lax.rsqrt(meansq + 1e-05) * gain_ref[...]).astype(bf16)


def product_kernel(hidden_ref, weight_ref, out_ref):
    depth = WIDTH // NX
    term = jnp.zeros((NX * TOK, weight_ref.shape[3]), f32)
    for k in range(NX):
        rows = weight_ref[:, k, :, :].reshape(depth, weight_ref.shape[3])
        term = term + dot(hidden_ref[:, k * depth : (k + 1) * depth], rows, 1, 0)
    term = term.astype(bf16)
    for k in range(NX):
        for j in range(out_ref.shape[1]):
            out_ref[k, j, :, :] = term[k * TOK : (k + 1) * TOK, j * COLS : (j + 1) * COLS]


def sum_kernel(parts_ref, out_ref):
    for k in range(NX):
        total = parts_ref[k, 0, :, :].astype(f32)
        for j in range(1, NTP):
            total = total + parts_ref[k, j, :, :].astype(f32)
        out_ref[:, k * COLS : (k + 1) * COLS] = total.astype(bf16)


def gather_x(part):
    return lax.all_to_all(
        jnp.broadcast_to(part[None], (NX,) + part.shape), "x", 0, 0, tiled=True
    )


def shape(*dims, dtype=bf16):
    return jax.ShapeDtypeStruct(dims, dtype)


def shards(x_input, b_input, c_input, step, log_decay, skip, gain, out_weight):
    depth = out_weight.shape[0]
    swap = out_weight.reshape(depth, NTP, NX, COLS).transpose(2, 0, 1, 3)
    swap = lax.all_to_all(swap.reshape(NX, depth, NTP * COLS), "x", 0, 0, tiled=True)

    send = call(fresh_kernel, shape(HEADS, ROWS, N), 4 * 10**7, 10**6, "fresh")(
        x_input, b_input, step, log_decay
    )
    send, swap = lax.optimization_barrier((send, swap))
    weight = lax.all_gather(swap, "z", axis=0)

    got = lax.all_to_all(send, "z", 0, 0, tiled=True)
    inner, scale = call(
        inner_kernel,
        (shape(TOK, WIDTH, dtype=f32), shape(TOK, WIDTH, dtype=f32)),
        10**8,
        2 * 10**6,
        "inner",
    )(x_input, b_input, c_input, step, log_decay, jnp.repeat(skip, P_SIZE)[None])
    row = call(row_kernel, shape(SUM_ROWS, N, dtype=f32), 10**6, 4 * 10**5, "row")(got)
    rows = gather_x(row)
    me = lax.axis_index("x").astype(jnp.int32)[None]
    entering = pl.pallas_call(
        enter_kernel,
        out_shape=shape(HEADS, P_SIZE, N),
        in_specs=[
            pl.BlockSpec(memory_space=pltpu.SMEM),
            pl.BlockSpec(memory_space=pltpu.VMEM),
            pl.BlockSpec(memory_space=pltpu.VMEM),
        ],
        name="enter",
        cost_estimate=pl.CostEstimate(flops=10**6, bytes_accessed=10**6, transcendentals=0),
    )(me, got, rows)
    states = lax.all_to_all(entering, "z", 0, 0, tiled=True)

    hidden = call(hidden_kernel, shape(TOK, WIDTH), 3 * 10**7, 2 * 10**6, "hidden")(
        inner, scale, c_input, states, gain[None]
    )
    everyone = gather_x(hidden).reshape(NX * TOK, WIDTH)

    tiles = 2
    parts = pl.pallas_call(
        product_kernel,
        grid=(NTP // tiles,),
        out_shape=shape(NX, NTP, TOK, COLS),
        in_specs=[
            pl.BlockSpec((NX * TOK, WIDTH), lambda n: (0, 0)),
            pl.BlockSpec((NZ, NX, depth, tiles * COLS), lambda n: (0, 0, 0, n)),
        ],
        out_specs=pl.BlockSpec((NX, tiles, TOK, COLS), lambda n: (0, n, 0, 0)),
        name="product",
        compiler_params=pltpu.CompilerParams(vmem_limit_bytes=32 * 2**20),
        cost_estimate=pl.CostEstimate(
            flops=2 * NX * TOK * WIDTH * NTP * COLS, bytes_accessed=4 * 10**6, transcendentals=0
        ),
    )(everyone, weight)
    parts = parts.reshape(NX * NTP, TOK, COLS)
    parts = lax.all_to_all(parts, ("x", "y", "c"), 0, 0, tiled=True)
    return call(sum_kernel, shape(TOK, NX * COLS), 10**6, 10**6, "sum")(
        parts.reshape(NX, NTP, TOK, COLS)
    )


def solution(mesh):
    fine = Mesh(mesh.devices.reshape(NX, NZ, NY, NC), ("x", "z", "y", "c"))
    ctx, tp = ("x", "z"), ("y", "c")
    in_specs = (
        P(ctx, tp),
        P(ctx, tp),
        P(ctx, tp),
        P(tp, ctx),
        P(tp, ctx),
        P(tp),
        P(tp),
        P(tp + ctx, None),
    )
    return jax.shard_map(
        shards, mesh=fine, in_specs=in_specs, out_specs=P(ctx, tp), check_vma=False
    )
```

time: 182 us -> 146 us (0.80)
  blocking collectives: 0 us -> 72.9 us
  waiting for transfers between devices: 76.5 us -> 19.2 us
  starting transfers between devices: 64.4 us -> 23.5 us
  other arithmetic: 14.9 us -> 0 us
  Pallas kernels: 0 us -> 7.4 us
  matrix products: 3.62 us -> 0 us
    all_to_all x0 -> x3, blocking collectives: none -> 72.9 us  [the longest x1 31.6 us: shards(): parts = lax.all_to_all(parts, ('x', 'y', 'c'), 0, 0, tiled=True)]
    all_gather x1, waiting for transfers between devices: 27.1 us -> 0.01 us  [shards(): weight = lax.all_gather(swap, 'z', axis=0)]
    ppermute x5 -> x0, starting transfers between devices: 25.5 us -> none  [the longest x4 15.2 us: project(): total = total + lax.ppermute(piece, axes, pairs).astype(f32)]
    all_to_all x3 -> x2, waiting for transfers between devices: 37.6 us -> 14.2 us  [the longest x1 13.5 us: shards(): states = lax.all_to_all(entering, 'z', 0, 0, tiled=True)]
    all_to_all x3 -> x2, starting transfers between devices: 31.3 us -> 19.2 us  [the longest x1 14.3 us: shards(): states = lax.all_to_all(entering, 'z', 0, 0, tiled=True)]
    unnamed x15 -> x0, other arithmetic: 9.14 us -> none
    pallas_call x0 -> x7, Pallas kernels: none -> 7.4 us  [the longest x1 2.1 us: shards(): pl.pallas_call(product_kernel, grid=(NTP // tiles,), out_shape=shape(NX,...]
    ppermute x5 -> x0, waiting for transfers between devices: 6.95 us -> none  [the longest x4 5.46 us: project(): total = total + lax.ppermute(piece, axes, pairs).astype(f32)]
  transfers between devices with their start and end apart: 11 -> 4, of which waited for: 8 -> 3; matrix products, arithmetic and copies ran while one was open for 8% -> 1% of each run, Pallas kernels for 0% -> 3%
where the time goes in v2:
time: 146 us; the launch traced here: 145 us
  blocking collectives  72.9 us (50%)
  starting transfers between devices  23.5 us (16%)
  waiting for transfers between devices  19.2 us (13%)
  between operations  13.5 us (9%)
  local copies, waits for them, and re-layouts  8.71 us (6%)
  Pallas kernels  7.4 us (5%)
    all_to_all x1, blocking collectives, shards(): parts = lax.all_to_all(parts, ('x', 'y', 'c'), 0, 0, tiled=True)  31.6 us
    all_to_all x1, blocking collectives, shards(): got = lax.all_to_all(send, 'z', 0, 0, tiled=True)  28.4 us
    all_to_all x1, starting transfers between devices, shards(): states = lax.all_to_all(entering, 'z', 0, 0, tiled=True)  14.3 us
    all_to_all x1, waiting for transfers between devices, shards(): states = lax.all_to_all(entering, 'z', 0, 0, tiled=True)  13.5 us
    all_to_all x1, blocking collectives, gather_x(): lax.all_to_all(jnp.broadcast_to(part[None], (NX,) + part.shape), 'x', 0,...  12.9 us
    unnamed x30, local copies, waits for them, and re-layouts  6.05 us
    all_to_all x1, waiting for transfers between devices, gather_x(): lax.all_to_all(jnp.broadcast_to(part[None], (NX,) + part.shape), 'x', 0,...  5 us
    all_to_all x1, starting transfers between devices, shards(): lax.all_to_all(swap.reshape(NX, depth, NTP * COLS), 'x', 0, 0, tiled=True)  4.97 us
  transfers between devices with their start and end apart: 4, of which 3 were waited for; matrix products, arithmetic and copies ran while one was open for 1% of the time, Pallas kernels for 3%

profile of v2, /device:TPU:1, one launch (start us, length us, event | category | flops | bytes accessed | tf_op | source)
XLA Modules:
  0.0 145.1 jit_solution(7608683503091487083)
XLA Ops:
  6.5 1.0 reshape.17
  7.6 0.7 reshape.18
  8.3 5.0 %all-to-all-start = ((bf16[4,16,1024]{2,1,0:T(8,128)(2,1)}), bf16[4,16,1024]{2,1,0:T(8,128)(2,1)S(1)}, u32[]{:S(2)}, u32[]{:S(2)}) async-start(bf16[4,16,1024]{2,1,0:T(8,128)(2,1)} %reshape.18), calls=%async_computation | async-start | bytes 262144 | tf_op jit(solution)/shard_map/all_to_all | solution.py:165
  13.3 0.9 copy-done.2
  14.3 0.8 copy-done.4
  15.0 0.7 copy-done.7
  15.7 0.7 copy-done.9
  16.4 1.1 fresh.1
  17.5 0.6 all-to-all-done
  18.1 0.7 copy-done.13
  18.8 28.4 %all_to_all.30.got_ref = bf16[16,80,128]{2,1,0:T(8,128)(2,1)S(1)} all-to-all(bf16[16,80,128]{2,1,0:T(8,128)(2,1)S(1)} %fresh.1), channel_id=1, replica_groups=mesh['x'=4,'z'=16,'y'=4,'c'=2] {'z'}, dimensions={0} | all-to-all | bytes 655360 | tf_op jit(solution)/shard_map/all_to_all | solution.py:173
  47.3 0.7 broadcast_in_dim.23
  48.0 4.2 %all-to-all-start.2 = ((f32[4,72,128]{2,1,0:T(8,128)}), f32[4,72,128]{2,1,0:T(8,128)S(1)}, u32[]{:S(2)}, u32[]{:S(2)}) async-start(f32[4,72,128]{2,1,0:T(8,128)} %broadcast_in_dim.23), calls=%async_computation.2 | async-start | bytes 294912 | tf_op jit(solution)/shard_map/all_to_all | solution.py:153
  52.2 5.0 %all-to-all-done.2.rows_ref = f32[4,72,128]{2,1,0:T(8,128)S(1)} async-done(((f32[4,72,128]{2,1,0:T(8,128)}), f32[4,72,128]{2,1,0:T(8,128)S(1)}, u32[]{:S(2)}, u32[]{:S(2)}) %all-to-all-start.2) | async-done | bytes 147488 | tf_op jit(solution)/shard_map/all_to_all | solution.py:153
  57.2 0.7 copy-done.12
  57.9 1.8 %enter.1 = bf16[16,64,128]{2,1,0:T(8,128)(2,1)} custom-call(s32[1]{0:T(128)} %bitcast.me_ref, bf16[16,80,128]{2,1,0:T(8,128)(2,1)} %copy-done, f32[4,72,128]{2,1,0:T(8,128)} %copy-done.12), custom_call_target="tpu_custom_call" | custom-call | flops 1000000 | bytes 1000000 | tf_op jit(solution)/shard_map/enter/pallas_call | solution.py:184
  59.7 14.3 %all-to-all-start.3 = ((bf16[16,64,128]{2,1,0:T(8,128)(2,1)}), bf16[16,64,128]{2,1,0:T(8,128)(2,1)S(1)}, u32[]{:S(2)}, u32[]{:S(2)}) async-start(bf16[16,64,128]{2,1,0:T(8,128)(2,1)} %enter.1), calls=%async_computation.3 | async-start | bytes 524288 | tf_op jit(solution)/shard_map/all_to_all | solution.py:195
  74.1 1.2 inner.1
  75.3 13.5 %all-to-all-done.3.state_ref = bf16[16,64,128]{2,1,0:T(8,128)(2,1)S(1)} async-done(((bf16[16,64,128]{2,1,0:T(8,128)(2,1)}), bf16[16,64,128]{2,1,0:T(8,128)(2,1)S(1)}, u32[]{:S(2)}, u32[]{:S(2)}) %all-to-all-start.3) | async-done | bytes 262176 | tf_op jit(solution)/shard_map/all_to_all | solution.py:195
  89.3 12.9 %all_to_all.31 = bf16[4,128,1024]{2,1,0:T(8,128)(2,1)S(1)} all-to-all(bf16[4,128,1024]{2,1,0:T(8,128)(2,1)S(1)} %broadcast_in_dim.25), channel_id=1, replica_groups=mesh['x'=4,'z'=16,'y'=4,'c'=2] {'x'}, dimensions={0} | all-to-all | bytes 2097152 | tf_op jit(solution)/shard_map/all_to_all | solution.py:153
  102.3 1.6 %copy-done.1 = bf16[64,16,1024]{2,1,0:T(8,128)(2,1)S(1)} copy-done((bf16[64,16,1024]{2,1,0:T(8,128)(2,1)S(1)}, bf16[64,16,1024]{2,1,0:T(8,128)(2,1)}, u32[]{:S(2)}) %copy-start.1) | copy-done | bytes 2097176
  103.8 2.1 %product.1 = bf16[4,8,128,128]{3,2,1,0:T(8,128)(2,1)S(1)} custom-call(bf16[512,1024]{1,0:T(8,128)(2,1)S(1)} %bitcast.12, bf16[16,4,16,1024]{3,2,1,0:T(8,128)(2,1)S(1)} %bitcast.14), custom_call_target="tpu_custom_call" | custom-call | flops 1073741824 | bytes 4000000 | tf_op jit(solution)/shard_map/product/pallas_call | solution.py:203
  106.0 31.6 %all_to_all.32 = bf16[32,128,128]{2,1,0:T(8,128)(2,1)S(1)} all-to-all(bf16[32,128,128]{2,1,0:T(8,128)(2,1)S(1)} %bitcast.13), channel_id=1, replica_groups=mesh['x'=4,'z'=16,'y'=4,'c'=2] {'x','y','c'}, dimensions={0} | all-to-all | bytes 2097152 | tf_op jit(solution)/shard_map/all_to_all | solution.py:219
  137.5 0.8 sum.1
  (32 shorter events, 0.8 us)
Async XLA Ops:
  7.5 66.4 %copy-start.14 = (f32[16]{0:T(128)S(1)}, f32[16]{0:T(128)}, u32[]{:S(2)}) copy-start(f32[16]{0:T(128)} %param.13) | copy-start | bytes 196
  7.6 66.6 %copy-start.3 = (bf16[128,1024]{1,0:T(8,128)(2,1)S(1)}, bf16[128,1024]{1,0:T(8,128)(2,1)}, u32[]{:S(2)}) copy-start(bf16[128,1024]{1,0:T(8,128)(2,1)} %x_ref.3) | copy-start | bytes 786436
  7.6 66.6 %copy-start.5 = (bf16[128,128]{1,0:T(8,128)(2,1)S(1)}, bf16[128,128]{1,0:T(8,128)(2,1)}, u32[]{:S(2)}) copy-start(bf16[128,128]{1,0:T(8,128)(2,1)} %b_ref.3) | copy-start | bytes 98308
  7.6 66.5 %copy-start.6 = (bf16[128,128]{1,0:T(8,128)(2,1)S(1)}, bf16[128,128]{1,0:T(8,128)(2,1)}, u32[]{:S(2)}) copy-start(bf16[128,128]{1,0:T(8,128)(2,1)} %c_ref.3) | copy-start | bytes 98308
  7.6 66.5 %copy-start.8 = (f32[16,128]{1,0:T(8,128)S(1)}, f32[16,128]{1,0:T(8,128)}, u32[]{:S(2)}) copy-start(f32[16,128]{1,0:T(8,128)} %step_ref.3) | copy-start | bytes 24580
  7.6 66.5 %copy-start.10 = (f32[16,128]{1,0:T(8,128)S(1)}, f32[16,128]{1,0:T(8,128)}, u32[]{:S(2)}) copy-start(f32[16,128]{1,0:T(8,128)} %logs_ref.3) | copy-start | bytes 24580
  8.3 80.5 %copy-start.11 = (f32[1024]{0:T(1024)S(1)}, f32[1024]{0:T(1024)}, u32[]{:S(2)}) copy-start(f32[1024]{0:T(1024)} %param.14) | copy-start | bytes 12292
  8.3 9.8 %all-to-all-start = ((bf16[4,16,1024]{2,1,0:T(8,128)(2,1)}), bf16[4,16,1024]{2,1,0:T(8,128)(2,1)S(1)}, u32[]{:S(2)}, u32[]{:S(2)}) async-start(bf16[4,16,1024]{2,1,0:T(8,128)(2,1)} %reshape.18), calls=%async_computation | async-start | bytes 262144 | tf_op jit(solution)/shard_map/all_to_all | solution.py:165
  13.3 89.0 %all-gather.3.cloned.1.call-start = ((), (), s32[]{:S(2)}) async-start(), calls=%async_computation.6 | async-start | bytes 2228224 | tf_op jit(solution)/shard_map/all_gather | solution.py:171
  13.3 0.9 copy-start.2
  14.3 0.8 copy-start.4
  15.0 0.7 copy-start.7
  15.7 0.7 copy-start.9
  18.1 0.7 copy-start.13
  47.2 10.0 %copy-start = (bf16[16,80,128]{2,1,0:T(8,128)(2,1)}, bf16[16,80,128]{2,1,0:T(8,128)(2,1)S(1)}, u32[]{:S(2)}) copy-start(bf16[16,80,128]{2,1,0:T(8,128)(2,1)S(1)} %all_to_all.30.got_ref) | copy-start | bytes 983044
  48.0 9.2 %all-to-all-start.2 = ((f32[4,72,128]{2,1,0:T(8,128)}), f32[4,72,128]{2,1,0:T(8,128)S(1)}, u32[]{:S(2)}, u32[]{:S(2)}) async-start(f32[4,72,128]{2,1,0:T(8,128)} %broadcast_in_dim.23), calls=%async_computation.2 | async-start | bytes 294912 | tf_op jit(solution)/shard_map/all_to_all | solution.py:153
  57.2 0.7 copy-start.12
  59.7 29.2 %all-to-all-start.3 = ((bf16[16,64,128]{2,1,0:T(8,128)(2,1)}), bf16[16,64,128]{2,1,0:T(8,128)(2,1)S(1)}, u32[]{:S(2)}, u32[]{:S(2)}) async-start(bf16[16,64,128]{2,1,0:T(8,128)(2,1)} %enter.1), calls=%async_computation.3 | async-start | bytes 524288 | tf_op jit(solution)/shard_map/all_to_all | solution.py:195
  102.3 1.6 %copy-start.1 = (bf16[64,16,1024]{2,1,0:T(8,128)(2,1)S(1)}, bf16[64,16,1024]{2,1,0:T(8,128)(2,1)}, u32[]{:S(2)}) copy-start(bf16[64,16,1024]{2,1,0:T(8,128)(2,1)} %all-gather.3.cloned.1.call-done) | copy-start | bytes 6291460
Sparse Core Ops, SparseCore 0:
  18.9 82.4 all-gather.2

commit v3 on v2

--- a/solution.py
+++ b/solution.py
@@ -16,18 +16,25 @@
 ROWS = P_SIZE + EXTRA
 SUM_ROWS = P_SIZE + 8
 COLS = 128
+VMEM = 56 * 2**20
 f32 = jnp.float32
 bf16 = jnp.bfloat16
 HIGH = lax.Precision.HIGHEST
 
 
-def call(kernel, out_shape, flops, moved, name):
+def call(kernel, out_shape, flops, moved, name, scalars=0, operands=0):
+    specs = {}
+    if scalars:
+        specs["in_specs"] = [pl.BlockSpec(memory_space=pltpu.SMEM)] * scalars + [
+            pl.BlockSpec(memory_space=pltpu.VMEM)
+        ] * operands
     return pl.pallas_call(
         kernel,
         out_shape=out_shape,
         name=name,
-        compiler_params=pltpu.CompilerParams(vmem_limit_bytes=32 * 2**20),
+        compiler_params=pltpu.CompilerParams(vmem_limit_bytes=VMEM),
         cost_estimate=pl.CostEstimate(flops=flops, bytes_accessed=moved, transcendentals=0),
+        **specs,
     )
 
 
@@ -49,6 +56,18 @@
 def spread_heads(per_head):
     owner = (iota((HEADS, WIDTH), 1) // P_SIZE == iota((HEADS, WIDTH), 0)).astype(f32)
     return dot(per_head, owner, 0, 0, HIGH)
+
+
+def pack_kernel(core_ref, weight_ref, out_ref):
+    first = core_ref[0] == 0
+    block = NX * COLS
+    for x in range(NX):
+        for y in range(NY):
+            even, odd = (
+                weight_ref[:, pl.ds((2 * y + c) * block + x * COLS, COLS)] for c in range(NC)
+            )
+            out_ref[x, :, pl.ds(y * COLS, COLS)] = jnp.where(first, even, odd)
+            out_ref[x, :, pl.ds((NY + y) * COLS, COLS)] = jnp.where(first, odd, even)
 
 
 def fresh_kernel(x_ref, b_ref, step_ref, logs_ref, out_ref):
@@ -84,8 +103,9 @@
         decay = block_decay(got_ref, k)
         state = jnp.exp(decay) * state + got_ref[k, :P_SIZE, :].astype(f32)
         whole = whole + decay
-    out_ref[:P_SIZE, :] = state
-    out_ref[P_SIZE:, :] = jnp.broadcast_to(whole, (8, N))
+    for k in range(NX):
+        out_ref[k, :P_SIZE, :] = state
+        out_ref[k, P_SIZE:, :] = jnp.broadcast_to(whole, (8, N))
 
 
 def enter_kernel(me_ref, got_ref, rows_ref, out_ref):
@@ -126,43 +146,75 @@
     states = state_ref[...].reshape(WIDTH, N)
     ssm = inner_ref[...] + scale_ref[...] * dot(c_ref[...], states, 1, 1)
     meansq = jnp.mean(ssm * ssm, axis=1, keepdims=True)
-    out_ref[...] = (ssm * lax.rsqrt(meansq + 1e-05) * gain_ref[...]).astype(bf16)
+    hidden = (ssm * lax.rsqrt(meansq + 1e-05) * gain_ref[...]).astype(bf16)
+    for k in range(NX):
+        out_ref[k, :, :] = hidden
 
 
 def product_kernel(hidden_ref, weight_ref, out_ref):
     depth = WIDTH // NX
-    term = jnp.zeros((NX * TOK, weight_ref.shape[3]), f32)
-    for k in range(NX):
-        rows = weight_ref[:, k, :, :].reshape(depth, weight_ref.shape[3])
-        term = term + dot(hidden_ref[:, k * depth : (k + 1) * depth], rows, 1, 0)
-    term = term.astype(bf16)
-    for k in range(NX):
-        for j in range(out_ref.shape[1]):
-            out_ref[k, j, :, :] = term[k * TOK : (k + 1) * TOK, j * COLS : (j + 1) * COLS]
+    wide = weight_ref.shape[3]
+    for k in range(NX):
+        rows = weight_ref[:, k, :, :].reshape(depth, wide)
+        for i in range(NX):
+            term = dot(hidden_ref[i, :, k * depth : (k + 1) * depth], rows, 1, 0)
+            for j in range(NY):
+                piece = term[:, j * COLS : (j + 1) * COLS]
+                if k == 0:
+                    out_ref[i, j, :, :] = piece
+                else:
+                    out_ref[i, j, :, :] += piece
+
+
+def other_kernel(hidden_ref, weight_ref, out_ref, total):
+    product_kernel(hidden_ref, weight_ref, total)
+    out_ref[...] = total[...].astype(bf16)
+
+
+def pair_kernel(mine_ref, other_ref, out_ref):
+    out_ref[...] = (mine_ref[...] + other_ref[...].astype(f32)).astype(bf16)
 
 
 def sum_kernel(parts_ref, out_ref):
     for k in range(NX):
         total = parts_ref[k, 0, :, :].astype(f32)
-        for j in range(1, NTP):
+        for j in range(1, NY):
             total = total + parts_ref[k, j, :, :].astype(f32)
         out_ref[:, k * COLS : (k + 1) * COLS] = total.astype(bf16)
 
 
-def gather_x(part):
-    return lax.all_to_all(
-        jnp.broadcast_to(part[None], (NX,) + part.shape), "x", 0, 0, tiled=True
-    )
-
-
 def shape(*dims, dtype=bf16):
     return jax.ShapeDtypeStruct(dims, dtype)
 
 
+def product(everyone, weight, half):
+    depth, wide = weight.shape[2], NY * COLS
+    return pl.pallas_call(
+        other_kernel if half else product_kernel,
+        grid=(1,),
+        out_shape=shape(NX, NY, TOK, COLS, dtype=bf16 if half else f32),
+        in_specs=[
+            pl.BlockSpec((NX, TOK, WIDTH), lambda n: (0, 0, 0)),
+            pl.BlockSpec((NZ, NX, depth, wide), lambda n: (0, 0, 0, half)),
+        ],
+        out_specs=pl.BlockSpec((NX, NY, TOK, COLS), lambda n: (0, 0, 0, 0)),
+        scratch_shapes=[pltpu.VMEM((NX, NY, TOK, COLS), f32)] if half else [],
+        name="other" if half else "mine",
+        compiler_params=pltpu.CompilerParams(vmem_limit_bytes=VMEM),
+        cost_estimate=pl.CostEstimate(
+            flops=2 * NX * TOK * WIDTH * wide, bytes_accessed=3 * 10**6, transcendentals=0
+        ),
+    )(everyone, weight)
+
+
 def shards(x_input, b_input, c_input, step, log_decay, skip, gain, out_weight):
     depth = out_weight.shape[0]
-    swap = out_weight.reshape(depth, NTP, NX, COLS).transpose(2, 0, 1, 3)
-    swap = lax.all_to_all(swap.reshape(NX, depth, NTP * COLS), "x", 0, 0, tiled=True)
+    core = lax.axis_index("c").astype(jnp.int32)[None]
+    me = lax.axis_index("x").astype(jnp.int32)[None]
+    swap = call(pack_kernel, shape(NX, depth, NTP * COLS), 0, 3 * 10**5, "pack", 1, 1)(
+        core, out_weight
+    )
+    swap = lax.all_to_all(swap, "x", 0, 0, tiled=True)
 
     send = call(fresh_kernel, shape(HEADS, ROWS, N), 4 * 10**7, 10**6, "fresh")(
         x_input, b_input, step, log_decay
@@ -178,47 +230,25 @@
         2 * 10**6,
         "inner",
     )(x_input, b_input, c_input, step, log_decay, jnp.repeat(skip, P_SIZE)[None])
-    row = call(row_kernel, shape(SUM_ROWS, N, dtype=f32), 10**6, 4 * 10**5, "row")(got)
-    rows = gather_x(row)
-    me = lax.axis_index("x").astype(jnp.int32)[None]
-    entering = pl.pallas_call(
-        enter_kernel,
-        out_shape=shape(HEADS, P_SIZE, N),
-        in_specs=[
-            pl.BlockSpec(memory_space=pltpu.SMEM),
-            pl.BlockSpec(memory_space=pltpu.VMEM),
-            pl.BlockSpec(memory_space=pltpu.VMEM),
-        ],
-        name="enter",
-        cost_estimate=pl.CostEstimate(flops=10**6, bytes_accessed=10**6, transcendentals=0),
-    )(me, got, rows)
+    row = call(row_kernel, shape(NX, SUM_ROWS, N, dtype=f32), 10**6, 4 * 10**5, "row")(got)
+    rows = lax.all_to_all(row, "x", 0, 0, tiled=True)
+    entering = call(enter_kernel, shape(HEADS, P_SIZE, N), 10**6, 10**6, "enter", 1, 2)(
+        me, got, rows
+    )
     states = lax.all_to_all(entering, "z", 0, 0, tiled=True)
 
-    hidden = call(hidden_kernel, shape(TOK, WIDTH), 3 * 10**7, 2 * 10**6, "hidden")(
+    hidden = call(hidden_kernel, shape(NX, TOK, WIDTH), 3 * 10**7, 2 * 10**6, "hidden")(
         inner, scale, c_input, states, gain[None]
     )
-    everyone = gather_x(hidden).reshape(NX * TOK, WIDTH)
-
-    tiles = 2
-    parts = pl.pallas_call(
-        product_kernel,
-        grid=(NTP // tiles,),
-        out_shape=shape(NX, NTP, TOK, COLS),
-        in_specs=[
-            pl.BlockSpec((NX * TOK, WIDTH), lambda n: (0, 0)),
-            pl.BlockSpec((NZ, NX, depth, tiles * COLS), lambda n: (0, 0, 0, n)),
-        ],
-        out_specs=pl.BlockSpec((NX, tiles, TOK, COLS), lambda n: (0, n, 0, 0)),
-        name="product",
-        compiler_params=pltpu.CompilerParams(vmem_limit_bytes=32 * 2**20),
-        cost_estimate=pl.CostEstimate(
-            flops=2 * NX * TOK * WIDTH * NTP * COLS, bytes_accessed=4 * 10**6, transcendentals=0
-        ),
-    )(everyone, weight)
-    parts = parts.reshape(NX * NTP, TOK, COLS)
-    parts = lax.all_to_all(parts, ("x", "y", "c"), 0, 0, tiled=True)
+    everyone = lax.all_to_all(hidden, "x", 0, 0, tiled=True)
+
+    other = product(everyone, weight, 1)
+    other = lax.ppermute(other, "c", [(0, 1), (1, 0)])
+    mine = product(everyone, weight, 0)
+    parts = call(pair_kernel, shape(NX, NY, TOK, COLS), 10**6, 2 * 10**6, "pair")(mine, other)
+    parts = lax.all_to_all(parts.reshape(NX * NY, TOK, COLS), ("x", "y"), 0, 0, tiled=True)
     return call(sum_kernel, shape(TOK, NX * COLS), 10**6, 10**6, "sum")(
-        parts.reshape(NX, NTP, TOK, COLS)
+        parts.reshape(NX, NY, TOK, COLS)
     )
 
 

time: 146 us -> 153 us (1.048)
  Pallas kernels: 7.4 us -> 23.8 us
  blocking collectives: 72.9 us -> 60.4 us
  starting transfers between devices: 23.5 us -> 33.4 us
  local copies, waits for them, and re-layouts: 8.71 us -> 3.56 us
  waiting for transfers between devices: 19.2 us -> 17.3 us
    all_to_all x2, blocking collectives: 44.5 us -> 31.3 us  [the longest x1 17.3 us: shards(): lax.all_to_all(parts.reshape(NX * NY, TOK, COLS), ('x', 'y'), 0, 0, tiled...]
    pallas_call x4 -> x7, Pallas kernels: 4.35 us -> 16.3 us  [the longest x2 6.29 us: product(): pl.pallas_call(other_kernel if half else product_kernel, grid=(1,), out_s...]
    ppermute x0 -> x1, starting transfers between devices: none -> 11.7 us  [shards(): other = lax.ppermute(other, 'c', [(0, 1), (1, 0)])]
    unnamed x30 -> x10, local copies, waits for them, and re-layouts: 6.05 us -> 2.81 us
    all_to_all x1, waiting for transfers between devices: 13.5 us -> 10.3 us  [shards(): states = lax.all_to_all(entering, 'z', 0, 0, tiled=True)]
    pallas_call x1, Pallas kernels: 1.17 us -> 2.95 us  [shards(): call(inner_kernel, (shape(TOK, WIDTH, dtype=f32), shape(TOK, WIDTH, dtype...]
    reshape x3 -> x0, local copies, waits for them, and re-layouts: 1.71 us -> none  [the longest x2 0.99 us: shards(): swap = out_weight.reshape(depth, NTP, NX, COLS).transpose(2, 0, 1, 3)]
    pallas_call x1, Pallas kernels: 1.09 us -> 2.79 us  [shards(): call(fresh_kernel, shape(HEADS, ROWS, N), 4 * 10 ** 7, 10 ** 6, 'fresh')]
  transfers between devices with their start and end apart: 4 -> 5, of which waited for: 3 -> 3; matrix products, arithmetic and copies ran while one was open for 1% -> 0% of each run, Pallas kernels for 3% -> 10%
where the time goes in v3:
time: 153 us; the launch traced here: 152 us
  blocking collectives  60.4 us (39%)
  starting transfers between devices  33.4 us (22%)
  Pallas kernels  23.8 us (16%)
  waiting for transfers between devices  17.3 us (11%)
  between operations  13.4 us (9%)
  local copies, waits for them, and re-layouts  3.56 us (2%)
    all_to_all x1, blocking collectives, shards(): got = lax.all_to_all(send, 'z', 0, 0, tiled=True)  29 us
    all_to_all x1, blocking collectives, shards(): lax.all_to_all(parts.reshape(NX * NY, TOK, COLS), ('x', 'y'), 0, 0, tiled...  17.3 us
    all_to_all x1, blocking collectives, shards(): everyone = lax.all_to_all(hidden, 'x', 0, 0, tiled=True)  14.1 us
    all_to_all x1, starting transfers between devices, shards(): states = lax.all_to_all(entering, 'z', 0, 0, tiled=True)  13.5 us
    ppermute x1, starting transfers between devices, shards(): other = lax.ppermute(other, 'c', [(0, 1), (1, 0)])  11.7 us
    all_to_all x1, waiting for transfers between devices, shards(): states = lax.all_to_all(entering, 'z', 0, 0, tiled=True)  10.3 us
    pallas_call x2, Pallas kernels, product(): pl.pallas_call(other_kernel if half else product_kernel, grid=(1,), out_s...  6.29 us
    all_to_all x1, waiting for transfers between devices, shards(): rows = lax.all_to_all(row, 'x', 0, 0, tiled=True)  4.92 us
  transfers between devices with their start and end apart: 5, of which 3 were waited for; matrix products, arithmetic and copies ran while one was open for 0% of the time, Pallas kernels for 10%

profile of v3, /device:TPU:1, one launch (start us, length us, event | category | flops | bytes accessed | tf_op | source)
XLA Modules:
  0.0 151.8 jit_solution(5374829299610978272)
XLA Ops:
  6.5 1.6 %pack.1 = bf16[4,16,1024]{2,1,0:T(8,128)(2,1)} custom-call(s32[1]{0:T(128)} %bitcast.1.core_ref, bf16[16,4096]{1,0:T(8,128)(2,1)} %weight_ref.1), custom_call_target="tpu_custom_call" | custom-call | bytes 300000 | tf_op jit(solution)/shard_map/pack/pallas_call | solution.py:214
  8.1 4.8 %all-to-all-start = ((bf16[4,16,1024]{2,1,0:T(8,128)(2,1)}), bf16[4,16,1024]{2,1,0:T(8,128)(2,1)S(1)}, u32[]{:S(2)}, u32[]{:S(2)}) async-start(bf16[4,16,1024]{2,1,0:T(8,128)(2,1)} %pack.1), calls=%async_computation | async-start | bytes 262144 | tf_op jit(solution)/shard_map/all_to_all | solution.py:217
  13.0 2.8 %fresh.1 = bf16[16,80,128]{2,1,0:T(8,128)(2,1)} custom-call(bf16[128,1024]{1,0:T(8,128)(2,1)} %x_ref.3, bf16[128,128]{1,0:T(8,128)(2,1)} %b_ref.3, f32[16,128]{1,0:T(8,128)} %step_ref.3, f32[16,128]{1,0:T(8,128)} %logs_ref.3), custom_call_target="tpu_custom_call" | custom-call | flops 40000000 | bytes 1000000 | tf_op jit(solution)/shard_map/fresh/pallas_call | solution.py:219
  15.8 2.0 %all-to-all-done = bf16[4,16,1024]{2,1,0:T(8,128)(2,1)S(1)} async-done(((bf16[4,16,1024]{2,1,0:T(8,128)(2,1)}), bf16[4,16,1024]{2,1,0:T(8,128)(2,1)S(1)}, u32[]{:S(2)}, u32[]{:S(2)}) %all-to-all-start) | async-done | bytes 131104 | tf_op jit(solution)/shard_map/all_to_all | solution.py:217
  18.5 29.0 %all_to_all.30.got_ref = bf16[16,80,128]{2,1,0:T(8,128)(2,1)} all-to-all(bf16[16,80,128]{2,1,0:T(8,128)(2,1)} %fresh.1), channel_id=1, replica_groups=mesh['x'=4,'z'=16,'y'=4,'c'=2] {'z'}, dimensions={0} | all-to-all | bytes 655360 | tf_op jit(solution)/shard_map/all_to_all | solution.py:225
  47.5 1.7 %row.1 = f32[4,72,128]{2,1,0:T(8,128)} custom-call(bf16[16,80,128]{2,1,0:T(8,128)(2,1)} %all_to_all.30.got_ref), custom_call_target="tpu_custom_call" | custom-call | flops 1000000 | bytes 400000 | tf_op jit(solution)/shard_map/row/pallas_call | solution.py:233
  49.2 3.3 %all-to-all-start.2 = ((f32[4,72,128]{2,1,0:T(8,128)}), f32[4,72,128]{2,1,0:T(8,128)S(1)}, u32[]{:S(2)}, u32[]{:S(2)}) async-start(f32[4,72,128]{2,1,0:T(8,128)} %row.1), calls=%async_computation.2 | async-start | bytes 294912 | tf_op jit(solution)/shard_map/all_to_all | solution.py:234
  52.6 4.9 %all-to-all-done.2.rows_ref = f32[4,72,128]{2,1,0:T(8,128)S(1)} async-done(((f32[4,72,128]{2,1,0:T(8,128)}), f32[4,72,128]{2,1,0:T(8,128)S(1)}, u32[]{:S(2)}, u32[]{:S(2)}) %all-to-all-start.2) | async-done | bytes 147488 | tf_op jit(solution)/shard_map/all_to_all | solution.py:234
  57.5 0.7 copy-done.1
  58.2 1.8 %enter.1 = bf16[16,64,128]{2,1,0:T(8,128)(2,1)} custom-call(s32[1]{0:T(128)} %bitcast.me_ref, bf16[16,80,128]{2,1,0:T(8,128)(2,1)} %all_to_all.30.got_ref, f32[4,72,128]{2,1,0:T(8,128)} %copy-done.1), custom_call_target="tpu_custom_call" | custom-call | flops 1000000 | bytes 1000000 | tf_op jit(solution)/shard_map/enter/pallas_call | solution.py:235
  60.0 13.5 %all-to-all-start.3 = ((bf16[16,64,128]{2,1,0:T(8,128)(2,1)}), bf16[16,64,128]{2,1,0:T(8,128)(2,1)S(1)}, u32[]{:S(2)}, u32[]{:S(2)}) async-start(bf16[16,64,128]{2,1,0:T(8,128)(2,1)} %enter.1), calls=%async_computation.3 | async-start | bytes 524288 | tf_op jit(solution)/shard_map/all_to_all | solution.py:238
  73.6 0.7 broadcast_in_dim_reshape.3.skip_ref
  74.3 3.0 %inner.1 = (f32[128,1024]{1,0:T(8,128)}, f32[128,1024]{1,0:T(8,128)}) custom-call(bf16[128,1024]{1,0:T(8,128)(2,1)} %x_ref.3, bf16[128,128]{1,0:T(8,128)(2,1)} %b_ref.3, bf16[128,128]{1,0:T(8,128)(2,1)} %c_ref.3, f32[16,128]{1,0:T(8,128)} %step_ref.3, f32[16,128]{1,0:T(8,128)} %logs_ref.3, f32[1,1024]{1,0:T(1,128)} %broadcast_in_dim_reshape.3.skip_ref), custom_call_target="tpu_custom_call" | custom-call | flops 100000000 | bytes 2000000 | tf_op jit(solution)/shard_map/inner/pallas_call | solution.py:226
  77.2 10.3 %all-to-all-done.3.state_ref = bf16[16,64,128]{2,1,0:T(8,128)(2,1)S(1)} async-done(((bf16[16,64,128]{2,1,0:T(8,128)(2,1)}), bf16[16,64,128]{2,1,0:T(8,128)(2,1)S(1)}, u32[]{:S(2)}, u32[]{:S(2)}) %all-to-all-start.3) | async-done | bytes 262176 | tf_op jit(solution)/shard_map/all_to_all | solution.py:238
  87.5 0.7 copy-done
  88.2 2.6 %hidden.1 = bf16[4,128,1024]{2,1,0:T(8,128)(2,1)} custom-call(f32[128,1024]{1,0:T(8,128)} %get-tuple-element.9.inner_ref, f32[128,1024]{1,0:T(8,128)} %get-tuple-element.10.scale_ref, bf16[128,128]{1,0:T(8,128)(2,1)} %c_ref.3, bf16[16,64,128]{2,1,0:T(8,128)(2,1)} %copy-done, f32[1,1024]{1,0:T(1,128)} %bitcast.10), custom_call_target="tpu_custom_call" | custom-call | flops 30000000 | bytes 2000000 | tf_op jit(solution)/shard_map/hidden/pallas_call | solution.py:240
  90.9 14.1 %all_to_all.31.hidden_ref = bf16[4,128,1024]{2,1,0:T(8,128)(2,1)} all-to-all(bf16[4,128,1024]{2,1,0:T(8,128)(2,1)} %hidden.1), channel_id=1, replica_groups=mesh['x'=4,'z'=16,'y'=4,'c'=2] {'x'}, dimensions={0} | all-to-all | bytes 2097152 | tf_op jit(solution)/shard_map/all_to_all | solution.py:243
  104.9 3.1 %other.1 = bf16[4,4,128,128]{3,2,1,0:T(8,128)(2,1)} custom-call(bf16[4,128,1024]{2,1,0:T(8,128)(2,1)} %all_to_all.31.hidden_ref, bf16[16,4,16,1024]{3,2,1,0:T(8,128)(2,1)} %bitcast.6), custom_call_target="tpu_custom_call" | custom-call | flops 536870912 | bytes 3000000 | tf_op jit(solution)/shard_map/other/pallas_call | solution.py:192
  108.0 11.7 %collective-permute-start = (bf16[4,4,128,128]{3,2,1,0:T(8,128)(2,1)}, bf16[4,4,128,128]{3,2,1,0:T(8,128)(2,1)S(1)}, u32[]{:S(2)}, u32[]{:S(2)}) collective-permute-start(bf16[4,4,128,128]{3,2,1,0:T(8,128)(2,1)} %other.1), channel_id=1, source_target_pairs={{0,1},{1,0},{2,3},{3,2},{4,5},{5,4},{6,7},{7,6},{8,9},{9,8},{10,11... | collective-permute-start | bytes 1572872 | tf_op jit(solution)/shard_map/ppermute | solution.py:246
  119.6 3.2 %mine.1.mine_ref = f32[4,4,128,128]{3,2,1,0:T(8,128)} custom-call(bf16[4,128,1024]{2,1,0:T(8,128)(2,1)} %all_to_all.31.hidden_ref, bf16[16,4,16,1024]{3,2,1,0:T(8,128)(2,1)} %bitcast.7), custom_call_target="tpu_custom_call" | custom-call | flops 536870912 | bytes 3000000 | tf_op jit(solution)/shard_map/mine/pallas_call | solution.py:192
  122.9 0.8 copy-done.3
  123.7 2.2 %pair.1 = bf16[4,4,128,128]{3,2,1,0:T(8,128)(2,1)} custom-call(f32[4,4,128,128]{3,2,1,0:T(8,128)} %mine.1.mine_ref, bf16[4,4,128,128]{3,2,1,0:T(8,128)(2,1)} %copy-done.3), custom_call_target="tpu_custom_call" | custom-call | flops 1000000 | bytes 2000000 | tf_op jit(solution)/shard_map/pair/pallas_call | solution.py:248
  125.9 17.3 %all_to_all.32 = bf16[16,128,128]{2,1,0:T(8,128)(2,1)} all-to-all(bf16[16,128,128]{2,1,0:T(8,128)(2,1)} %bitcast.9), channel_id=1, replica_groups=mesh['x'=4,'z'=16,'y'=4,'c'=2] {'x','y'}, dimensions={0} | all-to-all | bytes 1048576 | tf_op jit(solution)/shard_map/all_to_all | solution.py:249
  143.2 1.8 %sum.1 = bf16[128,512]{1,0:T(8,128)(2,1)} custom-call(bf16[4,4,128,128]{3,2,1,0:T(8,128)(2,1)} %bitcast.8), custom_call_target="tpu_custom_call" | custom-call | flops 1000000 | bytes 1000000 | tf_op jit(solution)/shard_map/sum/pallas_call | solution.py:250
  (12 shorter events, 0.8 us)
Async XLA Ops:
  6.5 67.0 %copy-start.4 = (f32[16]{0:T(128)S(1)}, f32[16]{0:T(128)}, u32[]{:S(2)}) copy-start(f32[16]{0:T(128)} %param.13) | copy-start | bytes 196
  8.1 9.7 %all-to-all-start = ((bf16[4,16,1024]{2,1,0:T(8,128)(2,1)}), bf16[4,16,1024]{2,1,0:T(8,128)(2,1)S(1)}, u32[]{:S(2)}, u32[]{:S(2)}) async-start(bf16[4,16,1024]{2,1,0:T(8,128)(2,1)} %pack.1), calls=%async_computation | async-start | bytes 262144 | tf_op jit(solution)/shard_map/all_to_all | solution.py:217
  13.0 91.9 %all-gather.3.cloned.1.call-start = ((), (), s32[]{:S(2)}) async-start(), calls=%async_computation.6 | async-start | bytes 2228224 | tf_op jit(solution)/shard_map/all_gather | solution.py:223
  17.8 0.7 copy-start.2
  49.2 8.3 %all-to-all-start.2 = ((f32[4,72,128]{2,1,0:T(8,128)}), f32[4,72,128]{2,1,0:T(8,128)S(1)}, u32[]{:S(2)}, u32[]{:S(2)}) async-start(f32[4,72,128]{2,1,0:T(8,128)} %row.1), calls=%async_computation.2 | async-start | bytes 294912 | tf_op jit(solution)/shard_map/all_to_all | solution.py:234
  57.5 0.7 copy-start.1
  60.0 27.6 %all-to-all-start.3 = ((bf16[16,64,128]{2,1,0:T(8,128)(2,1)}), bf16[16,64,128]{2,1,0:T(8,128)(2,1)S(1)}, u32[]{:S(2)}, u32[]{:S(2)}) async-start(bf16[16,64,128]{2,1,0:T(8,128)(2,1)} %enter.1), calls=%async_computation.3 | async-start | bytes 524288 | tf_op jit(solution)/shard_map/all_to_all | solution.py:238
  87.5 0.7 copy-start
  108.0 14.9 %collective-permute-start = (bf16[4,4,128,128]{3,2,1,0:T(8,128)(2,1)}, bf16[4,4,128,128]{3,2,1,0:T(8,128)(2,1)S(1)}, u32[]{:S(2)}, u32[]{:S(2)}) collective-permute-start(bf16[4,4,128,128]{3,2,1,0:T(8,128)(2,1)} %other.1), channel_id=1, source_target_pairs={{0,1},{1,0},{2,3},{3,2},{4,5},{5,4},{6,7},{7,6},{8,9},{9,8},{10,11... | collective-permute-start | bytes 1572872 | tf_op jit(solution)/shard_map/ppermute | solution.py:246
  122.9 0.8 copy-start.3
Sparse Core Ops, SparseCore 0:
  18.6 81.9 all-gather.2

commit v4 on v3

v4 whole, which is shorter than its diff:
```python
import jax
import jax.numpy as jnp
from jax import lax
from jax.experimental import pallas as pl
from jax.experimental.pallas import tpu as pltpu
from jax.sharding import Mesh, PartitionSpec as P

NX, NZ, NY, NC = 4, 16, 4, 2
NTP = NY * NC
TOK = 128
HEADS = 16
P_SIZE = 64
N = 128
WIDTH = HEADS * P_SIZE
CTX = NX * NZ
CHUNK = WIDTH // CTX
EXTRA = 8
COLS = 128
LARGE = 56 * 2**20
f32 = jnp.float32
bf16 = jnp.bfloat16
HIGH = lax.Precision.HIGHEST


def call(kernel, out_shape, flops, moved, name, vmem=32 * 2**20):
    return pl.pallas_call(
        kernel,
        out_shape=out_shape,
        name=name,
        compiler_params=pltpu.CompilerParams(vmem_limit_bytes=vmem),
        cost_estimate=pl.CostEstimate(flops=flops, bytes_accessed=moved, transcendentals=0),
    )


def iota(shape, axis):
    return lax.broadcasted_iota(jnp.int32, shape, axis)


def dot(a, b, ca, cb, precision=None):
    return lax.dot_general(
        a, b, (((ca,), (cb,)), ((), ())), precision=precision, preferred_element_type=f32
    )


def cumulative(logs):
    upto = (iota((TOK, TOK), 0) <= iota((TOK, TOK), 1)).astype(f32)
    return dot(logs, upto, 1, 0, HIGH)


def spread_heads(per_head):
    owner = (iota((HEADS, WIDTH), 1) // P_SIZE == iota((HEADS, WIDTH), 0)).astype(f32)
    return dot(per_head, owner, 0, 0, HIGH)


def pack_kernel(weight_ref, out_ref):
    for x in range(NX):
        for j in range(NTP):
            out_ref[x, :, j * COLS : (j + 1) * COLS] = weight_ref[:, pl.ds((j * NX + x) * COLS, COLS)]


def fresh_kernel(x_ref, b_ref, step_ref, logs_ref, out_ref):
    logs = logs_ref[...]
    cumul = cumulative(logs)
    total = dot(logs, jnp.ones((TOK, TOK), f32), 1, 0, HIGH)
    tail = jnp.exp(total - cumul) * step_ref[...]
    weighted = (x_ref[...].astype(f32) * spread_heads(tail)).astype(bf16)
    fresh = dot(weighted, b_ref[...], 0, 0).astype(bf16)
    high = total.astype(bf16)
    rest = total - high.astype(f32)
    middle = rest.astype(bf16)
    low = (rest - middle.astype(f32)).astype(bf16)
    row = iota((EXTRA, N), 0)
    for h in range(HEADS):
        first, second, third = (
            jnp.broadcast_to(part[h : h + 1].astype(f32), (EXTRA, N)) for part in (high, middle, low)
        )
        pieces = jnp.where(row == 0, first, jnp.where(row == 1, second, third))
        pieces = jnp.where(row < 3, pieces, 0.0).astype(bf16)
        for k in range(h * P_SIZE // CHUNK, (h + 1) * P_SIZE // CHUNK):
            out_ref[k, :CHUNK, :] = fresh[k * CHUNK : (k + 1) * CHUNK]
            out_ref[k, CHUNK:, :] = pieces


def scan_kernel(got_ref, out_ref):
    state = jnp.zeros((CHUNK, N), f32)
    for k in range(CTX):
        out_ref[k, :, :] = state.astype(bf16)
        pieces = got_ref[k, CHUNK:, :].astype(f32)
        decay = jnp.exp(pieces[0:1] + pieces[1:2] + pieces[2:3])
        state = decay * state + got_ref[k, :CHUNK, :].astype(f32)


def inner_kernel(x_ref, b_ref, c_ref, step_ref, logs_ref, skip_ref, out_ref, scale_ref):
    logs = logs_ref[...]
    cumul = cumulative(logs)
    upto = (iota((TOK, TOK), 1) <= iota((TOK, TOK), 0)).astype(f32)
    cumul_t = dot(upto, logs, 1, 1, HIGH)
    scale_ref[...] = spread_heads(jnp.exp(cumul))
    scores = dot(c_ref[...], b_ref[...], 1, 1)
    within = iota((TOK, TOK), 1) <= iota((TOK, TOK), 0)
    left = iota((TOK, 2 * P_SIZE), 1) < P_SIZE
    for pair in range(HEADS // 2):
        columns = slice(pair * 2 * P_SIZE, (pair + 1) * 2 * P_SIZE)
        values = x_ref[:, columns]
        both = []
        for h in (2 * pair, 2 * pair + 1):
            spread = cumul_t[:, h : h + 1] - cumul[h : h + 1, :]
            decay = jnp.exp(jnp.where(within, spread, -1e30))
            mixing = (scores * decay * step_ref[h : h + 1, :]).astype(bf16)
            both.append(dot(mixing, values, 1, 0))
        own = jnp.where(left, both[0], both[1])
        out_ref[:, columns] = own + skip_ref[:, columns] * values.astype(f32)


def hidden_kernel(inner_ref, scale_ref, c_ref, state_ref, gain_ref, out_ref):
    states = state_ref[...].reshape(WIDTH, N)
    ssm = inner_ref[...] + scale_ref[...] * dot(c_ref[...], states, 1, 1)
    meansq = jnp.mean(ssm * ssm, axis=1, keepdims=True)
    hidden = (ssm * lax.rsqrt(meansq + 1e-05) * gain_ref[...]).astype(bf16)
    for k in range(NX):
        out_ref[k, :, :] = hidden


def product_kernel(hidden_ref, weight_ref, out_ref):
    depth = WIDTH // NX
    wide = weight_ref.shape[3]
    for i in range(NX):
        term = jnp.zeros((TOK, wide), f32)
        for k in range(NX):
            rows = weight_ref[:, k, :, :].reshape(depth, wide)
            term = term + dot(hidden_ref[i, :, k * depth : (k + 1) * depth], rows, 1, 0)
        for j in range(wide // COLS):
            out_ref[i, j, :, :] = term[:, j * COLS : (j + 1) * COLS].astype(bf16)


def sum_kernel(parts_ref, out_ref):
    for k in range(NX):
        total = parts_ref[k, 0, :, :].astype(f32)
        for j in range(1, NTP):
            total = total + parts_ref[k, j, :, :].astype(f32)
        out_ref[:, k * COLS : (k + 1) * COLS] = total.astype(bf16)


def shape(*dims, dtype=bf16):
    return jax.ShapeDtypeStruct(dims, dtype)


def product(everyone, weight):
    depth, tiles = weight.shape[2], 2
    return pl.pallas_call(
        product_kernel,
        grid=(NTP // tiles,),
        out_shape=shape(NX, NTP, TOK, COLS),
        in_specs=[
            pl.BlockSpec((NX, TOK, WIDTH), lambda n: (0, 0, 0)),
            pl.BlockSpec((NZ, NX, depth, tiles * COLS), lambda n: (0, 0, 0, n)),
        ],
        out_specs=pl.BlockSpec((NX, tiles, TOK, COLS), lambda n: (0, n, 0, 0)),
        name="product",
        compiler_params=pltpu.CompilerParams(vmem_limit_bytes=LARGE),
        cost_estimate=pl.CostEstimate(
            flops=2 * NX * TOK * WIDTH * NTP * COLS, bytes_accessed=4 * 10**6, transcendentals=0
        ),
    )(everyone, weight)


def shards(x_input, b_input, c_input, step, log_decay, skip, gain, out_weight):
    depth = out_weight.shape[0]
    swap = call(pack_kernel, shape(NX, depth, NTP * COLS), 0, 3 * 10**5, "pack", LARGE)(out_weight)
    swap = lax.all_to_all(swap, "x", 0, 0, tiled=True)

    send = call(
        fresh_kernel, shape(CTX, CHUNK + EXTRA, N), 4 * 10**7, 10**6, "fresh", LARGE
    )(x_input, b_input, step, log_decay)
    send, swap = lax.optimization_barrier((send, swap))
    weight = lax.all_gather(swap, "z", axis=0)

    got = lax.all_to_all(send, ("x", "z"), 0, 0, tiled=True)
    inner, scale = call(
        inner_kernel,
        (shape(TOK, WIDTH, dtype=f32), shape(TOK, WIDTH, dtype=f32)),
        10**8,
        2 * 10**6,
        "inner",
    )(x_input, b_input, c_input, step, log_decay, jnp.repeat(skip, P_SIZE)[None])
    entering = call(scan_kernel, shape(CTX, CHUNK, N), 10**6, 7 * 10**5, "scan")(got)
    states = lax.all_to_all(entering, ("x", "z"), 0, 0, tiled=True)

    hidden = call(hidden_kernel, shape(NX, TOK, WIDTH), 3 * 10**7, 2 * 10**6, "hidden")(
        inner, scale, c_input, states, gain[None]
    )
    everyone = lax.all_to_all(hidden, "x", 0, 0, tiled=True)
    parts = product(everyone, weight).reshape(NX * NTP, TOK, COLS)
    parts = lax.all_to_all(parts, ("x", "y", "c"), 0, 0, tiled=True)
    return call(sum_kernel, shape(TOK, NX * COLS), 10**6, 10**6, "sum")(
        parts.reshape(NX, NTP, TOK, COLS)
    )


def solution(mesh):
    fine = Mesh(mesh.devices.reshape(NX, NZ, NY, NC), ("x", "z", "y", "c"))
    ctx, tp = ("x", "z"), ("y", "c")
    in_specs = (
        P(ctx, tp),
        P(ctx, tp),
        P(ctx, tp),
        P(tp, ctx),
        P(tp, ctx),
        P(tp),
        P(tp),
        P(tp + ctx, None),
    )
    return jax.shard_map(
        shards, mesh=fine, in_specs=in_specs, out_specs=P(ctx, tp), check_vma=False
    )
```

time: 153 us -> 147 us (0.961)
  blocking collectives: 60.4 us -> 84.3 us
  starting transfers between devices: 33.4 us -> 13.9 us
  Pallas kernels: 23.8 us -> 12.4 us
  waiting for transfers between devices: 17.3 us -> 21.3 us
  local copies, waits for them, and re-layouts: 3.56 us -> 0.83 us
    all_to_all x2, blocking collectives: 46.3 us -> 70.2 us  [the longest x1 41.3 us: shards(): got = lax.all_to_all(send, ('x', 'z'), 0, 0, tiled=True)]
    ppermute x1 -> x0, starting transfers between devices: 11.7 us -> none  [shards(): other = lax.ppermute(other, 'c', [(0, 1), (1, 0)])]
    all_to_all x2 -> x1, starting transfers between devices: 16.9 us -> 9.08 us  [shards(): states = lax.all_to_all(entering, ('x', 'z'), 0, 0, tiled=True)]
    pallas_call x7 -> x4, Pallas kernels: 16.4 us -> 10.1 us  [the longest x1 4.81 us: product(): pl.pallas_call(product_kernel, grid=(NTP // tiles,), out_shape=shape(NX,...]
    all_to_all x2 -> x1, waiting for transfers between devices: 15.2 us -> 19.3 us  [shards(): states = lax.all_to_all(entering, ('x', 'z'), 0, 0, tiled=True)]
    pallas_call x1, Pallas kernels: 2.62 us -> 0.36 us  [shards(): call(hidden_kernel, shape(NX, TOK, WIDTH), 3 * 10 ** 7, 2 * 10 ** 6, 'hid...]
    unnamed x10 -> x16, local copies, waits for them, and re-layouts: 2.81 us -> 0.68 us
    pallas_call x1, Pallas kernels: 2.95 us -> 1.16 us  [shards(): call(inner_kernel, (shape(TOK, WIDTH, dtype=f32), shape(TOK, WIDTH, dtype...]
  transfers between devices with their start and end apart: 5 -> 3, of which waited for: 3 -> 2; matrix products, arithmetic and copies ran while one was open for 0% -> 0% of each run, Pallas kernels for 10% -> 4%
where the time goes in v4:
time: 147 us; the launch traced here: 146 us
  blocking collectives  84.3 us (57%)
  waiting for transfers between devices  21.3 us (14%)
  starting transfers between devices  13.9 us (9%)
  between operations  13.5 us (9%)
  Pallas kernels  12.4 us (8%)
    all_to_all x1, blocking collectives, shards(): got = lax.all_to_all(send, ('x', 'z'), 0, 0, tiled=True)  41.3 us
    all_to_all x1, blocking collectives, shards(): parts = lax.all_to_all(parts, ('x', 'y', 'c'), 0, 0, tiled=True)  28.8 us
    all_to_all x1, waiting for transfers between devices, shards(): states = lax.all_to_all(entering, ('x', 'z'), 0, 0, tiled=True)  19.3 us
    all_to_all x1, blocking collectives, shards(): everyone = lax.all_to_all(hidden, 'x', 0, 0, tiled=True)  14.1 us
    all_to_all x1, starting transfers between devices, shards(): states = lax.all_to_all(entering, ('x', 'z'), 0, 0, tiled=True)  9.08 us
    all_to_all x1, starting transfers between devices, shards(): swap = lax.all_to_all(swap, 'x', 0, 0, tiled=True)  4.84 us
    pallas_call x1, Pallas kernels, product(): pl.pallas_call(product_kernel, grid=(NTP // tiles,), out_shape=shape(NX,...  4.81 us
  transfers between devices with their start and end apart: 3, of which 2 were waited for; matrix products, arithmetic and copies ran while one was open for 0% of the time, Pallas kernels for 4%

profile of v4, /device:TPU:1, one launch (start us, length us, event | category | flops | bytes accessed | tf_op | source)
XLA Modules:
  0.0 146.3 jit_solution(16010832120703670454)
XLA Ops:
  6.5 0.0 copy-start.1
  6.6 0.0 copy-start.5
  6.6 1.6 %pack.1 = bf16[4,16,1024]{2,1,0:T(8,128)(2,1)} custom-call(bf16[16,4096]{1,0:T(8,128)(2,1)} %weight_ref.1), custom_call_target="tpu_custom_call" | custom-call | bytes 300000 | tf_op jit(solution)/shard_map/pack/pallas_call | solution.py:169
  8.2 4.8 %all-to-all-start = ((bf16[4,16,1024]{2,1,0:T(8,128)(2,1)}), bf16[4,16,1024]{2,1,0:T(8,128)(2,1)S(1)}, u32[]{:S(2)}, u32[]{:S(2)}) async-start(bf16[4,16,1024]{2,1,0:T(8,128)(2,1)} %pack.1), calls=%async_computation | async-start | bytes 262144 | tf_op jit(solution)/shard_map/all_to_all | solution.py:170
  13.1 0.0 all-gather.3.cloned.1.call-start
  13.1 2.8 %fresh.1 = bf16[64,24,128]{2,1,0:T(8,128)(2,1)} custom-call(bf16[128,1024]{1,0:T(8,128)(2,1)} %x_ref.3, bf16[128,128]{1,0:T(8,128)(2,1)} %b_ref.3, f32[16,128]{1,0:T(8,128)} %step_ref.3, f32[16,128]{1,0:T(8,128)} %logs_ref.3), custom_call_target="tpu_custom_call" | custom-call | flops 40000000 | bytes 1000000 | tf_op jit(solution)/shard_map/fresh/pallas_call | solution.py:172
  15.9 2.0 %all-to-all-done = bf16[4,16,1024]{2,1,0:T(8,128)(2,1)S(1)} async-done(((bf16[4,16,1024]{2,1,0:T(8,128)(2,1)}), bf16[4,16,1024]{2,1,0:T(8,128)(2,1)S(1)}, u32[]{:S(2)}, u32[]{:S(2)}) %all-to-all-start) | async-done | bytes 131104 | tf_op jit(solution)/shard_map/all_to_all | solution.py:170
  17.9 0.7 copy-done.6
  18.5 0.0 all-gather.3.cloned.1.call-update
  18.6 41.3 %all_to_all.25.got_ref = bf16[64,24,128]{2,1,0:T(8,128)(2,1)S(1)} all-to-all(bf16[64,24,128]{2,1,0:T(8,128)(2,1)} %fresh.1), channel_id=1, replica_groups=mesh['x'=4,'z'=16,'y'=4,'c'=2] {'x','z'}, dimensions={0} | all-to-all | bytes 786432 | tf_op jit(solution)/shard_map/all_to_all | solution.py:178
  59.9 0.8 scan.1
  60.7 9.1 %all-to-all-start.2 = ((bf16[64,16,128]{2,1,0:T(8,128)(2,1)}), bf16[64,16,128]{2,1,0:T(8,128)(2,1)S(1)}, u32[]{:S(2)}, u32[]{:S(2)}) async-start(bf16[64,16,128]{2,1,0:T(8,128)(2,1)} %scan.1), calls=%async_computation.2 | async-start | bytes 524288 | tf_op jit(solution)/shard_map/all_to_all | solution.py:187
  69.8 0.1 broadcast_in_dim.6
  69.9 0.1 broadcast_in_dim_reshape.3.skip_ref
  70.0 0.0 copy-done.4
  70.0 0.0 copy-done.2
  70.0 0.0 copy-done.1
  70.0 1.2 inner.1
  71.2 19.3 %all-to-all-done.2.state_ref = bf16[64,16,128]{2,1,0:T(8,128)(2,1)S(1)} async-done(((bf16[64,16,128]{2,1,0:T(8,128)(2,1)}), bf16[64,16,128]{2,1,0:T(8,128)(2,1)S(1)}, u32[]{:S(2)}, u32[]{:S(2)}) %all-to-all-start.2) | async-done | bytes 262176 | tf_op jit(solution)/shard_map/all_to_all | solution.py:187
  90.5 0.4 hidden.1
  90.9 14.1 %all_to_all.26.hidden_ref = bf16[4,128,1024]{2,1,0:T(8,128)(2,1)} all-to-all(bf16[4,128,1024]{2,1,0:T(8,128)(2,1)S(1)} %hidden.1), channel_id=1, replica_groups=mesh['x'=4,'z'=16,'y'=4,'c'=2] {'x'}, dimensions={0} | all-to-all | bytes 2097152 | tf_op jit(solution)/shard_map/all_to_all | solution.py:192
  105.0 4.8 %product.1 = bf16[4,8,128,128]{3,2,1,0:T(8,128)(2,1)} custom-call(bf16[4,128,1024]{2,1,0:T(8,128)(2,1)} %all_to_all.26.hidden_ref, bf16[16,4,16,1024]{3,2,1,0:T(8,128)(2,1)} %bitcast.7), custom_call_target="tpu_custom_call" | custom-call | flops 1073741824 | bytes 4000000 | tf_op jit(solution)/shard_map/product/pallas_call | solution.py:150
  109.8 28.8 %all_to_all.27 = bf16[32,128,128]{2,1,0:T(8,128)(2,1)S(1)} all-to-all(bf16[32,128,128]{2,1,0:T(8,128)(2,1)} %bitcast.6), channel_id=1, replica_groups=mesh['x'=4,'z'=16,'y'=4,'c'=2] {'x','y','c'}, dimensions={0} | all-to-all | bytes 2097152 | tf_op jit(solution)/shard_map/all_to_all | solution.py:194
  138.6 0.8 sum.1
  (11 shorter events, 0.0 us)
Async XLA Ops:
  6.5 63.5 %copy-start.3 = (f32[16,128]{1,0:T(8,128)S(1)}, f32[16,128]{1,0:T(8,128)}, u32[]{:S(2)}) copy-start(f32[16,128]{1,0:T(8,128)} %step_ref.3) | copy-start | bytes 24580
  6.5 63.5 %copy-start.4 = (f32[16,128]{1,0:T(8,128)S(1)}, f32[16,128]{1,0:T(8,128)}, u32[]{:S(2)}) copy-start(f32[16,128]{1,0:T(8,128)} %logs_ref.3) | copy-start | bytes 24580
  6.5 63.5 %copy-start = (bf16[128,1024]{1,0:T(8,128)(2,1)S(1)}, bf16[128,1024]{1,0:T(8,128)(2,1)}, u32[]{:S(2)}) copy-start(bf16[128,1024]{1,0:T(8,128)(2,1)} %x_ref.3) | copy-start | bytes 786436
  6.5 63.5 %copy-start.2 = (bf16[128,128]{1,0:T(8,128)(2,1)S(1)}, bf16[128,128]{1,0:T(8,128)(2,1)}, u32[]{:S(2)}) copy-start(bf16[128,128]{1,0:T(8,128)(2,1)} %b_ref.3) | copy-start | bytes 98308
  6.5 63.3 %copy-start.7 = (f32[16]{0:T(128)S(1)}, f32[16]{0:T(128)}, u32[]{:S(2)}) copy-start(f32[16]{0:T(128)} %param.13) | copy-start | bytes 196
  6.5 63.5 %copy-start.1 = (bf16[128,128]{1,0:T(8,128)(2,1)S(1)}, bf16[128,128]{1,0:T(8,128)(2,1)}, u32[]{:S(2)}) copy-start(bf16[128,128]{1,0:T(8,128)(2,1)} %c_ref.3) | copy-start | bytes 98308
  6.6 84.0 %copy-start.5 = (f32[1024]{0:T(1024)S(1)}, f32[1024]{0:T(1024)}, u32[]{:S(2)}) copy-start(f32[1024]{0:T(1024)} %param.14) | copy-start | bytes 12292
  8.2 9.7 %all-to-all-start = ((bf16[4,16,1024]{2,1,0:T(8,128)(2,1)}), bf16[4,16,1024]{2,1,0:T(8,128)(2,1)S(1)}, u32[]{:S(2)}, u32[]{:S(2)}) async-start(bf16[4,16,1024]{2,1,0:T(8,128)(2,1)} %pack.1), calls=%async_computation | async-start | bytes 262144 | tf_op jit(solution)/shard_map/all_to_all | solution.py:170
  13.1 91.9 %all-gather.3.cloned.1.call-start = ((), (), s32[]{:S(2)}) async-start(), calls=%async_computation.5 | async-start | bytes 2228224 | tf_op jit(solution)/shard_map/all_gather | solution.py:176
  17.9 0.7 copy-start.6
  60.7 29.8 %all-to-all-start.2 = ((bf16[64,16,128]{2,1,0:T(8,128)(2,1)}), bf16[64,16,128]{2,1,0:T(8,128)(2,1)S(1)}, u32[]{:S(2)}, u32[]{:S(2)}) async-start(bf16[64,16,128]{2,1,0:T(8,128)(2,1)} %scan.1), calls=%async_computation.2 | async-start | bytes 524288 | tf_op jit(solution)/shard_map/all_to_all | solution.py:187
Sparse Core Ops, SparseCore 0:
  18.7 84.6 all-gather.2

commit v5 on v4

--- a/solution.py
+++ b/solution.py
@@ -6,6 +6,10 @@
 from jax.sharding import Mesh, PartitionSpec as P
 
 NX, NZ, NY, NC = 4, 16, 4, 2
+NL = 2
+NH = NZ // NL
+GROUP = NX * NL
+OFFSETS = (0, -1, 1, -2, 2, -3, 3, -4)
 NTP = NY * NC
 TOK = 128
 HEADS = 16
@@ -15,7 +19,8 @@
 CTX = NX * NZ
 CHUNK = WIDTH // CTX
 EXTRA = 8
-COLS = 128
+HALF = TOK // 2
+COLS = 64
 LARGE = 56 * 2**20
 f32 = jnp.float32
 bf16 = jnp.bfloat16
@@ -52,10 +57,26 @@
     return dot(per_head, owner, 0, 0, HIGH)
 
 
+def halves(low, high):
+    left = iota(low.shape, 1) < COLS
+    return (
+        jnp.where(left, low, pltpu.roll(high, COLS, 1)),
+        jnp.where(left, pltpu.roll(low, COLS, 1), high),
+    )
+
+
 def pack_kernel(weight_ref, out_ref):
-    for x in range(NX):
-        for j in range(NTP):
-            out_ref[x, :, j * COLS : (j + 1) * COLS] = weight_ref[:, pl.ds((j * NX + x) * COLS, COLS)]
+    wide = GROUP * COLS
+    for pair in range(GROUP // 2):
+        for j in range(NTP // 2):
+            even, odd = (
+                weight_ref[:, pl.ds((2 * j + i) * wide + pair * 2 * COLS, 2 * COLS)].astype(f32)
+                for i in range(2)
+            )
+            columns = slice(j * 2 * COLS, (j + 1) * 2 * COLS)
+            first, second = halves(even, odd)
+            out_ref[2 * pair, :, columns] = first.astype(bf16)
+            out_ref[2 * pair + 1, :, columns] = second.astype(bf16)
 
 
 def fresh_kernel(x_ref, b_ref, step_ref, logs_ref, out_ref):
@@ -117,65 +138,76 @@
     ssm = inner_ref[...] + scale_ref[...] * dot(c_ref[...], states, 1, 1)
     meansq = jnp.mean(ssm * ssm, axis=1, keepdims=True)
     hidden = (ssm * lax.rsqrt(meansq + 1e-05) * gain_ref[...]).astype(bf16)
-    for k in range(NX):
+    for k in range(GROUP):
         out_ref[k, :, :] = hidden
 
 
-def product_kernel(hidden_ref, weight_ref, out_ref):
+def product_kernel(me_ref, hidden_ref, *refs):
+    *blocks, out_ref, weight_ref = refs
+    me = me_ref[0]
+    for offset, block_ref in zip(OFFSETS, blocks):
+        weight_ref[lax.rem(me + (offset + NH), NH)] = block_ref[...]
     depth = WIDTH // NX
     wide = weight_ref.shape[3]
-    for i in range(NX):
+    for i in range(GROUP):
         term = jnp.zeros((TOK, wide), f32)
         for k in range(NX):
-            rows = weight_ref[:, k, :, :].reshape(depth, wide)
+            rows = weight_ref[:, k * NL : (k + 1) * NL, :, :].reshape(depth, wide)
             term = term + dot(hidden_ref[i, :, k * depth : (k + 1) * depth], rows, 1, 0)
-        for j in range(wide // COLS):
-            out_ref[i, j, :, :] = term[:, j * COLS : (j + 1) * COLS].astype(bf16)
+        for j in range(NTP // 2):
+            both = term[:, j * 2 * COLS : (j + 1) * 2 * COLS]
+            first, second = halves(both[:HALF], both[HALF:])
+            out_ref[i * NTP + 2 * j, :, :] = first.astype(bf16)
+            out_ref[i * NTP + 2 * j + 1, :, :] = second.astype(bf16)
 
 
 def sum_kernel(parts_ref, out_ref):
-    for k in range(NX):
-        total = parts_ref[k, 0, :, :].astype(f32)
-        for j in range(1, NTP):
-            total = total + parts_ref[k, j, :, :].astype(f32)
-        out_ref[:, k * COLS : (k + 1) * COLS] = total.astype(bf16)
+    for pair in range(GROUP // 2):
+        totals = []
+        for k in (2 * pair, 2 * pair + 1):
+            total = parts_ref[k * NTP, :, :].astype(f32)
+            for j in range(1, NTP):
+                total = total + parts_ref[k * NTP + j, :, :].astype(f32)
+            totals.append(total)
+        columns = slice(pair * 2 * COLS, (pair + 1) * 2 * COLS)
+        first, second = halves(*totals)
+        out_ref[:HALF, columns] = first.astype(bf16)
+        out_ref[HALF:, columns] = second.astype(bf16)
 
 
 def shape(*dims, dtype=bf16):
     return jax.ShapeDtypeStruct(dims, dtype)
 
 
-def product(everyone, weight):
-    depth, tiles = weight.shape[2], 2
-    return pl.pallas_call(
-        product_kernel,
-        grid=(NTP // tiles,),
-        out_shape=shape(NX, NTP, TOK, COLS),
-        in_specs=[
-            pl.BlockSpec((NX, TOK, WIDTH), lambda n: (0, 0, 0)),
-            pl.BlockSpec((NZ, NX, depth, tiles * COLS), lambda n: (0, 0, 0, n)),
-        ],
-        out_specs=pl.BlockSpec((NX, tiles, TOK, COLS), lambda n: (0, n, 0, 0)),
-        name="product",
-        compiler_params=pltpu.CompilerParams(vmem_limit_bytes=LARGE),
-        cost_estimate=pl.CostEstimate(
-            flops=2 * NX * TOK * WIDTH * NTP * COLS, bytes_accessed=4 * 10**6, transcendentals=0
-        ),
-    )(everyone, weight)
+def ring(up, down):
+    return (
+        lax.ppermute(up, "zh", [(i, (i + 1) % NH) for i in range(NH)]),
+        lax.ppermute(down, "zh", [(i, (i - 1) % NH) for i in range(NH)]),
+    )
 
 
 def shards(x_input, b_input, c_input, step, log_decay, skip, gain, out_weight):
+    ctx = ("x", "zh", "zl")
+    members = ("x", "zl")
     depth = out_weight.shape[0]
-    swap = call(pack_kernel, shape(NX, depth, NTP * COLS), 0, 3 * 10**5, "pack", LARGE)(out_weight)
-    swap = lax.all_to_all(swap, "x", 0, 0, tiled=True)
-
+    own = call(
+        pack_kernel, shape(GROUP, depth, NTP * COLS), 0, 3 * 10**5, "pack", LARGE
+    )(out_weight)
+    own = lax.all_to_all(own, members, 0, 0, tiled=True)
     send = call(
         fresh_kernel, shape(CTX, CHUNK + EXTRA, N), 4 * 10**7, 10**6, "fresh", LARGE
     )(x_input, b_input, step, log_decay)
-    send, swap = lax.optimization_barrier((send, swap))
-    weight = lax.all_gather(swap, "z", axis=0)
-
-    got = lax.all_to_all(send, ("x", "z"), 0, 0, tiled=True)
+    send, own = lax.optimization_barrier((send, own))
+
+    got = lax.all_to_all(send, ctx, 0, 0, tiled=True)
+    up1, down1 = ring(own, own)
+    up2, down2 = ring(up1, down1)
+    got, up2, down2 = lax.optimization_barrier((got, up2, down2))
+    entering = call(scan_kernel, shape(CTX, CHUNK, N), 10**6, 7 * 10**5, "scan")(got)
+    entering, up2, down2 = lax.optimization_barrier((entering, up2, down2))
+    states = lax.all_to_all(entering, ctx, 0, 0, tiled=True)
+    up3, down3 = ring(up2, down2)
+    up4 = ring(up3, up3)[0]
     inner, scale = call(
         inner_kernel,
         (shape(TOK, WIDTH, dtype=f32), shape(TOK, WIDTH, dtype=f32)),
@@ -183,23 +215,33 @@
         2 * 10**6,
         "inner",
     )(x_input, b_input, c_input, step, log_decay, jnp.repeat(skip, P_SIZE)[None])
-    entering = call(scan_kernel, shape(CTX, CHUNK, N), 10**6, 7 * 10**5, "scan")(got)
-    states = lax.all_to_all(entering, ("x", "z"), 0, 0, tiled=True)
-
-    hidden = call(hidden_kernel, shape(NX, TOK, WIDTH), 3 * 10**7, 2 * 10**6, "hidden")(
+    states, up4, down3 = lax.optimization_barrier((states, up4, down3))
+
+    hidden = call(hidden_kernel, shape(GROUP, TOK, WIDTH), 3 * 10**7, 2 * 10**6, "hidden")(
         inner, scale, c_input, states, gain[None]
     )
-    everyone = lax.all_to_all(hidden, "x", 0, 0, tiled=True)
-    parts = product(everyone, weight).reshape(NX * NTP, TOK, COLS)
-    parts = lax.all_to_all(parts, ("x", "y", "c"), 0, 0, tiled=True)
-    return call(sum_kernel, shape(TOK, NX * COLS), 10**6, 10**6, "sum")(
-        parts.reshape(NX, NTP, TOK, COLS)
-    )
+    everyone = lax.all_to_all(hidden, members, 0, 0, tiled=True)
+    blocks = (own, up1, down1, up2, down2, up3, down3, up4)
+    me = lax.axis_index("zh").astype(jnp.int32)[None]
+    vmem = pl.BlockSpec(memory_space=pltpu.VMEM)
+    parts = pl.pallas_call(
+        product_kernel,
+        out_shape=shape(GROUP * NTP, HALF, 2 * COLS),
+        in_specs=[pl.BlockSpec(memory_space=pltpu.SMEM)] + [vmem] * (1 + len(blocks)),
+        scratch_shapes=[pltpu.VMEM((NH, GROUP, depth, NTP * COLS), bf16)],
+        name="product",
+        compiler_params=pltpu.CompilerParams(vmem_limit_bytes=32 * 2**20),
+        cost_estimate=pl.CostEstimate(
+            flops=2 * GROUP * TOK * WIDTH * NTP * COLS, bytes_accessed=4 * 10**6, transcendentals=0
+        ),
+    )(me, everyone, *blocks)
+    parts = lax.all_to_all(parts, members + ("y", "c"), 0, 0, tiled=True)
+    return call(sum_kernel, shape(TOK, GROUP * COLS), 10**6, 10**6, "sum")(parts)
 
 
 def solution(mesh):
-    fine = Mesh(mesh.devices.reshape(NX, NZ, NY, NC), ("x", "z", "y", "c"))
-    ctx, tp = ("x", "z"), ("y", "c")
+    fine = Mesh(mesh.devices.reshape(NX, NH, NL, NY, NC), ("x", "zh", "zl", "y", "c"))
+    ctx, tp = ("x", "zh", "zl"), ("y", "c")
     in_specs = (
         P(ctx, tp),
         P(ctx, tp),

time: 147 us -> 165 us (1.12)
  blocking collectives: 84.3 us -> 30.4 us
  starting transfers between devices: 13.9 us -> 65.8 us
  waiting for transfers between devices: 21.3 us -> 56.8 us
  between operations: 13.5 us -> 0.19 us
  Pallas kernels: 12.4 us -> 9.36 us
    all_to_all x3 -> x1, blocking collectives: 84.3 us -> 30.4 us  [shards(): parts = lax.all_to_all(parts, members + ('y', 'c'), 0, 0, tiled=True)]
    ppermute x0 -> x7, waiting for transfers between devices: none -> 32.8 us  [the longest x4 31.5 us: ring(): lax.ppermute(up, 'zh', [(i, (i + 1) % NH) for i in range(NH)])]
    all_to_all x2 -> x4, starting transfers between devices: 13.9 us -> 41.7 us  [the longest x1 15.8 us: shards(): states = lax.all_to_all(entering, ctx, 0, 0, tiled=True)]
    ppermute x0 -> x7, starting transfers between devices: none -> 24.1 us  [the longest x3 12.6 us: ring(): lax.ppermute(down, 'zh', [(i, (i - 1) % NH) for i in range(NH)])]
    pallas_call x4, Pallas kernels: 7.61 us -> 4.54 us  [the longest x1 1.73 us: shards(): call(pack_kernel, shape(GROUP, depth, NTP * COLS), 0, 3 * 10 ** 5, 'pack'...]
    all_to_all x2 -> x4, waiting for transfers between devices: 21.3 us -> 24 us  [the longest x1 21.2 us: shards(): everyone = lax.all_to_all(hidden, members, 0, 0, tiled=True)]
  transfers between devices with their start and end apart: 3 -> 11, of which waited for: 2 -> 7; matrix products, arithmetic and copies ran while one was open for 0% -> 0% of each run, Pallas kernels for 4% -> 2%
where the time goes in v5:
time: 165 us; the launch traced here: 164 us
  starting transfers between devices  65.8 us (40%)
  waiting for transfers between devices  56.8 us (34%)
  blocking collectives  30.4 us (18%)
  Pallas kernels  9.36 us (6%)
    ppermute x4, waiting for transfers between devices, ring(): lax.ppermute(up, 'zh', [(i, (i + 1) % NH) for i in range(NH)])  31.5 us
    all_to_all x1, blocking collectives, shards(): parts = lax.all_to_all(parts, members + ('y', 'c'), 0, 0, tiled=True)  30.4 us
    all_to_all x1, waiting for transfers between devices, shards(): everyone = lax.all_to_all(hidden, members, 0, 0, tiled=True)  21.2 us
    all_to_all x1, starting transfers between devices, shards(): states = lax.all_to_all(entering, ctx, 0, 0, tiled=True)  15.8 us
    all_to_all x1, starting transfers between devices, shards(): got = lax.all_to_all(send, ctx, 0, 0, tiled=True)  15.5 us
    ppermute x3, starting transfers between devices, ring(): lax.ppermute(down, 'zh', [(i, (i - 1) % NH) for i in range(NH)])  12.6 us
    ppermute x4, starting transfers between devices, ring(): lax.ppermute(up, 'zh', [(i, (i + 1) % NH) for i in range(NH)])  11.5 us
    all_to_all x1, starting transfers between devices, shards(): own = lax.all_to_all(own, members, 0, 0, tiled=True)  6.2 us
  transfers between devices with their start and end apart: 11, of which 7 were waited for; matrix products, arithmetic and copies ran while one was open for 0% of the time, Pallas kernels for 2%

profile of v5, /device:TPU:1, one launch (start us, length us, event | category | flops | bytes accessed | tf_op | source)
XLA Modules:
  0.0 164.1 jit_solution(15066034828903346903)
XLA Ops:
  0.1 1.7 %pack.1 = bf16[8,16,512]{2,1,0:T(8,128)(2,1)} custom-call(bf16[16,4096]{1,0:T(8,128)(2,1)} %weight_ref.1), custom_call_target="tpu_custom_call" | custom-call | bytes 300000 | tf_op jit(solution)/shard_map/pack/pallas_call | solution.py:193
  1.8 6.2 %all-to-all-start = ((bf16[8,16,512]{2,1,0:T(8,128)(2,1)}), bf16[8,16,512]{2,1,0:T(8,128)(2,1)S(1)}, u32[]{:S(2)}, u32[]{:S(2)}) async-start(bf16[8,16,512]{2,1,0:T(8,128)(2,1)} %pack.1), calls=%async_computation | async-start | bytes 262144 | tf_op jit(solution)/shard_map/all_to_all | solution.py:196
  8.0 2.8 %fresh.1 = bf16[64,24,128]{2,1,0:T(8,128)(2,1)} custom-call(bf16[128,1024]{1,0:T(8,128)(2,1)} %x_ref.3, bf16[128,128]{1,0:T(8,128)(2,1)} %b_ref.3, f32[16,128]{1,0:T(8,128)} %step_ref.3, f32[16,128]{1,0:T(8,128)} %logs_ref.3), custom_call_target="tpu_custom_call" | custom-call | flops 40000000 | bytes 1000000 | tf_op jit(solution)/shard_map/fresh/pallas_call | solution.py:197
  10.8 2.7 %all-to-all-done.refs_0_ = bf16[8,16,512]{2,1,0:T(8,128)(2,1)S(1)} async-done(((bf16[8,16,512]{2,1,0:T(8,128)(2,1)}), bf16[8,16,512]{2,1,0:T(8,128)(2,1)S(1)}, u32[]{:S(2)}, u32[]{:S(2)}) %all-to-all-start) | async-done | bytes 131104 | tf_op jit(solution)/shard_map/all_to_all | solution.py:196
  13.5 15.5 %all-to-all-start.1 = ((bf16[64,24,128]{2,1,0:T(8,128)(2,1)}), bf16[64,24,128]{2,1,0:T(8,128)(2,1)S(1)}, u32[]{:S(2)}, u32[]{:S(2)}) async-start(bf16[64,24,128]{2,1,0:T(8,128)(2,1)} %fresh.1), calls=%async_computation.1 | async-start | bytes 786432 | tf_op jit(solution)/shard_map/all_to_all | solution.py:202
  29.1 3.8 %collective-permute-start = (bf16[8,16,512]{2,1,0:T(8,128)(2,1)S(1)}, bf16[8,16,512]{2,1,0:T(8,128)(2,1)S(1)}, u32[]{:S(2)}, u32[]{:S(2)}) collective-permute-start(bf16[8,16,512]{2,1,0:T(8,128)(2,1)S(1)} %all-to-all-done.refs_0_), channel_id=1, source_target_pairs={{0,16},{16,32},{32,48},{48,64},{64,80},{80,96},{96,112},{112,0},{1... | collective-permute-start | bytes 393224 | tf_op jit(solution)/shard_map/ppermute | solution.py:184
  32.9 3.6 %collective-permute-start.2 = (bf16[8,16,512]{2,1,0:T(8,128)(2,1)S(1)}, bf16[8,16,512]{2,1,0:T(8,128)(2,1)S(1)}, u32[]{:S(2)}, u32[]{:S(2)}) collective-permute-start(bf16[8,16,512]{2,1,0:T(8,128)(2,1)S(1)} %all-to-all-done.refs_0_), channel_id=1, source_target_pairs={{0,112},{16,0},{32,16},{48,32},{64,48},{80,64},{96,80},{112,96},{1... | collective-permute-start | bytes 393224 | tf_op jit(solution)/shard_map/ppermute | solution.py:185
  36.5 15.0 %collective-permute-done.refs_1_ = bf16[8,16,512]{2,1,0:T(8,128)(2,1)S(1)} collective-permute-done((bf16[8,16,512]{2,1,0:T(8,128)(2,1)S(1)}, bf16[8,16,512]{2,1,0:T(8,128)(2,1)S(1)}, u32[]{:S(2)}, u32[]{:S(2)}) %collective-permute-start) | collective-permute-done | bytes 131104 | tf_op jit(solution)/shard_map/ppermute | solution.py:184
  51.5 1.9 %collective-permute-start.1 = (bf16[8,16,512]{2,1,0:T(8,128)(2,1)S(1)}, bf16[8,16,512]{2,1,0:T(8,128)(2,1)S(1)}, u32[]{:S(2)}, u32[]{:S(2)}) collective-permute-start(bf16[8,16,512]{2,1,0:T(8,128)(2,1)S(1)} %collective-permute-done.refs_1_), channel_id=1, source_target_pairs={{0,16},{16,32},{32,48},{48,64},{64,80},{80,96},{96,112},{112,0},{1... | collective-permute-start | bytes 393224 | tf_op jit(solution)/shard_map/ppermute | solution.py:184
  53.4 5.5 %collective-permute-start.3 = (bf16[8,16,512]{2,1,0:T(8,128)(2,1)S(1)}, bf16[8,16,512]{2,1,0:T(8,128)(2,1)S(1)}, u32[]{:S(2)}, u32[]{:S(2)}) collective-permute-start(bf16[8,16,512]{2,1,0:T(8,128)(2,1)S(1)} %collective-permute-done.2.refs_2_), channel_id=1, source_target_pairs={{0,112},{16,0},{32,16},{48,32},{64,48},{80,64},{96,80},{112,96},{1... | collective-permute-start | bytes 393224 | tf_op jit(solution)/shard_map/ppermute | solution.py:185
  58.9 1.8 %collective-permute-done.1.refs_3_ = bf16[8,16,512]{2,1,0:T(8,128)(2,1)S(1)} collective-permute-done((bf16[8,16,512]{2,1,0:T(8,128)(2,1)S(1)}, bf16[8,16,512]{2,1,0:T(8,128)(2,1)S(1)}, u32[]{:S(2)}, u32[]{:S(2)}) %collective-permute-start.1) | collective-permute-done | bytes 131104 | tf_op jit(solution)/shard_map/ppermute | solution.py:184
  60.7 1.3 collective-permute-done.3.refs_4_
  62.9 15.8 %all-to-all-start.2 = ((bf16[64,16,128]{2,1,0:T(8,128)(2,1)}), bf16[64,16,128]{2,1,0:T(8,128)(2,1)S(1)}, u32[]{:S(2)}, u32[]{:S(2)}) async-start(bf16[64,16,128]{2,1,0:T(8,128)(2,1)} %scan.1), calls=%async_computation.2 | async-start | bytes 524288 | tf_op jit(solution)/shard_map/all_to_all | solution.py:208
  78.7 3.8 %collective-permute-start.4 = (bf16[8,16,512]{2,1,0:T(8,128)(2,1)S(1)}, bf16[8,16,512]{2,1,0:T(8,128)(2,1)S(1)}, u32[]{:S(2)}, u32[]{:S(2)}) collective-permute-start(bf16[8,16,512]{2,1,0:T(8,128)(2,1)S(1)} %collective-permute-done.1.refs_3_), channel_id=1, source_target_pairs={{0,16},{16,32},{32,48},{48,64},{64,80},{80,96},{96,112},{112,0},{1... | collective-permute-start | bytes 393224 | tf_op jit(solution)/shard_map/ppermute | solution.py:184
  82.5 3.6 %collective-permute-start.6 = (bf16[8,16,512]{2,1,0:T(8,128)(2,1)S(1)}, bf16[8,16,512]{2,1,0:T(8,128)(2,1)S(1)}, u32[]{:S(2)}, u32[]{:S(2)}) collective-permute-start(bf16[8,16,512]{2,1,0:T(8,128)(2,1)S(1)} %collective-permute-done.3.refs_4_), channel_id=1, source_target_pairs={{0,112},{16,0},{32,16},{48,32},{64,48},{80,64},{96,80},{112,96},{1... | collective-permute-start | bytes 393224 | tf_op jit(solution)/shard_map/ppermute | solution.py:185
  86.1 10.2 %collective-permute-done.4.refs_5_ = bf16[8,16,512]{2,1,0:T(8,128)(2,1)S(1)} collective-permute-done((bf16[8,16,512]{2,1,0:T(8,128)(2,1)S(1)}, bf16[8,16,512]{2,1,0:T(8,128)(2,1)S(1)}, u32[]{:S(2)}, u32[]{:S(2)}) %collective-permute-start.4) | collective-permute-done | bytes 131104 | tf_op jit(solution)/shard_map/ppermute | solution.py:184
  96.4 1.9 %collective-permute-start.5 = (bf16[8,16,512]{2,1,0:T(8,128)(2,1)S(1)}, bf16[8,16,512]{2,1,0:T(8,128)(2,1)S(1)}, u32[]{:S(2)}, u32[]{:S(2)}) collective-permute-start(bf16[8,16,512]{2,1,0:T(8,128)(2,1)S(1)} %collective-permute-done.4.refs_5_), channel_id=1, source_target_pairs={{0,16},{16,32},{32,48},{48,64},{64,80},{80,96},{96,112},{112,0},{1... | collective-permute-start | bytes 393224 | tf_op jit(solution)/shard_map/ppermute | solution.py:184
  98.5 1.2 inner.1
  99.7 4.5 %collective-permute-done.5.refs_7_ = bf16[8,16,512]{2,1,0:T(8,128)(2,1)S(1)} collective-permute-done((bf16[8,16,512]{2,1,0:T(8,128)(2,1)S(1)}, bf16[8,16,512]{2,1,0:T(8,128)(2,1)S(1)}, u32[]{:S(2)}, u32[]{:S(2)}) %collective-permute-start.5) | collective-permute-done | bytes 131104 | tf_op jit(solution)/shard_map/ppermute | solution.py:184
  104.6 1.3 copy-done
  105.9 4.1 %all-to-all-start.3 = ((bf16[8,128,1024]{2,1,0:T(8,128)(2,1)}), bf16[8,128,1024]{2,1,0:T(8,128)(2,1)S(1)}, u32[]{:S(2)}, u32[]{:S(2)}) async-start(bf16[8,128,1024]{2,1,0:T(8,128)(2,1)} %copy-done), calls=%async_computation.3 | async-start | bytes 4194304 | tf_op jit(solution)/shard_map/all_to_all | solution.py:223
  110.0 21.2 %all-to-all-done.3.hidden_ref = bf16[8,128,1024]{2,1,0:T(8,128)(2,1)S(1)} async-done(((bf16[8,128,1024]{2,1,0:T(8,128)(2,1)}), bf16[8,128,1024]{2,1,0:T(8,128)(2,1)S(1)}, u32[]{:S(2)}, u32[]{:S(2)}) %all-to-all-start.3) | async-done | bytes 2097184 | tf_op jit(solution)/shard_map/all_to_all | solution.py:223
  131.3 1.5 product.1
  132.8 30.4 %all_to_all.25.parts_ref = bf16[64,64,128]{2,1,0:T(8,128)(2,1)S(1)} all-to-all(bf16[64,64,128]{2,1,0:T(8,128)(2,1)S(1)} %product.1), channel_id=1, replica_groups=mesh['x'=4,'zh'=8,'zl'=2,'y'=4,'c'=2] {'x','zl','y','c'}, dimensions={0} | all-to-all | bytes 2097152 | tf_op jit(solution)/shard_map/all_to_all | solution.py:238
  (24 shorter events, 2.3 us)
Async XLA Ops:
  0.0 98.5 %copy-start.4 = (f32[16,128]{1,0:T(8,128)S(1)}, f32[16,128]{1,0:T(8,128)}, u32[]{:S(2)}) copy-start(f32[16,128]{1,0:T(8,128)} %step_ref.3) | copy-start | bytes 24580
  0.0 98.5 %copy-start.5 = (f32[16,128]{1,0:T(8,128)S(1)}, f32[16,128]{1,0:T(8,128)}, u32[]{:S(2)}) copy-start(f32[16,128]{1,0:T(8,128)} %logs_ref.3) | copy-start | bytes 24580
  0.0 98.5 %copy-start.1 = (bf16[128,1024]{1,0:T(8,128)(2,1)S(1)}, bf16[128,1024]{1,0:T(8,128)(2,1)}, u32[]{:S(2)}) copy-start(bf16[128,1024]{1,0:T(8,128)(2,1)} %x_ref.3) | copy-start | bytes 786436
  0.0 98.5 %copy-start.3 = (bf16[128,128]{1,0:T(8,128)(2,1)S(1)}, bf16[128,128]{1,0:T(8,128)(2,1)}, u32[]{:S(2)}) copy-start(bf16[128,128]{1,0:T(8,128)(2,1)} %b_ref.3) | copy-start | bytes 98308
  0.0 98.3 %copy-start.7 = (f32[16]{0:T(128)S(1)}, f32[16]{0:T(128)}, u32[]{:S(2)}) copy-start(f32[16]{0:T(128)} %param.13) | copy-start | bytes 196
  0.0 98.5 %copy-start.2 = (bf16[128,128]{1,0:T(8,128)(2,1)S(1)}, bf16[128,128]{1,0:T(8,128)(2,1)}, u32[]{:S(2)}) copy-start(bf16[128,128]{1,0:T(8,128)(2,1)} %c_ref.3) | copy-start | bytes 98308
  0.0 104.1 %copy-start.6 = (f32[1024]{0:T(1024)S(1)}, f32[1024]{0:T(1024)}, u32[]{:S(2)}) copy-start(f32[1024]{0:T(1024)} %param.14) | copy-start | bytes 12292
  1.8 11.8 %all-to-all-start = ((bf16[8,16,512]{2,1,0:T(8,128)(2,1)}), bf16[8,16,512]{2,1,0:T(8,128)(2,1)S(1)}, u32[]{:S(2)}, u32[]{:S(2)}) async-start(bf16[8,16,512]{2,1,0:T(8,128)(2,1)} %pack.1), calls=%async_computation | async-start | bytes 262144 | tf_op jit(solution)/shard_map/all_to_all | solution.py:196
  13.5 48.5 %all-to-all-start.1 = ((bf16[64,24,128]{2,1,0:T(8,128)(2,1)}), bf16[64,24,128]{2,1,0:T(8,128)(2,1)S(1)}, u32[]{:S(2)}, u32[]{:S(2)}) async-start(bf16[64,24,128]{2,1,0:T(8,128)(2,1)} %fresh.1), calls=%async_computation.1 | async-start | bytes 786432 | tf_op jit(solution)/shard_map/all_to_all | solution.py:202
  29.1 22.4 %collective-permute-start = (bf16[8,16,512]{2,1,0:T(8,128)(2,1)S(1)}, bf16[8,16,512]{2,1,0:T(8,128)(2,1)S(1)}, u32[]{:S(2)}, u32[]{:S(2)}) collective-permute-start(bf16[8,16,512]{2,1,0:T(8,128)(2,1)S(1)} %all-to-all-done.refs_0_), channel_id=1, source_target_pairs={{0,16},{16,32},{32,48},{48,64},{64,80},{80,96},{96,112},{112,0},{1... | collective-permute-start | bytes 393224 | tf_op jit(solution)/shard_map/ppermute | solution.py:184
  32.9 20.5 %collective-permute-start.2 = (bf16[8,16,512]{2,1,0:T(8,128)(2,1)S(1)}, bf16[8,16,512]{2,1,0:T(8,128)(2,1)S(1)}, u32[]{:S(2)}, u32[]{:S(2)}) collective-permute-start(bf16[8,16,512]{2,1,0:T(8,128)(2,1)S(1)} %all-to-all-done.refs_0_), channel_id=1, source_target_pairs={{0,112},{16,0},{32,16},{48,32},{64,48},{80,64},{96,80},{112,96},{1... | collective-permute-start | bytes 393224 | tf_op jit(solution)/shard_map/ppermute | solution.py:185
  51.5 9.2 %collective-permute-start.1 = (bf16[8,16,512]{2,1,0:T(8,128)(2,1)S(1)}, bf16[8,16,512]{2,1,0:T(8,128)(2,1)S(1)}, u32[]{:S(2)}, u32[]{:S(2)}) collective-permute-start(bf16[8,16,512]{2,1,0:T(8,128)(2,1)S(1)} %collective-permute-done.refs_1_), channel_id=1, source_target_pairs={{0,16},{16,32},{32,48},{48,64},{64,80},{80,96},{96,112},{112,0},{1... | collective-permute-start | bytes 393224 | tf_op jit(solution)/shard_map/ppermute | solution.py:184
  53.4 8.6 %collective-permute-start.3 = (bf16[8,16,512]{2,1,0:T(8,128)(2,1)S(1)}, bf16[8,16,512]{2,1,0:T(8,128)(2,1)S(1)}, u32[]{:S(2)}, u32[]{:S(2)}) collective-permute-start(bf16[8,16,512]{2,1,0:T(8,128)(2,1)S(1)} %collective-permute-done.2.refs_2_), channel_id=1, source_target_pairs={{0,112},{16,0},{32,16},{48,32},{64,48},{80,64},{96,80},{112,96},{1... | collective-permute-start | bytes 393224 | tf_op jit(solution)/shard_map/ppermute | solution.py:185
  62.9 41.3 %all-to-all-start.2 = ((bf16[64,16,128]{2,1,0:T(8,128)(2,1)}), bf16[64,16,128]{2,1,0:T(8,128)(2,1)S(1)}, u32[]{:S(2)}, u32[]{:S(2)}) async-start(bf16[64,16,128]{2,1,0:T(8,128)(2,1)} %scan.1), calls=%async_computation.2 | async-start | bytes 524288 | tf_op jit(solution)/shard_map/all_to_all | solution.py:208
  78.7 17.6 %collective-permute-start.4 = (bf16[8,16,512]{2,1,0:T(8,128)(2,1)S(1)}, bf16[8,16,512]{2,1,0:T(8,128)(2,1)S(1)}, u32[]{:S(2)}, u32[]{:S(2)}) collective-permute-start(bf16[8,16,512]{2,1,0:T(8,128)(2,1)S(1)} %collective-permute-done.1.refs_3_), channel_id=1, source_target_pairs={{0,16},{16,32},{32,48},{48,64},{64,80},{80,96},{96,112},{112,0},{1... | collective-permute-start | bytes 393224 | tf_op jit(solution)/shard_map/ppermute | solution.py:184
  82.5 17.1 %collective-permute-start.6 = (bf16[8,16,512]{2,1,0:T(8,128)(2,1)S(1)}, bf16[8,16,512]{2,1,0:T(8,128)(2,1)S(1)}, u32[]{:S(2)}, u32[]{:S(2)}) collective-permute-start(bf16[8,16,512]{2,1,0:T(8,128)(2,1)S(1)} %collective-permute-done.3.refs_4_), channel_id=1, source_target_pairs={{0,112},{16,0},{32,16},{48,32},{64,48},{80,64},{96,80},{112,96},{1... | collective-permute-start | bytes 393224 | tf_op jit(solution)/shard_map/ppermute | solution.py:185
  96.4 7.8 %collective-permute-start.5 = (bf16[8,16,512]{2,1,0:T(8,128)(2,1)S(1)}, bf16[8,16,512]{2,1,0:T(8,128)(2,1)S(1)}, u32[]{:S(2)}, u32[]{:S(2)}) collective-permute-start(bf16[8,16,512]{2,1,0:T(8,128)(2,1)S(1)} %collective-permute-done.4.refs_5_), channel_id=1, source_target_pairs={{0,16},{16,32},{32,48},{48,64},{64,80},{80,96},{96,112},{112,0},{1... | collective-permute-start | bytes 393224 | tf_op jit(solution)/shard_map/ppermute | solution.py:184
  104.6 1.3 copy-start
  105.9 25.3 %all-to-all-start.3 = ((bf16[8,128,1024]{2,1,0:T(8,128)(2,1)}), bf16[8,128,1024]{2,1,0:T(8,128)(2,1)S(1)}, u32[]{:S(2)}, u32[]{:S(2)}) async-start(bf16[8,128,1024]{2,1,0:T(8,128)(2,1)} %copy-done), calls=%async_computation.3 | async-start | bytes 4194304 | tf_op jit(solution)/shard_map/all_to_all | solution.py:223

commit v6 on v4

--- a/solution.py
+++ b/solution.py
@@ -52,10 +52,13 @@
     return dot(per_head, owner, 0, 0, HIGH)
 
 
-def pack_kernel(weight_ref, out_ref):
+def pack_kernel(weight_ref, out_ref, held_ref, sem):
+    copy = pltpu.make_async_copy(weight_ref, held_ref, sem)
+    copy.start()
+    copy.wait()
     for x in range(NX):
         for j in range(NTP):
-            out_ref[x, :, j * COLS : (j + 1) * COLS] = weight_ref[:, pl.ds((j * NX + x) * COLS, COLS)]
+            out_ref[x, :, j * COLS : (j + 1) * COLS] = held_ref[:, pl.ds((j * NX + x) * COLS, COLS)]
 
 
 def fresh_kernel(x_ref, b_ref, step_ref, logs_ref, out_ref):
@@ -121,16 +124,35 @@
         out_ref[k, :, :] = hidden
 
 
-def product_kernel(hidden_ref, weight_ref, out_ref):
+def product_kernel(hidden_ref, weight_ref, out_ref, tokens_ref, held_ref, total_ref, sems):
     depth = WIDTH // NX
     wide = weight_ref.shape[3]
-    for i in range(NX):
-        term = jnp.zeros((TOK, wide), f32)
-        for k in range(NX):
-            rows = weight_ref[:, k, :, :].reshape(depth, wide)
-            term = term + dot(hidden_ref[i, :, k * depth : (k + 1) * depth], rows, 1, 0)
-        for j in range(wide // COLS):
-            out_ref[i, j, :, :] = term[:, j * COLS : (j + 1) * COLS].astype(bf16)
+    copies = []
+    for k in range(NX):
+        part = hidden_ref.at[:, :, pl.ds(k * depth, depth)]
+        copies.append(
+            (
+                pltpu.make_async_copy(part, tokens_ref.at[k], sems.at[0, k]),
+                pltpu.make_async_copy(weight_ref.at[:, k], held_ref.at[k], sems.at[1, k]),
+            )
+        )
+    for pair in copies:
+        for copy in pair:
+            copy.start()
+    for k in range(NX):
+        for copy in copies[k]:
+            copy.wait()
+        rows = held_ref[k].reshape(depth, wide)
+        for i in range(NX):
+            term = dot(tokens_ref[k, i], rows, 1, 0)
+            if k == 0:
+                total_ref[i] = term
+            elif k < NX - 1:
+                total_ref[i] += term
+            else:
+                term = (total_ref[i] + term).astype(bf16)
+                for j in range(wide // COLS):
+                    out_ref[i, j, :, :] = term[:, j * COLS : (j + 1) * COLS]
 
 
 def sum_kernel(parts_ref, out_ref):
@@ -146,18 +168,19 @@
 
 
 def product(everyone, weight):
-    depth, tiles = weight.shape[2], 2
+    depth, wide = weight.shape[2], weight.shape[3]
     return pl.pallas_call(
         product_kernel,
-        grid=(NTP // tiles,),
         out_shape=shape(NX, NTP, TOK, COLS),
-        in_specs=[
-            pl.BlockSpec((NX, TOK, WIDTH), lambda n: (0, 0, 0)),
-            pl.BlockSpec((NZ, NX, depth, tiles * COLS), lambda n: (0, 0, 0, n)),
+        in_specs=[pl.BlockSpec(memory_space=pl.ANY)] * 2,
+        scratch_shapes=[
+            pltpu.VMEM((NX, NX, TOK, WIDTH // NX), bf16),
+            pltpu.VMEM((NX, NZ, depth, wide), bf16),
+            pltpu.VMEM((NX, TOK, wide), f32),
+            pltpu.SemaphoreType.DMA((2, NX)),
         ],
-        out_specs=pl.BlockSpec((NX, tiles, TOK, COLS), lambda n: (0, n, 0, 0)),
         name="product",
-        compiler_params=pltpu.CompilerParams(vmem_limit_bytes=LARGE),
+        compiler_params=pltpu.CompilerParams(vmem_limit_bytes=52 * 2**20),
         cost_estimate=pl.CostEstimate(
             flops=2 * NX * TOK * WIDTH * NTP * COLS, bytes_accessed=4 * 10**6, transcendentals=0
         ),
@@ -166,7 +189,15 @@
 
 def shards(x_input, b_input, c_input, step, log_decay, skip, gain, out_weight):
     depth = out_weight.shape[0]
-    swap = call(pack_kernel, shape(NX, depth, NTP * COLS), 0, 3 * 10**5, "pack", LARGE)(out_weight)
+    swap = pl.pallas_call(
+        pack_kernel,
+        out_shape=shape(NX, depth, NTP * COLS),
+        in_specs=[pl.BlockSpec(memory_space=pl.ANY)],
+        scratch_shapes=[pltpu.VMEM(out_weight.shape, bf16), pltpu.SemaphoreType.DMA(())],
+        name="pack",
+        compiler_params=pltpu.CompilerParams(vmem_limit_bytes=LARGE),
+        cost_estimate=pl.CostEstimate(flops=0, bytes_accessed=3 * 10**5, transcendentals=0),
+    )(out_weight)
     swap = lax.all_to_all(swap, "x", 0, 0, tiled=True)
 
     send = call(

time: 147 us -> 144 us (0.980)
  Pallas kernels: 12.4 us -> 10.3 us
    pallas_call x2, Pallas kernels: 6.45 us -> 4.3 us  [the longest x1 2.65 us: product(): pl.pallas_call(product_kernel, out_shape=shape(NX, NTP, TOK, COLS), in_sp...]
where the time goes in v6:
time: 144 us
  blocking collectives  84.1 us (58%)
  waiting for transfers between devices  21.4 us (15%)
  starting transfers between devices  13.9 us (10%)
  between operations  13.5 us (9%)
  Pallas kernels  10.3 us (7%)
    all_to_all x1, blocking collectives, shards(): got = lax.all_to_all(send, ('x', 'z'), 0, 0, tiled=True)  41.3 us
    all_to_all x1, blocking collectives, shards(): parts = lax.all_to_all(parts, ('x', 'y', 'c'), 0, 0, tiled=True)  28.7 us
    all_to_all x1, waiting for transfers between devices, shards(): states = lax.all_to_all(entering, ('x', 'z'), 0, 0, tiled=True)  19.3 us
    all_to_all x1, blocking collectives, shards(): everyone = lax.all_to_all(hidden, 'x', 0, 0, tiled=True)  14.1 us
    all_to_all x1, starting transfers between devices, shards(): states = lax.all_to_all(entering, ('x', 'z'), 0, 0, tiled=True)  9.08 us
    all_to_all x1, starting transfers between devices, shards(): swap = lax.all_to_all(swap, 'x', 0, 0, tiled=True)  4.85 us
  transfers between devices with their start and end apart: 3, of which 2 were waited for; matrix products, arithmetic and copies ran while one was open for 0% of the time, Pallas kernels for 4%

profile of v6, /device:TPU:1, one launch (start us, length us, event | category | flops | bytes accessed | tf_op | source)
XLA Modules:
  0.0 144.0 jit_solution(5341505173679212930)
XLA Ops:
  6.5 0.0 copy-start.1
  6.6 0.0 copy-start.5
  6.6 1.6 %pack.1 = bf16[4,16,1024]{2,1,0:T(8,128)(2,1)} custom-call(bf16[16,4096]{1,0:T(8,128)(2,1)} %weight_ref.1), custom_call_target="tpu_custom_call" | custom-call | bytes 300000 | tf_op jit(solution)/shard_map/pack/pallas_call | solution.py:192
  8.2 4.9 %all-to-all-start = ((bf16[4,16,1024]{2,1,0:T(8,128)(2,1)}), bf16[4,16,1024]{2,1,0:T(8,128)(2,1)S(1)}, u32[]{:S(2)}, u32[]{:S(2)}) async-start(bf16[4,16,1024]{2,1,0:T(8,128)(2,1)} %pack.1), calls=%async_computation | async-start | bytes 262144 | tf_op jit(solution)/shard_map/all_to_all | solution.py:201
  13.1 0.0 all-gather.3.cloned.1.call-start
  13.1 2.8 %fresh.1 = bf16[64,24,128]{2,1,0:T(8,128)(2,1)} custom-call(bf16[128,1024]{1,0:T(8,128)(2,1)} %x_ref.3, bf16[128,128]{1,0:T(8,128)(2,1)} %b_ref.3, f32[16,128]{1,0:T(8,128)} %step_ref.3, f32[16,128]{1,0:T(8,128)} %logs_ref.3), custom_call_target="tpu_custom_call" | custom-call | flops 40000000 | bytes 1000000 | tf_op jit(solution)/shard_map/fresh/pallas_call | solution.py:203
  15.9 2.0 %all-to-all-done = bf16[4,16,1024]{2,1,0:T(8,128)(2,1)S(1)} async-done(((bf16[4,16,1024]{2,1,0:T(8,128)(2,1)}), bf16[4,16,1024]{2,1,0:T(8,128)(2,1)S(1)}, u32[]{:S(2)}, u32[]{:S(2)}) %all-to-all-start) | async-done | bytes 131104 | tf_op jit(solution)/shard_map/all_to_all | solution.py:201
  17.9 0.7 copy-done.6
  18.6 0.0 all-gather.3.cloned.1.call-update
  18.6 41.3 %all_to_all.25.got_ref = bf16[64,24,128]{2,1,0:T(8,128)(2,1)S(1)} all-to-all(bf16[64,24,128]{2,1,0:T(8,128)(2,1)} %fresh.1), channel_id=1, replica_groups=mesh['x'=4,'z'=16,'y'=4,'c'=2] {'x','z'}, dimensions={0} | all-to-all | bytes 786432 | tf_op jit(solution)/shard_map/all_to_all | solution.py:209
  59.9 0.8 scan.1
  60.8 9.1 %all-to-all-start.2 = ((bf16[64,16,128]{2,1,0:T(8,128)(2,1)}), bf16[64,16,128]{2,1,0:T(8,128)(2,1)S(1)}, u32[]{:S(2)}, u32[]{:S(2)}) async-start(bf16[64,16,128]{2,1,0:T(8,128)(2,1)} %scan.1), calls=%async_computation.2 | async-start | bytes 524288 | tf_op jit(solution)/shard_map/all_to_all | solution.py:218
  69.9 0.0 copy-done.7
  69.9 0.1 broadcast_in_dim.6
  69.9 0.1 broadcast_in_dim_reshape.3.skip_ref
  70.0 0.0 copy-done.3
  70.0 0.0 copy-done.4
  70.1 1.2 inner.1
  71.2 19.3 %all-to-all-done.2.state_ref = bf16[64,16,128]{2,1,0:T(8,128)(2,1)S(1)} async-done(((bf16[64,16,128]{2,1,0:T(8,128)(2,1)}), bf16[64,16,128]{2,1,0:T(8,128)(2,1)S(1)}, u32[]{:S(2)}, u32[]{:S(2)}) %all-to-all-start.2) | async-done | bytes 262176 | tf_op jit(solution)/shard_map/all_to_all | solution.py:218
  90.5 0.4 hidden.1
  90.9 14.1 %all_to_all.26.hidden_ref = bf16[4,128,1024]{2,1,0:T(8,128)(2,1)} all-to-all(bf16[4,128,1024]{2,1,0:T(8,128)(2,1)S(1)} %hidden.1), channel_id=1, replica_groups=mesh['x'=4,'z'=16,'y'=4,'c'=2] {'x'}, dimensions={0} | all-to-all | bytes 2097152 | tf_op jit(solution)/shard_map/all_to_all | solution.py:223
  105.0 2.7 %product.1 = bf16[4,8,128,128]{3,2,1,0:T(8,128)(2,1)S(1)} custom-call(bf16[4,128,1024]{2,1,0:T(8,128)(2,1)} %all_to_all.26.hidden_ref, bf16[16,4,16,1024]{3,2,1,0:T(8,128)(2,1)} %bitcast.7), custom_call_target="tpu_custom_call" | custom-call | flops 1073741824 | bytes 4000000 | tf_op jit(solution)/shard_map/product/pallas_call | solution.py:172
  107.7 28.7 %all_to_all.27 = bf16[32,128,128]{2,1,0:T(8,128)(2,1)S(1)} all-to-all(bf16[32,128,128]{2,1,0:T(8,128)(2,1)S(1)} %bitcast.5), channel_id=1, replica_groups=mesh['x'=4,'z'=16,'y'=4,'c'=2] {'x','y','c'}, dimensions={0} | all-to-all | bytes 2097152 | tf_op jit(solution)/shard_map/all_to_all | solution.py:225
  136.3 0.8 sum.1
  (11 shorter events, 0.0 us)
Async XLA Ops:
  6.5 63.5 %copy-start.3 = (f32[16,128]{1,0:T(8,128)S(1)}, f32[16,128]{1,0:T(8,128)}, u32[]{:S(2)}) copy-start(f32[16,128]{1,0:T(8,128)} %step_ref.3) | copy-start | bytes 24580
  6.5 63.5 %copy-start.4 = (f32[16,128]{1,0:T(8,128)S(1)}, f32[16,128]{1,0:T(8,128)}, u32[]{:S(2)}) copy-start(f32[16,128]{1,0:T(8,128)} %logs_ref.3) | copy-start | bytes 24580
  6.5 63.5 %copy-start = (bf16[128,1024]{1,0:T(8,128)(2,1)S(1)}, bf16[128,1024]{1,0:T(8,128)(2,1)}, u32[]{:S(2)}) copy-start(bf16[128,1024]{1,0:T(8,128)(2,1)} %x_ref.3) | copy-start | bytes 786436
  6.5 63.5 %copy-start.2 = (bf16[128,128]{1,0:T(8,128)(2,1)S(1)}, bf16[128,128]{1,0:T(8,128)(2,1)}, u32[]{:S(2)}) copy-start(bf16[128,128]{1,0:T(8,128)(2,1)} %b_ref.3) | copy-start | bytes 98308
  6.5 63.3 %copy-start.7 = (f32[16]{0:T(128)S(1)}, f32[16]{0:T(128)}, u32[]{:S(2)}) copy-start(f32[16]{0:T(128)} %param.13) | copy-start | bytes 196
  6.5 63.5 %copy-start.1 = (bf16[128,128]{1,0:T(8,128)(2,1)S(1)}, bf16[128,128]{1,0:T(8,128)(2,1)}, u32[]{:S(2)}) copy-start(bf16[128,128]{1,0:T(8,128)(2,1)} %c_ref.3) | copy-start | bytes 98308
  6.6 84.0 %copy-start.5 = (f32[1024]{0:T(1024)S(1)}, f32[1024]{0:T(1024)}, u32[]{:S(2)}) copy-start(f32[1024]{0:T(1024)} %param.14) | copy-start | bytes 12292
  8.2 9.7 %all-to-all-start = ((bf16[4,16,1024]{2,1,0:T(8,128)(2,1)}), bf16[4,16,1024]{2,1,0:T(8,128)(2,1)S(1)}, u32[]{:S(2)}, u32[]{:S(2)}) async-start(bf16[4,16,1024]{2,1,0:T(8,128)(2,1)} %pack.1), calls=%async_computation | async-start | bytes 262144 | tf_op jit(solution)/shard_map/all_to_all | solution.py:201
  13.1 91.9 %all-gather.3.cloned.1.call-start = ((), (), s32[]{:S(2)}) async-start(), calls=%async_computation.5 | async-start | bytes 2228224 | tf_op jit(solution)/shard_map/all_gather | solution.py:207
  17.9 0.7 copy-start.6
  60.8 29.8 %all-to-all-start.2 = ((bf16[64,16,128]{2,1,0:T(8,128)(2,1)}), bf16[64,16,128]{2,1,0:T(8,128)(2,1)S(1)}, u32[]{:S(2)}, u32[]{:S(2)}) async-start(bf16[64,16,128]{2,1,0:T(8,128)(2,1)} %scan.1), calls=%async_computation.2 | async-start | bytes 524288 | tf_op jit(solution)/shard_map/all_to_all | solution.py:218
Sparse Core Ops, SparseCore 0:
  18.7 84.6 all-gather.2

commit v7 on v6

--- a/solution.py
+++ b/solution.py
@@ -1,3 +1,5 @@
+import functools
+
 import jax
 import jax.numpy as jnp
 from jax import lax
@@ -52,13 +54,18 @@
     return dot(per_head, owner, 0, 0, HIGH)
 
 
-def pack_kernel(weight_ref, out_ref, held_ref, sem):
+def pack_kernel(core_ref, weight_ref, out_ref, held_ref, sem):
     copy = pltpu.make_async_copy(weight_ref, held_ref, sem)
     copy.start()
     copy.wait()
+    first = core_ref[0] == 0
     for x in range(NX):
-        for j in range(NTP):
-            out_ref[x, :, j * COLS : (j + 1) * COLS] = held_ref[:, pl.ds((j * NX + x) * COLS, COLS)]
+        for y in range(NY):
+            even, odd = (
+                held_ref[:, pl.ds(((y * NC + c) * NX + x) * COLS, COLS)] for c in range(NC)
+            )
+            out_ref[x, :, y * COLS : (y + 1) * COLS] = jnp.where(first, even, odd)
+            out_ref[x, :, (NY + y) * COLS : (NY + y + 1) * COLS] = jnp.where(first, odd, even)
 
 
 def fresh_kernel(x_ref, b_ref, step_ref, logs_ref, out_ref):
@@ -124,16 +131,17 @@
         out_ref[k, :, :] = hidden
 
 
-def product_kernel(hidden_ref, weight_ref, out_ref, tokens_ref, held_ref, total_ref, sems):
+def product_kernel(half, hidden_ref, weight_ref, out_ref, tokens_ref, held_ref, total_ref, sems):
     depth = WIDTH // NX
-    wide = weight_ref.shape[3]
+    wide = NY * COLS
     copies = []
     for k in range(NX):
         part = hidden_ref.at[:, :, pl.ds(k * depth, depth)]
+        rows = weight_ref.at[:, k, :, pl.ds(half * wide, wide)]
         copies.append(
             (
                 pltpu.make_async_copy(part, tokens_ref.at[k], sems.at[0, k]),
-                pltpu.make_async_copy(weight_ref.at[:, k], held_ref.at[k], sems.at[1, k]),
+                pltpu.make_async_copy(rows, held_ref.at[k], sems.at[1, k]),
             )
         )
     for pair in copies:
@@ -150,15 +158,19 @@
             elif k < NX - 1:
                 total_ref[i] += term
             else:
-                term = (total_ref[i] + term).astype(bf16)
-                for j in range(wide // COLS):
+                term = (total_ref[i] + term).astype(out_ref.dtype)
+                for j in range(NY):
                     out_ref[i, j, :, :] = term[:, j * COLS : (j + 1) * COLS]
 
 
+def pair_kernel(mine_ref, other_ref, out_ref):
+    out_ref[...] = (mine_ref[...] + other_ref[...].astype(f32)).astype(bf16)
+
+
 def sum_kernel(parts_ref, out_ref):
     for k in range(NX):
         total = parts_ref[k, 0, :, :].astype(f32)
-        for j in range(1, NTP):
+        for j in range(1, NY):
             total = total + parts_ref[k, j, :, :].astype(f32)
         out_ref[:, k * COLS : (k + 1) * COLS] = total.astype(bf16)
 
@@ -167,11 +179,11 @@
     return jax.ShapeDtypeStruct(dims, dtype)
 
 
-def product(everyone, weight):
-    depth, wide = weight.shape[2], weight.shape[3]
+def product(everyone, weight, half):
+    depth, wide = weight.shape[2], NY * COLS
     return pl.pallas_call(
-        product_kernel,
-        out_shape=shape(NX, NTP, TOK, COLS),
+        functools.partial(product_kernel, half),
+        out_shape=shape(NX, NY, TOK, COLS, dtype=bf16 if half else f32),
         in_specs=[pl.BlockSpec(memory_space=pl.ANY)] * 2,
         scratch_shapes=[
             pltpu.VMEM((NX, NX, TOK, WIDTH // NX), bf16),
@@ -179,25 +191,26 @@
             pltpu.VMEM((NX, TOK, wide), f32),
             pltpu.SemaphoreType.DMA((2, NX)),
         ],
-        name="product",
+        name="other" if half else "mine",
         compiler_params=pltpu.CompilerParams(vmem_limit_bytes=52 * 2**20),
         cost_estimate=pl.CostEstimate(
-            flops=2 * NX * TOK * WIDTH * NTP * COLS, bytes_accessed=4 * 10**6, transcendentals=0
+            flops=2 * NX * TOK * WIDTH * wide, bytes_accessed=3 * 10**6, transcendentals=0
         ),
     )(everyone, weight)
 
 
 def shards(x_input, b_input, c_input, step, log_decay, skip, gain, out_weight):
     depth = out_weight.shape[0]
+    core = lax.axis_index("c").astype(jnp.int32)[None]
     swap = pl.pallas_call(
         pack_kernel,
         out_shape=shape(NX, depth, NTP * COLS),
-        in_specs=[pl.BlockSpec(memory_space=pl.ANY)],
+        in_specs=[pl.BlockSpec(memory_space=pltpu.SMEM), pl.BlockSpec(memory_space=pl.ANY)],
         scratch_shapes=[pltpu.VMEM(out_weight.shape, bf16), pltpu.SemaphoreType.DMA(())],
         name="pack",
         compiler_params=pltpu.CompilerParams(vmem_limit_bytes=LARGE),
         cost_estimate=pl.CostEstimate(flops=0, bytes_accessed=3 * 10**5, transcendentals=0),
-    )(out_weight)
+    )(core, out_weight)
     swap = lax.all_to_all(swap, "x", 0, 0, tiled=True)
 
     send = call(
@@ -221,10 +234,13 @@
         inner, scale, c_input, states, gain[None]
     )
     everyone = lax.all_to_all(hidden, "x", 0, 0, tiled=True)
-    parts = product(everyone, weight).reshape(NX * NTP, TOK, COLS)
-    parts = lax.all_to_all(parts, ("x", "y", "c"), 0, 0, tiled=True)
+    other = product(everyone, weight, 1)
+    other = lax.ppermute(other, "c", [(0, 1), (1, 0)])
+    mine = product(everyone, weight, 0)
+    parts = call(pair_kernel, shape(NX, NY, TOK, COLS), 10**6, 2 * 10**6, "pair")(mine, other)
+    parts = lax.all_to_all(parts.reshape(NX * NY, TOK, COLS), ("x", "y"), 0, 0, tiled=True)
     return call(sum_kernel, shape(TOK, NX * COLS), 10**6, 10**6, "sum")(
-        parts.reshape(NX, NTP, TOK, COLS)
+        parts.reshape(NX, NY, TOK, COLS)
     )
 
 

time: 144 us -> 141 us (0.979)
  blocking collectives: 84.1 us -> 70.3 us
  starting transfers between devices: 13.9 us -> 22.5 us
  Pallas kernels: 10.3 us -> 11.9 us
    all_to_all x1, blocking collectives: 28.7 us -> 14.9 us  [shards(): lax.all_to_all(parts.reshape(NX * NY, TOK, COLS), ('x', 'y'), 0, 0, tiled...]
    ppermute x0 -> x1, starting transfers between devices: none -> 8.57 us  [shards(): other = lax.ppermute(other, 'c', [(0, 1), (1, 0)])]
    pallas_call x1 -> x3, Pallas kernels: 2.65 us -> 4.28 us  [the longest x2 4.19 us: product(): pl.pallas_call(functools.partial(product_kernel, half), out_shape=shape(N...]
  transfers between devices with their start and end apart: 3 -> 4, of which waited for: 2 -> 2; matrix products, arithmetic and copies ran while one was open for 0% -> 0% of each run, Pallas kernels for 4% -> 5%
where the time goes in v7:
time: 141 us; the launch traced here: 140 us
  blocking collectives  70.3 us (50%)
  starting transfers between devices  22.5 us (16%)
  waiting for transfers between devices  21.4 us (15%)
  between operations  13.5 us (10%)
  Pallas kernels  11.9 us (8%)
    all_to_all x1, blocking collectives, shards(): got = lax.all_to_all(send, ('x', 'z'), 0, 0, tiled=True)  41.3 us
    all_to_all x1, waiting for transfers between devices, shards(): states = lax.all_to_all(entering, ('x', 'z'), 0, 0, tiled=True)  19.3 us
    all_to_all x1, blocking collectives, shards(): lax.all_to_all(parts.reshape(NX * NY, TOK, COLS), ('x', 'y'), 0, 0, tiled...  14.9 us
    all_to_all x1, blocking collectives, shards(): everyone = lax.all_to_all(hidden, 'x', 0, 0, tiled=True)  14.1 us
    all_to_all x1, starting transfers between devices, shards(): states = lax.all_to_all(entering, ('x', 'z'), 0, 0, tiled=True)  9.07 us
    ppermute x1, starting transfers between devices, shards(): other = lax.ppermute(other, 'c', [(0, 1), (1, 0)])  8.57 us
    all_to_all x1, starting transfers between devices, shards(): swap = lax.all_to_all(swap, 'x', 0, 0, tiled=True)  4.85 us
    pallas_call x2, Pallas kernels, product(): pl.pallas_call(functools.partial(product_kernel, half), out_shape=shape(N...  4.19 us
  transfers between devices with their start and end apart: 4, of which 2 were waited for; matrix products, arithmetic and copies ran while one was open for 0% of the time, Pallas kernels for 5%

profile of v7, /device:TPU:1, one launch (start us, length us, event | category | flops | bytes accessed | tf_op | source)
XLA Modules:
  0.0 140.4 jit_solution(13984189686799829688)
XLA Ops:
  6.6 1.7 %pack.1 = bf16[4,16,1024]{2,1,0:T(8,128)(2,1)} custom-call(s32[1]{0:T(128)} %bitcast.core_ref, bf16[16,4096]{1,0:T(8,128)(2,1)} %weight_ref.1), custom_call_target="tpu_custom_call" | custom-call | bytes 300000 | tf_op jit(solution)/shard_map/pack/pallas_call | solution.py:205
  8.2 4.9 %all-to-all-start = ((bf16[4,16,1024]{2,1,0:T(8,128)(2,1)}), bf16[4,16,1024]{2,1,0:T(8,128)(2,1)S(1)}, u32[]{:S(2)}, u32[]{:S(2)}) async-start(bf16[4,16,1024]{2,1,0:T(8,128)(2,1)} %pack.1), calls=%async_computation | async-start | bytes 262144 | tf_op jit(solution)/shard_map/all_to_all | solution.py:214
  13.1 0.0 all-gather.3.cloned.1.call-start
  13.1 2.8 %fresh.1 = bf16[64,24,128]{2,1,0:T(8,128)(2,1)} custom-call(bf16[128,1024]{1,0:T(8,128)(2,1)} %x_ref.3, bf16[128,128]{1,0:T(8,128)(2,1)} %b_ref.3, f32[16,128]{1,0:T(8,128)} %step_ref.3, f32[16,128]{1,0:T(8,128)} %logs_ref.3), custom_call_target="tpu_custom_call" | custom-call | flops 40000000 | bytes 1000000 | tf_op jit(solution)/shard_map/fresh/pallas_call | solution.py:216
  15.9 2.0 %all-to-all-done = bf16[4,16,1024]{2,1,0:T(8,128)(2,1)S(1)} async-done(((bf16[4,16,1024]{2,1,0:T(8,128)(2,1)}), bf16[4,16,1024]{2,1,0:T(8,128)(2,1)S(1)}, u32[]{:S(2)}, u32[]{:S(2)}) %all-to-all-start) | async-done | bytes 131104 | tf_op jit(solution)/shard_map/all_to_all | solution.py:214
  17.9 0.7 copy-done.7
  18.6 0.0 all-gather.3.cloned.1.call-update
  18.6 41.3 %all_to_all.25.got_ref = bf16[64,24,128]{2,1,0:T(8,128)(2,1)S(1)} all-to-all(bf16[64,24,128]{2,1,0:T(8,128)(2,1)} %fresh.1), channel_id=1, replica_groups=mesh['x'=4,'z'=16,'y'=4,'c'=2] {'x','z'}, dimensions={0} | all-to-all | bytes 786432 | tf_op jit(solution)/shard_map/all_to_all | solution.py:222
  59.9 0.9 scan.1
  60.8 9.1 %all-to-all-start.2 = ((bf16[64,16,128]{2,1,0:T(8,128)(2,1)}), bf16[64,16,128]{2,1,0:T(8,128)(2,1)S(1)}, u32[]{:S(2)}, u32[]{:S(2)}) async-start(bf16[64,16,128]{2,1,0:T(8,128)(2,1)} %scan.1), calls=%async_computation.2 | async-start | bytes 524288 | tf_op jit(solution)/shard_map/all_to_all | solution.py:231
  69.9 0.1 broadcast_in_dim.9
  69.9 0.1 broadcast_in_dim_reshape.3.skip_ref
  70.0 0.0 copy-done.5
  70.0 1.2 inner.1
  71.2 19.3 %all-to-all-done.2.state_ref = bf16[64,16,128]{2,1,0:T(8,128)(2,1)S(1)} async-done(((bf16[64,16,128]{2,1,0:T(8,128)(2,1)}), bf16[64,16,128]{2,1,0:T(8,128)(2,1)S(1)}, u32[]{:S(2)}, u32[]{:S(2)}) %all-to-all-start.2) | async-done | bytes 262176 | tf_op jit(solution)/shard_map/all_to_all | solution.py:231
  90.6 0.4 hidden.1
  90.9 14.1 %all_to_all.26.hidden_ref = bf16[4,128,1024]{2,1,0:T(8,128)(2,1)S(1)} all-to-all(bf16[4,128,1024]{2,1,0:T(8,128)(2,1)S(1)} %hidden.1), channel_id=1, replica_groups=mesh['x'=4,'z'=16,'y'=4,'c'=2] {'x'}, dimensions={0} | all-to-all | bytes 2097152 | tf_op jit(solution)/shard_map/all_to_all | solution.py:236
  105.0 2.2 %other.1 = bf16[4,4,128,128]{3,2,1,0:T(8,128)(2,1)S(1)} custom-call(bf16[4,128,1024]{2,1,0:T(8,128)(2,1)S(1)} %all_to_all.26.hidden_ref, bf16[16,4,16,1024]{3,2,1,0:T(8,128)(2,1)} %bitcast.8), custom_call_target="tpu_custom_call" | custom-call | flops 536870912 | bytes 3000000 | tf_op jit(solution)/shard_map/other/pallas_call | solution.py:184
  107.2 8.6 %collective-permute-start = (bf16[4,4,128,128]{3,2,1,0:T(8,128)(2,1)S(1)}, bf16[4,4,128,128]{3,2,1,0:T(8,128)(2,1)S(1)}, u32[]{:S(2)}, u32[]{:S(2)}) collective-permute-start(bf16[4,4,128,128]{3,2,1,0:T(8,128)(2,1)S(1)} %other.1), channel_id=1, source_target_pairs={{0,1},{1,0},{2,3},{3,2},{4,5},{5,4},{6,7},{7,6},{8,9},{9,8},{10,11... | collective-permute-start | bytes 1572872 | tf_op jit(solution)/shard_map/ppermute | solution.py:238
  115.8 2.0 %mine.1.mine_ref = f32[4,4,128,128]{3,2,1,0:T(8,128)S(1)} custom-call(bf16[4,128,1024]{2,1,0:T(8,128)(2,1)} %copy-done, bf16[16,4,16,1024]{3,2,1,0:T(8,128)(2,1)} %bitcast.9), custom_call_target="tpu_custom_call" | custom-call | flops 536870912 | bytes 3000000 | tf_op jit(solution)/shard_map/mine/pallas_call | solution.py:184
  117.8 0.0 collective-permute-done.other_ref
  117.8 0.1 pair.1
  117.9 14.9 %all_to_all.27 = bf16[16,128,128]{2,1,0:T(8,128)(2,1)S(1)} all-to-all(bf16[16,128,128]{2,1,0:T(8,128)(2,1)S(1)} %bitcast.6), channel_id=1, replica_groups=mesh['x'=4,'z'=16,'y'=4,'c'=2] {'x','y'}, dimensions={0} | all-to-all | bytes 1048576 | tf_op jit(solution)/shard_map/all_to_all | solution.py:241
  132.8 0.7 sum.1
  (17 shorter events, 0.0 us)
Async XLA Ops:
  6.5 63.5 %copy-start.5 = (f32[16,128]{1,0:T(8,128)S(1)}, f32[16,128]{1,0:T(8,128)}, u32[]{:S(2)}) copy-start(f32[16,128]{1,0:T(8,128)} %logs_ref.3) | copy-start | bytes 24580
  6.5 63.5 %copy-start.4 = (f32[16,128]{1,0:T(8,128)S(1)}, f32[16,128]{1,0:T(8,128)}, u32[]{:S(2)}) copy-start(f32[16,128]{1,0:T(8,128)} %step_ref.3) | copy-start | bytes 24580
  6.5 63.5 %copy-start.3 = (bf16[128,128]{1,0:T(8,128)(2,1)S(1)}, bf16[128,128]{1,0:T(8,128)(2,1)}, u32[]{:S(2)}) copy-start(bf16[128,128]{1,0:T(8,128)(2,1)} %b_ref.3) | copy-start | bytes 98308
  6.5 63.5 %copy-start.1 = (bf16[128,1024]{1,0:T(8,128)(2,1)S(1)}, bf16[128,1024]{1,0:T(8,128)(2,1)}, u32[]{:S(2)}) copy-start(bf16[128,1024]{1,0:T(8,128)(2,1)} %x_ref.3) | copy-start | bytes 786436
  6.5 63.3 %copy-start.8 = (f32[16]{0:T(128)S(1)}, f32[16]{0:T(128)}, u32[]{:S(2)}) copy-start(f32[16]{0:T(128)} %param.13) | copy-start | bytes 196
  6.5 63.5 %copy-start.2 = (bf16[128,128]{1,0:T(8,128)(2,1)S(1)}, bf16[128,128]{1,0:T(8,128)(2,1)}, u32[]{:S(2)}) copy-start(bf16[128,128]{1,0:T(8,128)(2,1)} %c_ref.3) | copy-start | bytes 98308
  6.6 84.0 %copy-start.6 = (f32[1024]{0:T(1024)S(1)}, f32[1024]{0:T(1024)}, u32[]{:S(2)}) copy-start(f32[1024]{0:T(1024)} %param.14) | copy-start | bytes 12292
  8.2 9.7 %all-to-all-start = ((bf16[4,16,1024]{2,1,0:T(8,128)(2,1)}), bf16[4,16,1024]{2,1,0:T(8,128)(2,1)S(1)}, u32[]{:S(2)}, u32[]{:S(2)}) async-start(bf16[4,16,1024]{2,1,0:T(8,128)(2,1)} %pack.1), calls=%async_computation | async-start | bytes 262144 | tf_op jit(solution)/shard_map/all_to_all | solution.py:214
  13.1 91.9 %all-gather.3.cloned.1.call-start = ((), (), s32[]{:S(2)}) async-start(), calls=%async_computation.5 | async-start | bytes 2228224 | tf_op jit(solution)/shard_map/all_gather | solution.py:220
  17.9 0.7 copy-start.7
  60.8 29.8 %all-to-all-start.2 = ((bf16[64,16,128]{2,1,0:T(8,128)(2,1)}), bf16[64,16,128]{2,1,0:T(8,128)(2,1)S(1)}, u32[]{:S(2)}, u32[]{:S(2)}) async-start(bf16[64,16,128]{2,1,0:T(8,128)(2,1)} %scan.1), calls=%async_computation.2 | async-start | bytes 524288 | tf_op jit(solution)/shard_map/all_to_all | solution.py:231
  105.0 10.8 %copy-start = (bf16[4,128,1024]{2,1,0:T(8,128)(2,1)}, bf16[4,128,1024]{2,1,0:T(8,128)(2,1)S(1)}, u32[]{:S(2)}) copy-start(bf16[4,128,1024]{2,1,0:T(8,128)(2,1)S(1)} %all_to_all.26.hidden_ref) | copy-start | bytes 3145732
  107.2 10.6 %collective-permute-start = (bf16[4,4,128,128]{3,2,1,0:T(8,128)(2,1)S(1)}, bf16[4,4,128,128]{3,2,1,0:T(8,128)(2,1)S(1)}, u32[]{:S(2)}, u32[]{:S(2)}) collective-permute-start(bf16[4,4,128,128]{3,2,1,0:T(8,128)(2,1)S(1)} %other.1), channel_id=1, source_target_pairs={{0,1},{1,0},{2,3},{3,2},{4,5},{5,4},{6,7},{7,6},{8,9},{9,8},{10,11... | collective-permute-start | bytes 1572872 | tf_op jit(solution)/shard_map/ppermute | solution.py:238
Sparse Core Ops, SparseCore 0:
  18.7 84.4 all-gather.2

commit v8 on v7

v8 whole, which is shorter than its diff:
```python
import functools

import jax
import jax.numpy as jnp
from jax import lax
from jax.experimental import pallas as pl
from jax.experimental.pallas import tpu as pltpu
from jax.sharding import Mesh, PartitionSpec as P

NX, NZ, NY, NC = 4, 16, 4, 2
NL = 2
NH = NZ // NL
GROUP = NX * NL
NTP = NY * NC
TOK = 128
HEADS = 16
P_SIZE = 64
N = 128
WIDTH = HEADS * P_SIZE
CTX = NX * NZ
CHUNK = WIDTH // CTX
EXTRA = 8
COLS = 128
QUAD = WIDTH // NX
PART = QUAD // NL
LARGE = 56 * 2**20
f32 = jnp.float32
bf16 = jnp.bfloat16
HIGH = lax.Precision.HIGHEST


def call(kernel, out_shape, flops, moved, name, vmem=32 * 2**20):
    return pl.pallas_call(
        kernel,
        out_shape=out_shape,
        name=name,
        compiler_params=pltpu.CompilerParams(vmem_limit_bytes=vmem),
        cost_estimate=pl.CostEstimate(flops=flops, bytes_accessed=moved, transcendentals=0),
    )


def iota(shape, axis):
    return lax.broadcasted_iota(jnp.int32, shape, axis)


def dot(a, b, ca, cb, precision=None):
    return lax.dot_general(
        a, b, (((ca,), (cb,)), ((), ())), precision=precision, preferred_element_type=f32
    )


def cumulative(logs):
    upto = (iota((TOK, TOK), 0) <= iota((TOK, TOK), 1)).astype(f32)
    return dot(logs, upto, 1, 0, HIGH)


def spread_heads(per_head, head):
    owner = (head == iota((HEADS, WIDTH), 0)).astype(f32)
    return dot(per_head, owner, 0, 0, HIGH)


def sorted_head():
    channel = iota((HEADS, WIDTH), 1)
    return channel // QUAD * (QUAD // P_SIZE) + channel % PART // (P_SIZE // NL)


def sorting():
    to = iota((QUAD, QUAD), 1)
    source = to % PART // 32 * P_SIZE + to % 32 // 16 * 32 + to // PART * 16 + to % 16
    return (iota((QUAD, QUAD), 0) == source).astype(bf16)


def pack_kernel(place_ref, weight_ref, *refs):
    *pieces, held_ref, sem = refs
    copy = pltpu.make_async_copy(weight_ref, held_ref, sem)
    copy.start()
    copy.wait()
    first = place_ref[0] == 0
    me = place_ref[1]
    for k, out_ref in enumerate(pieces):
        x = lax.rem(me + k, NX)
        for y in range(NY):
            even, odd = (
                held_ref[:, pl.ds(pl.multiple_of(((y * NC + c) * NX + x) * COLS, COLS), COLS)]
                for c in range(NC)
            )
            out_ref[:, y * COLS : (y + 1) * COLS] = jnp.where(first, even, odd)
            out_ref[:, (NY + y) * COLS : (NY + y + 1) * COLS] = jnp.where(first, odd, even)


def fresh_kernel(x_ref, b_ref, step_ref, logs_ref, out_ref):
    logs = logs_ref[...]
    cumul = cumulative(logs)
    total = dot(logs, jnp.ones((TOK, TOK), f32), 1, 0, HIGH)
    tail = jnp.exp(total - cumul) * step_ref[...]
    weighted = (x_ref[...].astype(f32) * spread_heads(tail, iota((HEADS, WIDTH), 1) // P_SIZE)).astype(bf16)
    fresh = dot(weighted, b_ref[...], 0, 0).astype(bf16)
    high = total.astype(bf16)
    rest = total - high.astype(f32)
    middle = rest.astype(bf16)
    low = (rest - middle.astype(f32)).astype(bf16)
    row = iota((EXTRA, N), 0)
    for h in range(HEADS):
        first, second, third = (
            jnp.broadcast_to(part[h : h + 1].astype(f32), (EXTRA, N)) for part in (high, middle, low)
        )
        pieces = jnp.where(row == 0, first, jnp.where(row == 1, second, third))
        pieces = jnp.where(row < 3, pieces, 0.0).astype(bf16)
        for k in range(h * P_SIZE // CHUNK, (h + 1) * P_SIZE // CHUNK):
            out_ref[k, :CHUNK, :] = fresh[k * CHUNK : (k + 1) * CHUNK]
            out_ref[k, CHUNK:, :] = pieces


def scan_kernel(got_ref, out_ref):
    state = jnp.zeros((CHUNK, N), f32)
    for k in range(CTX):
        out_ref[k, :, :] = state.astype(bf16)
        pieces = got_ref[k, CHUNK:, :].astype(f32)
        decay = jnp.exp(pieces[0:1] + pieces[1:2] + pieces[2:3])
        state = decay * state + got_ref[k, :CHUNK, :].astype(f32)


def inner_kernel(x_ref, b_ref, c_ref, step_ref, logs_ref, skip_ref, out_ref, scale_ref):
    logs = logs_ref[...]
    cumul = cumulative(logs)
    upto = (iota((TOK, TOK), 1) <= iota((TOK, TOK), 0)).astype(f32)
    cumul_t = dot(upto, logs, 1, 1, HIGH)
    scale_ref[...] = spread_heads(jnp.exp(cumul), sorted_head())
    scores = dot(c_ref[...], b_ref[...], 1, 1)
    within = iota((TOK, TOK), 1) <= iota((TOK, TOK), 0)
    lane_head = iota((TOK, QUAD), 1) % PART // (P_SIZE // NL)
    order = sorting()
    for quad in range(NX):
        columns = slice(quad * QUAD, (quad + 1) * QUAD)
        values = dot(x_ref[:, columns], order, 1, 0).astype(bf16)
        own = skip_ref[:, columns] * values.astype(f32)
        for i in range(QUAD // P_SIZE):
            h = quad * (QUAD // P_SIZE) + i
            spread = cumul_t[:, h : h + 1] - cumul[h : h + 1, :]
            decay = jnp.exp(jnp.where(within, spread, -1e30))
            mixing = (scores * decay * step_ref[h : h + 1, :]).astype(bf16)
            own = own + jnp.where(lane_head == i, dot(mixing, values, 1, 0), 0.0)
        out_ref[:, columns] = own


def hidden_kernel(inner_ref, scale_ref, c_ref, state_ref, gain_ref, out_ref):
    slots = [
        (quad * 4 + i) * 4 + j * NL + parity
        for quad in range(NX)
        for parity in range(NL)
        for i in range(4)
        for j in range(2)
    ]
    states = jnp.concatenate([state_ref[slot] for slot in slots], axis=0)
    ssm = inner_ref[...] + scale_ref[...] * dot(c_ref[...], states, 1, 1)
    meansq = jnp.mean(ssm * ssm, axis=1, keepdims=True)
    hidden = (ssm * lax.rsqrt(meansq + 1e-05) * gain_ref[...]).astype(bf16)
    for quad in range(NX):
        for parity in range(NL):
            begin = quad * QUAD + parity * PART
            part = hidden[:, begin : begin + PART]
            for x in range(NX):
                out_ref[x * NL + parity, :, quad * PART : (quad + 1) * PART] = part


def product_kernel(half, me_ref, hidden_ref, weight_ref, out_ref, tokens_ref, held_ref, sems):
    wide = NY * COLS
    me = me_ref[0]
    copies = []
    for k in range(NX):
        part = hidden_ref.at[:, :, pl.ds(k * PART, PART)]
        rows = weight_ref.at[:, k, :, pl.ds(half * wide, wide)]
        copies.append(pltpu.make_async_copy(part, tokens_ref.at[k], sems.at[0, k]))
        copies.append(pltpu.make_async_copy(rows, held_ref.at[k], sems.at[1, k]))
    for copy in copies:
        copy.start()
    for copy in copies:
        copy.wait()
    low, high = (held_ref[k : k + 2].reshape(2 * PART, wide) for k in (0, 2))
    x = [lax.rem(me + (NX - k), NX) for k in range(NX)]
    for i in range(GROUP):
        left = jnp.concatenate([tokens_ref[x[0], i], tokens_ref[x[1], i]], axis=1)
        right = jnp.concatenate([tokens_ref[x[2], i], tokens_ref[x[3], i]], axis=1)
        term = (dot(left, low, 1, 0) + dot(right, high, 1, 0)).astype(out_ref.dtype)
        for j in range(NY):
            out_ref[i, j, :, :] = term[:, j * COLS : (j + 1) * COLS]


def pair_kernel(mine_ref, other_ref, out_ref):
    out_ref[...] = (mine_ref[...] + other_ref[...].astype(f32)).astype(bf16)


def sum_kernel(parts_ref, out_ref):
    for k in range(NX):
        total = parts_ref[k, 0, :, :].astype(f32)
        for j in range(1, NL * NY):
            total = total + parts_ref[k, j, :, :].astype(f32)
        out_ref[:, k * COLS : (k + 1) * COLS] = total.astype(bf16)


def shape(*dims, dtype=bf16):
    return jax.ShapeDtypeStruct(dims, dtype)


def product(me, everyone, weight, half):
    depth, wide = weight.shape[2], NY * COLS
    return pl.pallas_call(
        functools.partial(product_kernel, half),
        out_shape=shape(GROUP, NY, TOK, COLS, dtype=bf16 if half else f32),
        in_specs=[pl.BlockSpec(memory_space=pltpu.SMEM)] + [pl.BlockSpec(memory_space=pl.ANY)] * 2,
        scratch_shapes=[
            pltpu.VMEM((NX, GROUP, TOK, PART), bf16),
            pltpu.VMEM((NX, NH, depth, wide), bf16),
            pltpu.SemaphoreType.DMA((2, NX)),
        ],
        name="other" if half else "mine",
        compiler_params=pltpu.CompilerParams(vmem_limit_bytes=52 * 2**20),
        cost_estimate=pl.CostEstimate(
            flops=GROUP * TOK * WIDTH * wide, bytes_accessed=3 * 10**6, transcendentals=0
        ),
    )(me, everyone, weight)


def sort_channels(per_channel):
    return per_channel.reshape(NX, 4, 2, NL, 16).transpose(0, 3, 1, 2, 4).reshape(1, WIDTH)


def shards(x_input, b_input, c_input, step, log_decay, skip, gain, out_weight):
    ctx = ("x", "zh", "zl")
    depth = out_weight.shape[0]
    me = lax.axis_index("x").astype(jnp.int32)
    core = lax.axis_index("c").astype(jnp.int32)
    send = call(
        fresh_kernel, shape(CTX, CHUNK + EXTRA, N), 4 * 10**7, 10**6, "fresh", LARGE
    )(x_input, b_input, step, log_decay)
    got = lax.all_to_all(send, ctx, 0, 0, tiled=True)

    out_weight, _ = lax.optimization_barrier((out_weight, send))
    pieces = pl.pallas_call(
        pack_kernel,
        out_shape=(shape(depth, NTP * COLS),) * NX,
        in_specs=[pl.BlockSpec(memory_space=pltpu.SMEM), pl.BlockSpec(memory_space=pl.ANY)],
        scratch_shapes=[pltpu.VMEM(out_weight.shape, bf16), pltpu.SemaphoreType.DMA(())],
        name="pack",
        compiler_params=pltpu.CompilerParams(vmem_limit_bytes=LARGE),
        cost_estimate=pl.CostEstimate(flops=0, bytes_accessed=3 * 10**5, transcendentals=0),
    )(jnp.stack([core, me]), out_weight)
    pieces = [
        lax.ppermute(piece, "x", [(i, (i + k) % NX) for i in range(NX)]) if k else piece
        for k, piece in enumerate(pieces)
    ]
    swap = jnp.stack(pieces)
    weight = lax.all_gather(swap, "zh", axis=0)

    inner, scale = call(
        inner_kernel,
        (shape(TOK, WIDTH, dtype=f32), shape(TOK, WIDTH, dtype=f32)),
        10**8,
        2 * 10**6,
        "inner",
    )(x_input, b_input, c_input, step, log_decay, sort_channels(jnp.repeat(skip, P_SIZE)))
    entering = call(scan_kernel, shape(CTX, CHUNK, N), 10**6, 7 * 10**5, "scan")(got)
    states = lax.all_to_all(entering, ctx, 0, 0, tiled=True)
    states, weight = lax.optimization_barrier((states, weight))

    hidden = call(hidden_kernel, shape(GROUP, TOK, WIDTH // NL), 3 * 10**7, 2 * 10**6, "hidden")(
        inner, scale, c_input, states, sort_channels(gain)
    )
    everyone = lax.all_to_all(hidden, ("x", "zl"), 0, 0, tiled=True)
    other = product(me[None], everyone, weight, 1)
    other = lax.ppermute(other, "c", [(0, 1), (1, 0)])
    mine = product(me[None], everyone, weight, 0)
    parts = call(pair_kernel, shape(GROUP, NY, TOK, COLS), 10**6, 2 * 10**6, "pair")(mine, other)
    parts = parts.reshape(GROUP * NY, TOK, COLS)
    parts = lax.all_to_all(parts, ("x", "zl", "y"), 0, 0, tiled=True)
    return call(sum_kernel, shape(TOK, NX * COLS), 10**6, 10**6, "sum")(
        parts.reshape(NX, NL * NY, TOK, COLS)
    )


def solution(mesh):
    fine = Mesh(mesh.devices.reshape(NX, NH, NL, NY, NC), ("x", "zh", "zl", "y", "c"))
    ctx, tp = ("x", "zh", "zl"), ("y", "c")
    in_specs = (
        P(ctx, tp),
        P(ctx, tp),
        P(ctx, tp),
        P(tp, ctx),
        P(tp, ctx),
        P(tp),
        P(tp),
        P(tp + ctx, None),
    )
    return jax.shard_map(
        shards, mesh=fine, in_specs=in_specs, out_specs=P(ctx, tp), check_vma=False
    )
```

time: 141 us -> 166 us (1.18)
  blocking collectives: 70.3 us -> 40.1 us
  waiting for transfers between devices: 21.4 us -> 49.9 us
  starting transfers between devices: 22.5 us -> 42.9 us
  Pallas kernels: 11.9 us -> 14.8 us
  other arithmetic: 0 us -> 2.04 us
    all_gather x1, waiting for transfers between devices: 0.01 us -> 39.9 us  [shards(): weight = lax.all_gather(swap, 'zh', axis=0)]
    all_to_all x3 -> x2, blocking collectives: 70.3 us -> 40.1 us  [the longest x1 21.5 us: shards(): parts = lax.all_to_all(parts, ('x', 'zl', 'y'), 0, 0, tiled=True)]
    all_to_all x2, waiting for transfers between devices: 21.4 us -> 7.76 us  [the longest x1 7.76 us: shards(): got = lax.all_to_all(send, ctx, 0, 0, tiled=True)]
    all_to_all x2, starting transfers between devices: 13.9 us -> 26.7 us  [the longest x1 19.1 us: shards(): got = lax.all_to_all(send, ctx, 0, 0, tiled=True)]
    ppermute x0 -> x3, starting transfers between devices: none -> 10.4 us  [shards(): lax.ppermute(piece, 'x', [(i, (i + k) % NX) for i in range(NX)])]
    ppermute x1, starting transfers between devices: 8.57 us -> 5.76 us  [shards(): other = lax.ppermute(other, 'c', [(0, 1), (1, 0)])]
    ppermute x0 -> x3, waiting for transfers between devices: none -> 2.16 us  [shards(): lax.ppermute(piece, 'x', [(i, (i + k) % NX) for i in range(NX)])]
    pallas_call x5, Pallas kernels: 6.3 us -> 8.42 us  [the longest x2 5.58 us: product(): pl.pallas_call(functools.partial(product_kernel, half), out_shape=shape(G...]
  transfers between devices with their start and end apart: 4 -> 7, of which waited for: 2 -> 3; matrix products, arithmetic and copies ran while one was open for 0% -> 2% of each run, Pallas kernels for 5% -> 5%
where the time goes in v8:
time: 166 us; the launch traced here: 165 us
  waiting for transfers between devices  49.9 us (30%)
  starting transfers between devices  42.9 us (26%)
  blocking collectives  40.1 us (24%)
  Pallas kernels  14.8 us (9%)
  between operations  13.6 us (8%)
  local copies, waits for them, and re-layouts  2.11 us (1%)
  other arithmetic  2.04 us (1%)
    all_gather x1, waiting for transfers between devices, shards(): weight = lax.all_gather(swap, 'zh', axis=0)  39.9 us
    all_to_all x1, blocking collectives, shards(): parts = lax.all_to_all(parts, ('x', 'zl', 'y'), 0, 0, tiled=True)  21.5 us
    all_to_all x1, starting transfers between devices, shards(): got = lax.all_to_all(send, ctx, 0, 0, tiled=True)  19.1 us
    all_to_all x1, blocking collectives, shards(): everyone = lax.all_to_all(hidden, ('x', 'zl'), 0, 0, tiled=True)  18.6 us
    ppermute x3, starting transfers between devices, shards(): lax.ppermute(piece, 'x', [(i, (i + k) % NX) for i in range(NX)])  10.4 us
    all_to_all x1, waiting for transfers between devices, shards(): got = lax.all_to_all(send, ctx, 0, 0, tiled=True)  7.76 us
    all_to_all x1, starting transfers between devices, shards(): states = lax.all_to_all(entering, ctx, 0, 0, tiled=True)  7.58 us
    ppermute x1, starting transfers between devices, shards(): other = lax.ppermute(other, 'c', [(0, 1), (1, 0)])  5.76 us
  transfers between devices with their start and end apart: 7, of which 3 were waited for; matrix products, arithmetic and copies ran while one was open for 2% of the time, Pallas kernels for 5%

profile of v8, /device:TPU:1, one launch (start us, length us, event | category | flops | bytes accessed | tf_op | source)
XLA Modules:
  0.0 165.4 jit_solution(7938368889528879951)
XLA Ops:
  6.6 2.9 %fresh.1 = bf16[64,24,128]{2,1,0:T(8,128)(2,1)} custom-call(bf16[128,1024]{1,0:T(8,128)(2,1)} %x_ref.3, bf16[128,128]{1,0:T(8,128)(2,1)} %b_ref.3, f32[16,128]{1,0:T(8,128)} %step_ref.3, f32[16,128]{1,0:T(8,128)} %logs_ref.3), custom_call_target="tpu_custom_call" | custom-call | flops 40000000 | bytes 1000000 | tf_op jit(solution)/shard_map/fresh/pallas_call | solution.py:233
  9.5 19.1 %all-to-all-start = ((bf16[64,24,128]{2,1,0:T(8,128)(2,1)}), bf16[64,24,128]{2,1,0:T(8,128)(2,1)S(1)}, u32[]{:S(2)}, u32[]{:S(2)}) async-start(bf16[64,24,128]{2,1,0:T(8,128)(2,1)} %fresh.1), calls=%async_computation | async-start | bytes 786432 | tf_op jit(solution)/shard_map/all_to_all | solution.py:236
  28.6 0.6 pad_add_fusion.place_ref
  29.2 2.2 %pack.1 = (bf16[16,1024]{1,0:T(8,128)(2,1)}, bf16[16,1024]{1,0:T(8,128)(2,1)}, bf16[16,1024]{1,0:T(8,128)(2,1)}, bf16[16,1024]{1,0:T(8,128)(2,1)}) custom-call(s32[2]{0:T(128)} %pad_add_fusion.place_ref, bf16[16,4096]{1,0:T(8,128)(2,1)} %weight_ref), custom_call_target="tpu_custom_call" | custom-call | bytes 300000 | tf_op jit(solution)/shard_map/pack/pallas_call | solution.py:239
  31.5 2.9 %collective-permute-start = (bf16[16,1024]{1,0:T(8,128)(2,1)}, bf16[16,1024]{1,0:T(8,128)(2,1)S(1)}, u32[]{:S(2)}, u32[]{:S(2)}) collective-permute-start(bf16[16,1024]{1,0:T(8,128)(2,1)} %get-tuple-element.18), channel_id=1, source_target_pairs={{0,128},{128,256},{256,384},{384,0},{1,129},{129,257},{257,385},{3... | collective-permute-start | bytes 98312 | tf_op jit(solution)/shard_map/ppermute | solution.py:249
  34.4 4.5 %collective-permute-start.1 = (bf16[16,1024]{1,0:T(8,128)(2,1)}, bf16[16,1024]{1,0:T(8,128)(2,1)S(1)}, u32[]{:S(2)}, u32[]{:S(2)}) collective-permute-start(bf16[16,1024]{1,0:T(8,128)(2,1)} %get-tuple-element.19), channel_id=1, source_target_pairs={{0,256},{128,384},{256,0},{384,128},{1,257},{129,385},{257,1},{385... | collective-permute-start | bytes 98312 | tf_op jit(solution)/shard_map/ppermute | solution.py:249
  38.9 3.0 %collective-permute-start.2 = (bf16[16,1024]{1,0:T(8,128)(2,1)}, bf16[16,1024]{1,0:T(8,128)(2,1)S(1)}, u32[]{:S(2)}, u32[]{:S(2)}) collective-permute-start(bf16[16,1024]{1,0:T(8,128)(2,1)} %get-tuple-element.20), channel_id=1, source_target_pairs={{0,384},{128,0},{256,128},{384,256},{1,385},{129,1},{257,129},{385... | collective-permute-start | bytes 98312 | tf_op jit(solution)/shard_map/ppermute | solution.py:249
  41.9 2.2 %collective-permute-done.2 = bf16[16,1024]{1,0:T(8,128)(2,1)S(1)} collective-permute-done((bf16[16,1024]{1,0:T(8,128)(2,1)}, bf16[16,1024]{1,0:T(8,128)(2,1)S(1)}, u32[]{:S(2)}, u32[]{:S(2)}) %collective-permute-start.2) | collective-permute-done | bytes 32800 | tf_op jit(solution)/shard_map/ppermute | solution.py:249
  44.1 1.4 pad_maximum_fusion
  45.6 7.8 %all-to-all-done.got_ref = bf16[64,24,128]{2,1,0:T(8,128)(2,1)S(1)} async-done(((bf16[64,24,128]{2,1,0:T(8,128)(2,1)}), bf16[64,24,128]{2,1,0:T(8,128)(2,1)S(1)}, u32[]{:S(2)}, u32[]{:S(2)}) %all-to-all-start) | async-done | bytes 393248 | tf_op jit(solution)/shard_map/all_to_all | solution.py:236
  53.3 0.8 scan.1
  54.2 7.6 %all-to-all-start.1 = ((bf16[64,16,128]{2,1,0:T(8,128)(2,1)}), bf16[64,16,128]{2,1,0:T(8,128)(2,1)S(1)}, u32[]{:S(2)}, u32[]{:S(2)}) async-start(bf16[64,16,128]{2,1,0:T(8,128)(2,1)} %scan.1), calls=%async_computation.1 | async-start | bytes 524288 | tf_op jit(solution)/shard_map/all_to_all | solution.py:263
  61.9 0.1 reshape.19.skip_ref
  62.3 1.8 %inner.1 = (f32[128,1024]{1,0:T(8,128)S(1)}, f32[128,1024]{1,0:T(8,128)S(1)}) custom-call(bf16[128,1024]{1,0:T(8,128)(2,1)S(1)} %copy-done.2, bf16[128,128]{1,0:T(8,128)(2,1)S(1)} %copy-done.4, bf16[128,128]{1,0:T(8,128)(2,1)S(1)} %copy-done.3, f32[16,128]{1,0:T(8,128)S(1)} %copy-done.5, f32[16,128]{1,0:T(8,128)S(1)} %copy-done.6, ...), custom_call_target="tpu_custom_call" | custom-call | flops 100000000 | bytes 2000000 | tf_op jit(solution)/shard_map/inner/pallas_call | solution.py:255
  64.2 39.9 %all-gather.3.cloned.1.call-done = bf16[32,16,1024]{2,1,0:T(8,128)(2,1)} async-done(((bf16[4,16,1024]{2,1,0:T(8,128)(2,1)}), bf16[32,16,1024]{2,1,0:T(8,128)(2,1)}) %all-gather.3.cloned.1.call-update) | async-done | bytes 1048592 | tf_op jit(solution)/shard_map/all_gather | solution.py:253
  104.1 0.4 hidden.1
  104.5 18.6 %all_to_all.20.hidden_ref = bf16[8,128,512]{2,1,0:T(8,128)(2,1)} all-to-all(bf16[8,128,512]{2,1,0:T(8,128)(2,1)S(1)} %hidden.1), channel_id=1, replica_groups=mesh['x'=4,'zh'=8,'zl'=2,'y'=4,'c'=2] {'x','zl'}, dimensions={0} | all-to-all | bytes 2097152 | tf_op jit(solution)/shard_map/all_to_all | solution.py:269
  123.2 2.3 %other.1 = bf16[8,4,128,128]{3,2,1,0:T(8,128)(2,1)S(1)} custom-call(s32[1]{0:T(128)} %bitcast.me_ref, bf16[8,128,512]{2,1,0:T(8,128)(2,1)} %all_to_all.20.hidden_ref, bf16[8,4,16,1024]{3,2,1,0:T(8,128)(2,1)} %bitcast.12), custom_call_target="tpu_custom_call" | custom-call | flops 536870912 | bytes 3000000 | tf_op jit(solution)/shard_map/other/pallas_call | solution.py:207
  125.4 5.8 %collective-permute-start.3 = (bf16[8,4,128,128]{3,2,1,0:T(8,128)(2,1)S(1)}, bf16[8,4,128,128]{3,2,1,0:T(8,128)(2,1)S(1)}, u32[]{:S(2)}, u32[]{:S(2)}) collective-permute-start(bf16[8,4,128,128]{3,2,1,0:T(8,128)(2,1)S(1)} %other.1), channel_id=1, source_target_pairs={{0,1},{1,0},{2,3},{3,2},{4,5},{5,4},{6,7},{7,6},{8,9},{9,8},{10,11... | collective-permute-start | bytes 3145736 | tf_op jit(solution)/shard_map/ppermute | solution.py:271
  131.2 3.3 %mine.1.mine_ref = f32[8,4,128,128]{3,2,1,0:T(8,128)} custom-call(s32[1]{0:T(128)} %bitcast.me_ref, bf16[8,128,512]{2,1,0:T(8,128)(2,1)S(1)} %copy-done, bf16[8,4,16,1024]{3,2,1,0:T(8,128)(2,1)} %bitcast.13), custom_call_target="tpu_custom_call" | custom-call | flops 536870912 | bytes 3000000 | tf_op jit(solution)/shard_map/mine/pallas_call | solution.py:207
  134.6 1.6 copy-done.1
  136.1 0.2 pair.1
  136.3 21.5 %all_to_all.21 = bf16[32,128,128]{2,1,0:T(8,128)(2,1)S(1)} all-to-all(bf16[32,128,128]{2,1,0:T(8,128)(2,1)S(1)} %bitcast.11), channel_id=1, replica_groups=mesh['x'=4,'zh'=8,'zl'=2,'y'=4,'c'=2] {'x','zl','y'}, dimensions={0} | all-to-all | bytes 2097152 | tf_op jit(solution)/shard_map/all_to_all | solution.py:275
  157.8 0.8 sum.1
  (28 shorter events, 0.5 us)
Async XLA Ops:
  6.5 55.7 %copy-start.6 = (f32[16,128]{1,0:T(8,128)S(1)}, f32[16,128]{1,0:T(8,128)}, u32[]{:S(2)}) copy-start(f32[16,128]{1,0:T(8,128)} %logs_ref.3) | copy-start | bytes 24580
  6.5 55.7 %copy-start.5 = (f32[16,128]{1,0:T(8,128)S(1)}, f32[16,128]{1,0:T(8,128)}, u32[]{:S(2)}) copy-start(f32[16,128]{1,0:T(8,128)} %step_ref.3) | copy-start | bytes 24580
  6.5 55.8 %copy-start.4 = (bf16[128,128]{1,0:T(8,128)(2,1)S(1)}, bf16[128,128]{1,0:T(8,128)(2,1)}, u32[]{:S(2)}) copy-start(bf16[128,128]{1,0:T(8,128)(2,1)} %b_ref.3) | copy-start | bytes 98308
  6.5 55.8 %copy-start.2 = (bf16[128,1024]{1,0:T(8,128)(2,1)S(1)}, bf16[128,1024]{1,0:T(8,128)(2,1)}, u32[]{:S(2)}) copy-start(bf16[128,1024]{1,0:T(8,128)(2,1)} %x_ref.3) | copy-start | bytes 786436
  6.5 55.2 %copy-start.8 = (f32[16]{0:T(128)S(1)}, f32[16]{0:T(128)}, u32[]{:S(2)}) copy-start(f32[16]{0:T(128)} %param.13) | copy-start | bytes 196
  6.5 55.5 %copy-start.7 = (f32[1024]{0:T(1024)S(1)}, f32[1024]{0:T(1024)}, u32[]{:S(2)}) copy-start(f32[1024]{0:T(1024)} %param.14) | copy-start | bytes 12292
  6.6 55.8 %copy-start.3 = (bf16[128,128]{1,0:T(8,128)(2,1)S(1)}, bf16[128,128]{1,0:T(8,128)(2,1)}, u32[]{:S(2)}) copy-start(bf16[128,128]{1,0:T(8,128)(2,1)} %c_ref.3) | copy-start | bytes 98308
  9.5 43.9 %all-to-all-start = ((bf16[64,24,128]{2,1,0:T(8,128)(2,1)}), bf16[64,24,128]{2,1,0:T(8,128)(2,1)S(1)}, u32[]{:S(2)}, u32[]{:S(2)}) async-start(bf16[64,24,128]{2,1,0:T(8,128)(2,1)} %fresh.1), calls=%async_computation | async-start | bytes 786432 | tf_op jit(solution)/shard_map/all_to_all | solution.py:236
  28.6 75.5 %all-gather.3.cloned.1.call-start = ((), (), s32[]{:S(2)}) async-start(), calls=%async_computation.4 | async-start | bytes 1179648 | tf_op jit(solution)/shard_map/all_gather | solution.py:253
  31.5 10.4 %collective-permute-start = (bf16[16,1024]{1,0:T(8,128)(2,1)}, bf16[16,1024]{1,0:T(8,128)(2,1)S(1)}, u32[]{:S(2)}, u32[]{:S(2)}) collective-permute-start(bf16[16,1024]{1,0:T(8,128)(2,1)} %get-tuple-element.18), channel_id=1, source_target_pairs={{0,128},{128,256},{256,384},{384,0},{1,129},{129,257},{257,385},{3... | collective-permute-start | bytes 98312 | tf_op jit(solution)/shard_map/ppermute | solution.py:249
  34.4 7.5 %collective-permute-start.1 = (bf16[16,1024]{1,0:T(8,128)(2,1)}, bf16[16,1024]{1,0:T(8,128)(2,1)S(1)}, u32[]{:S(2)}, u32[]{:S(2)}) collective-permute-start(bf16[16,1024]{1,0:T(8,128)(2,1)} %get-tuple-element.19), channel_id=1, source_target_pairs={{0,256},{128,384},{256,0},{384,128},{1,257},{129,385},{257,1},{385... | collective-permute-start | bytes 98312 | tf_op jit(solution)/shard_map/ppermute | solution.py:249
  38.9 5.2 %collective-permute-start.2 = (bf16[16,1024]{1,0:T(8,128)(2,1)}, bf16[16,1024]{1,0:T(8,128)(2,1)S(1)}, u32[]{:S(2)}, u32[]{:S(2)}) collective-permute-start(bf16[16,1024]{1,0:T(8,128)(2,1)} %get-tuple-element.20), channel_id=1, source_target_pairs={{0,384},{128,0},{256,128},{384,256},{1,385},{129,1},{257,129},{385... | collective-permute-start | bytes 98312 | tf_op jit(solution)/shard_map/ppermute | solution.py:249
  54.2 49.9 %all-to-all-start.1 = ((bf16[64,16,128]{2,1,0:T(8,128)(2,1)}), bf16[64,16,128]{2,1,0:T(8,128)(2,1)S(1)}, u32[]{:S(2)}, u32[]{:S(2)}) async-start(bf16[64,16,128]{2,1,0:T(8,128)(2,1)} %scan.1), calls=%async_computation.1 | async-start | bytes 524288 | tf_op jit(solution)/shard_map/all_to_all | solution.py:263
  123.2 8.1 %copy-start = (bf16[8,128,512]{2,1,0:T(8,128)(2,1)S(1)}, bf16[8,128,512]{2,1,0:T(8,128)(2,1)}, u32[]{:S(2)}) copy-start(bf16[8,128,512]{2,1,0:T(8,128)(2,1)} %all_to_all.20.hidden_ref) | copy-start | bytes 3145732
  125.4 9.1 %collective-permute-start.3 = (bf16[8,4,128,128]{3,2,1,0:T(8,128)(2,1)S(1)}, bf16[8,4,128,128]{3,2,1,0:T(8,128)(2,1)S(1)}, u32[]{:S(2)}, u32[]{:S(2)}) collective-permute-start(bf16[8,4,128,128]{3,2,1,0:T(8,128)(2,1)S(1)} %other.1), channel_id=1, source_target_pairs={{0,1},{1,0},{2,3},{3,2},{4,5},{5,4},{6,7},{7,6},{8,9},{9,8},{10,11... | collective-permute-start | bytes 3145736 | tf_op jit(solution)/shard_map/ppermute | solution.py:271
  134.5 1.6 copy-start.1
Sparse Core Ops, SparseCore 0:
  45.7 58.3 all-gather.2

commit v9 on v7

--- a/solution.py
+++ b/solution.py
@@ -16,7 +16,7 @@
 WIDTH = HEADS * P_SIZE
 CTX = NX * NZ
 CHUNK = WIDTH // CTX
-EXTRA = 8
+PAIRS = CHUNK // 2
 COLS = 128
 LARGE = 56 * 2**20
 f32 = jnp.float32
@@ -76,28 +76,23 @@
     weighted = (x_ref[...].astype(f32) * spread_heads(tail)).astype(bf16)
     fresh = dot(weighted, b_ref[...], 0, 0).astype(bf16)
     high = total.astype(bf16)
-    rest = total - high.astype(f32)
-    middle = rest.astype(bf16)
-    low = (rest - middle.astype(f32)).astype(bf16)
-    row = iota((EXTRA, N), 0)
+    low = (total - high.astype(f32)).astype(bf16)
+    row = iota((2, N), 0)
     for h in range(HEADS):
-        first, second, third = (
-            jnp.broadcast_to(part[h : h + 1].astype(f32), (EXTRA, N)) for part in (high, middle, low)
-        )
-        pieces = jnp.where(row == 0, first, jnp.where(row == 1, second, third))
-        pieces = jnp.where(row < 3, pieces, 0.0).astype(bf16)
+        first, second = (jnp.broadcast_to(part[h : h + 1].astype(f32), (2, N)) for part in (high, low))
+        pieces = jnp.where(row == 0, first, second).astype(bf16)
         for k in range(h * P_SIZE // CHUNK, (h + 1) * P_SIZE // CHUNK):
-            out_ref[k, :CHUNK, :] = fresh[k * CHUNK : (k + 1) * CHUNK]
-            out_ref[k, CHUNK:, :] = pieces
+            out_ref[k, :PAIRS, :, :] = fresh[k * CHUNK : (k + 1) * CHUNK].reshape(PAIRS, 2, N)
+            out_ref[k, PAIRS, :, :] = pieces
 
 
 def scan_kernel(got_ref, out_ref):
     state = jnp.zeros((CHUNK, N), f32)
     for k in range(CTX):
         out_ref[k, :, :] = state.astype(bf16)
-        pieces = got_ref[k, CHUNK:, :].astype(f32)
-        decay = jnp.exp(pieces[0:1] + pieces[1:2] + pieces[2:3])
-        state = decay * state + got_ref[k, :CHUNK, :].astype(f32)
+        pieces = got_ref[k, PAIRS, :, :].astype(f32)
+        decay = jnp.exp(pieces[0:1] + pieces[1:2])
+        state = decay * state + got_ref[k, :PAIRS, :, :].reshape(CHUNK, N).astype(f32)
 
 
 def inner_kernel(x_ref, b_ref, c_ref, step_ref, logs_ref, skip_ref, out_ref, scale_ref):
@@ -214,7 +209,7 @@
     swap = lax.all_to_all(swap, "x", 0, 0, tiled=True)
 
     send = call(
-        fresh_kernel, shape(CTX, CHUNK + EXTRA, N), 4 * 10**7, 10**6, "fresh", LARGE
+        fresh_kernel, shape(CTX, PAIRS + 1, 2, N), 4 * 10**7, 10**6, "fresh", LARGE
     )(x_input, b_input, step, log_decay)
     send, swap = lax.optimization_barrier((send, swap))
     weight = lax.all_gather(swap, "z", axis=0)

time: 141 us -> 138 us (0.979)
  blocking collectives: 70.3 us -> 66.5 us
    all_to_all x1, blocking collectives: 41.3 us -> 36.5 us  [shards(): got = lax.all_to_all(send, ('x', 'z'), 0, 0, tiled=True)]
    all_to_all x1, blocking collectives: 14.9 us -> 16.3 us  [shards(): lax.all_to_all(parts.reshape(NX * NY, TOK, COLS), ('x', 'y'), 0, 0, tiled...]
  transfers between devices with their start and end apart: 4 -> 4, of which waited for: 2 -> 3; matrix products, arithmetic and copies ran while one was open for 0% -> 0% of each run, Pallas kernels for 5% -> 5%
where the time goes in v9:
time: 138 us; the launch traced here: 137 us
  blocking collectives  66.5 us (48%)
  starting transfers between devices  22.3 us (16%)
  waiting for transfers between devices  22.3 us (16%)
  between operations  13.5 us (10%)
  Pallas kernels  11.7 us (8%)
    all_to_all x1, blocking collectives, shards(): got = lax.all_to_all(send, ('x', 'z'), 0, 0, tiled=True)  36.5 us
    all_to_all x1, waiting for transfers between devices, shards(): states = lax.all_to_all(entering, ('x', 'z'), 0, 0, tiled=True)  19.8 us
    all_to_all x1, blocking collectives, shards(): lax.all_to_all(parts.reshape(NX * NY, TOK, COLS), ('x', 'y'), 0, 0, tiled...  16.3 us
    all_to_all x1, blocking collectives, shards(): everyone = lax.all_to_all(hidden, 'x', 0, 0, tiled=True)  13.7 us
    ppermute x1, starting transfers between devices, shards(): other = lax.ppermute(other, 'c', [(0, 1), (1, 0)])  8.76 us
    all_to_all x1, starting transfers between devices, shards(): states = lax.all_to_all(entering, ('x', 'z'), 0, 0, tiled=True)  8.7 us
    all_to_all x1, starting transfers between devices, shards(): swap = lax.all_to_all(swap, 'x', 0, 0, tiled=True)  4.85 us
    pallas_call x2, Pallas kernels, product(): pl.pallas_call(functools.partial(product_kernel, half), out_shape=shape(N...  3.95 us
  transfers between devices with their start and end apart: 4, of which 3 were waited for; matrix products, arithmetic and copies ran while one was open for 0% of the time, Pallas kernels for 5%

profile of v9, /device:TPU:1, one launch (start us, length us, event | category | flops | bytes accessed | tf_op | source)
XLA Modules:
  0.0 137.2 jit_solution(2767042949805158403)
XLA Ops:
  6.6 1.7 %pack.1 = bf16[4,16,1024]{2,1,0:T(8,128)(2,1)} custom-call(s32[1]{0:T(128)} %bitcast.core_ref, bf16[16,4096]{1,0:T(8,128)(2,1)} %weight_ref.1), custom_call_target="tpu_custom_call" | custom-call | bytes 300000 | tf_op jit(solution)/shard_map/pack/pallas_call | solution.py:200
  8.2 4.9 %all-to-all-start = ((bf16[4,16,1024]{2,1,0:T(8,128)(2,1)}), bf16[4,16,1024]{2,1,0:T(8,128)(2,1)S(1)}, u32[]{:S(2)}, u32[]{:S(2)}) async-start(bf16[4,16,1024]{2,1,0:T(8,128)(2,1)} %pack.1), calls=%async_computation | async-start | bytes 262144 | tf_op jit(solution)/shard_map/all_to_all | solution.py:209
  13.1 0.0 all-gather.3.cloned.1.call-start
  13.1 2.8 %fresh.1 = bf16[64,9,2,128]{3,2,1,0:T(2,128)(2,1)} custom-call(bf16[128,1024]{1,0:T(8,128)(2,1)} %x_ref.3, bf16[128,128]{1,0:T(8,128)(2,1)} %b_ref.3, f32[16,128]{1,0:T(8,128)} %step_ref.3, f32[16,128]{1,0:T(8,128)} %logs_ref.3), custom_call_target="tpu_custom_call" | custom-call | flops 40000000 | bytes 1000000 | tf_op jit(solution)/shard_map/fresh/pallas_call | solution.py:211
  15.9 2.0 %all-to-all-done = bf16[4,16,1024]{2,1,0:T(8,128)(2,1)S(1)} async-done(((bf16[4,16,1024]{2,1,0:T(8,128)(2,1)}), bf16[4,16,1024]{2,1,0:T(8,128)(2,1)S(1)}, u32[]{:S(2)}, u32[]{:S(2)}) %all-to-all-start) | async-done | bytes 131104 | tf_op jit(solution)/shard_map/all_to_all | solution.py:209
  17.9 0.7 copy-done.7
  18.6 0.0 all-gather.3.cloned.1.call-update
  18.6 36.5 %all_to_all.25.got_ref = bf16[64,9,2,128]{3,2,1,0:T(2,128)(2,1)S(1)} all-to-all(bf16[64,9,2,128]{3,2,1,0:T(2,128)(2,1)} %fresh.1), channel_id=1, replica_groups=mesh['x'=4,'z'=16,'y'=4,'c'=2] {'x','z'}, dimensions={0} | all-to-all | bytes 589824 | tf_op jit(solution)/shard_map/all_to_all | solution.py:217
  55.1 1.0 scan.1
  56.0 8.7 %all-to-all-start.2 = ((bf16[64,16,128]{2,1,0:T(8,128)(2,1)}), bf16[64,16,128]{2,1,0:T(8,128)(2,1)S(1)}, u32[]{:S(2)}, u32[]{:S(2)}) async-start(bf16[64,16,128]{2,1,0:T(8,128)(2,1)} %scan.1), calls=%async_computation.2 | async-start | bytes 524288 | tf_op jit(solution)/shard_map/all_to_all | solution.py:226
  64.7 0.1 broadcast_in_dim.9
  64.8 0.1 broadcast_in_dim_reshape.3.skip_ref
  64.9 1.2 inner.1
  66.1 19.8 %all-to-all-done.2.state_ref = bf16[64,16,128]{2,1,0:T(8,128)(2,1)S(1)} async-done(((bf16[64,16,128]{2,1,0:T(8,128)(2,1)}), bf16[64,16,128]{2,1,0:T(8,128)(2,1)S(1)}, u32[]{:S(2)}, u32[]{:S(2)}) %all-to-all-start.2) | async-done | bytes 262176 | tf_op jit(solution)/shard_map/all_to_all | solution.py:226
  85.9 0.4 hidden.1
  86.3 13.7 %all_to_all.26.hidden_ref = bf16[4,128,1024]{2,1,0:T(8,128)(2,1)S(1)} all-to-all(bf16[4,128,1024]{2,1,0:T(8,128)(2,1)S(1)} %hidden.1), channel_id=1, replica_groups=mesh['x'=4,'z'=16,'y'=4,'c'=2] {'x'}, dimensions={0} | all-to-all | bytes 2097152 | tf_op jit(solution)/shard_map/all_to_all | solution.py:231
  100.0 0.5 all-gather.3.cloned.1.call-done
  100.5 1.9 %other.1 = bf16[4,4,128,128]{3,2,1,0:T(8,128)(2,1)S(1)} custom-call(bf16[4,128,1024]{2,1,0:T(8,128)(2,1)S(1)} %all_to_all.26.hidden_ref, bf16[16,4,16,1024]{3,2,1,0:T(8,128)(2,1)} %bitcast.8), custom_call_target="tpu_custom_call" | custom-call | flops 536870912 | bytes 3000000 | tf_op jit(solution)/shard_map/other/pallas_call | solution.py:179
  102.4 8.8 %collective-permute-start = (bf16[4,4,128,128]{3,2,1,0:T(8,128)(2,1)S(1)}, bf16[4,4,128,128]{3,2,1,0:T(8,128)(2,1)S(1)}, u32[]{:S(2)}, u32[]{:S(2)}) collective-permute-start(bf16[4,4,128,128]{3,2,1,0:T(8,128)(2,1)S(1)} %other.1), channel_id=1, source_target_pairs={{0,1},{1,0},{2,3},{3,2},{4,5},{5,4},{6,7},{7,6},{8,9},{9,8},{10,11... | collective-permute-start | bytes 1572872 | tf_op jit(solution)/shard_map/ppermute | solution.py:233
  111.2 2.0 %mine.1.mine_ref = f32[4,4,128,128]{3,2,1,0:T(8,128)S(1)} custom-call(bf16[4,128,1024]{2,1,0:T(8,128)(2,1)} %copy-done, bf16[16,4,16,1024]{3,2,1,0:T(8,128)(2,1)} %bitcast.9), custom_call_target="tpu_custom_call" | custom-call | flops 536870912 | bytes 3000000 | tf_op jit(solution)/shard_map/mine/pallas_call | solution.py:179
  113.2 0.0 collective-permute-done.other_ref
  113.2 0.1 pair.1
  113.3 16.3 %all_to_all.27 = bf16[16,128,128]{2,1,0:T(8,128)(2,1)S(1)} all-to-all(bf16[16,128,128]{2,1,0:T(8,128)(2,1)S(1)} %bitcast.6), channel_id=1, replica_groups=mesh['x'=4,'z'=16,'y'=4,'c'=2] {'x','y'}, dimensions={0} | all-to-all | bytes 1048576 | tf_op jit(solution)/shard_map/all_to_all | solution.py:236
  129.7 0.7 sum.1
  (17 shorter events, 0.0 us)
Async XLA Ops:
  6.5 58.4 %copy-start.5 = (f32[16,128]{1,0:T(8,128)S(1)}, f32[16,128]{1,0:T(8,128)}, u32[]{:S(2)}) copy-start(f32[16,128]{1,0:T(8,128)} %logs_ref.3) | copy-start | bytes 24580
  6.5 58.4 %copy-start.4 = (f32[16,128]{1,0:T(8,128)S(1)}, f32[16,128]{1,0:T(8,128)}, u32[]{:S(2)}) copy-start(f32[16,128]{1,0:T(8,128)} %step_ref.3) | copy-start | bytes 24580
  6.5 58.4 %copy-start.3 = (bf16[128,128]{1,0:T(8,128)(2,1)S(1)}, bf16[128,128]{1,0:T(8,128)(2,1)}, u32[]{:S(2)}) copy-start(bf16[128,128]{1,0:T(8,128)(2,1)} %b_ref.3) | copy-start | bytes 98308
  6.5 58.4 %copy-start.1 = (bf16[128,1024]{1,0:T(8,128)(2,1)S(1)}, bf16[128,1024]{1,0:T(8,128)(2,1)}, u32[]{:S(2)}) copy-start(bf16[128,1024]{1,0:T(8,128)(2,1)} %x_ref.3) | copy-start | bytes 786436
  6.5 58.2 %copy-start.8 = (f32[16]{0:T(128)S(1)}, f32[16]{0:T(128)}, u32[]{:S(2)}) copy-start(f32[16]{0:T(128)} %param.13) | copy-start | bytes 196
  6.5 58.4 %copy-start.2 = (bf16[128,128]{1,0:T(8,128)(2,1)S(1)}, bf16[128,128]{1,0:T(8,128)(2,1)}, u32[]{:S(2)}) copy-start(bf16[128,128]{1,0:T(8,128)(2,1)} %c_ref.3) | copy-start | bytes 98308
  6.6 79.4 %copy-start.6 = (f32[1024]{0:T(1024)S(1)}, f32[1024]{0:T(1024)}, u32[]{:S(2)}) copy-start(f32[1024]{0:T(1024)} %param.14) | copy-start | bytes 12292
  8.2 9.7 %all-to-all-start = ((bf16[4,16,1024]{2,1,0:T(8,128)(2,1)}), bf16[4,16,1024]{2,1,0:T(8,128)(2,1)S(1)}, u32[]{:S(2)}, u32[]{:S(2)}) async-start(bf16[4,16,1024]{2,1,0:T(8,128)(2,1)} %pack.1), calls=%async_computation | async-start | bytes 262144 | tf_op jit(solution)/shard_map/all_to_all | solution.py:209
  13.1 87.4 %all-gather.3.cloned.1.call-start = ((), (), s32[]{:S(2)}) async-start(), calls=%async_computation.5 | async-start | bytes 2228224 | tf_op jit(solution)/shard_map/all_gather | solution.py:215
  17.9 0.7 copy-start.7
  56.0 29.9 %all-to-all-start.2 = ((bf16[64,16,128]{2,1,0:T(8,128)(2,1)}), bf16[64,16,128]{2,1,0:T(8,128)(2,1)S(1)}, u32[]{:S(2)}, u32[]{:S(2)}) async-start(bf16[64,16,128]{2,1,0:T(8,128)(2,1)} %scan.1), calls=%async_computation.2 | async-start | bytes 524288 | tf_op jit(solution)/shard_map/all_to_all | solution.py:226
  100.0 11.2 %copy-start = (bf16[4,128,1024]{2,1,0:T(8,128)(2,1)}, bf16[4,128,1024]{2,1,0:T(8,128)(2,1)S(1)}, u32[]{:S(2)}) copy-start(bf16[4,128,1024]{2,1,0:T(8,128)(2,1)S(1)} %all_to_all.26.hidden_ref) | copy-start | bytes 3145732
  102.4 10.8 %collective-permute-start = (bf16[4,4,128,128]{3,2,1,0:T(8,128)(2,1)S(1)}, bf16[4,4,128,128]{3,2,1,0:T(8,128)(2,1)S(1)}, u32[]{:S(2)}, u32[]{:S(2)}) collective-permute-start(bf16[4,4,128,128]{3,2,1,0:T(8,128)(2,1)S(1)} %other.1), channel_id=1, source_target_pairs={{0,1},{1,0},{2,3},{3,2},{4,5},{5,4},{6,7},{7,6},{8,9},{9,8},{10,11... | collective-permute-start | bytes 1572872 | tf_op jit(solution)/shard_map/ppermute | solution.py:233
Sparse Core Ops, SparseCore 0:
  18.7 81.7 all-gather.2

commit v10 on v9

--- a/solution.py
+++ b/solution.py
@@ -54,10 +54,7 @@
     return dot(per_head, owner, 0, 0, HIGH)
 
 
-def pack_kernel(core_ref, weight_ref, out_ref, held_ref, sem):
-    copy = pltpu.make_async_copy(weight_ref, held_ref, sem)
-    copy.start()
-    copy.wait()
+def pack_kernel(core_ref, held_ref, out_ref):
     first = core_ref[0] == 0
     for x in range(NX):
         for y in range(NY):
@@ -126,28 +123,22 @@
         out_ref[k, :, :] = hidden
 
 
-def product_kernel(half, hidden_ref, weight_ref, out_ref, tokens_ref, held_ref, total_ref, sems):
+def product_kernel(half, hidden_ref, weight_ref, out_ref, held_ref, total_ref, sems):
     depth = WIDTH // NX
     wide = NY * COLS
-    copies = []
+    copies = [
+        pltpu.make_async_copy(
+            weight_ref.at[:, k, :, pl.ds(half * wide, wide)], held_ref.at[k], sems.at[k]
+        )
+        for k in range(NX)
+    ]
+    for copy in copies:
+        copy.start()
     for k in range(NX):
-        part = hidden_ref.at[:, :, pl.ds(k * depth, depth)]
-        rows = weight_ref.at[:, k, :, pl.ds(half * wide, wide)]
-        copies.append(
-            (
-                pltpu.make_async_copy(part, tokens_ref.at[k], sems.at[0, k]),
-                pltpu.make_async_copy(rows, held_ref.at[k], sems.at[1, k]),
-            )
-        )
-    for pair in copies:
-        for copy in pair:
-            copy.start()
-    for k in range(NX):
-        for copy in copies[k]:
-            copy.wait()
+        copies[k].wait()
         rows = held_ref[k].reshape(depth, wide)
         for i in range(NX):
-            term = dot(tokens_ref[k, i], rows, 1, 0)
+            term = dot(hidden_ref[i, :, k * depth : (k + 1) * depth], rows, 1, 0)
             if k == 0:
                 total_ref[i] = term
             elif k < NX - 1:
@@ -179,15 +170,14 @@
     return pl.pallas_call(
         functools.partial(product_kernel, half),
         out_shape=shape(NX, NY, TOK, COLS, dtype=bf16 if half else f32),
-        in_specs=[pl.BlockSpec(memory_space=pl.ANY)] * 2,
+        in_specs=[pl.BlockSpec(memory_space=pltpu.VMEM), pl.BlockSpec(memory_space=pl.ANY)],
         scratch_shapes=[
-            pltpu.VMEM((NX, NX, TOK, WIDTH // NX), bf16),
             pltpu.VMEM((NX, NZ, depth, wide), bf16),
             pltpu.VMEM((NX, TOK, wide), f32),
-            pltpu.SemaphoreType.DMA((2, NX)),
+            pltpu.SemaphoreType.DMA((NX,)),
         ],
         name="other" if half else "mine",
-        compiler_params=pltpu.CompilerParams(vmem_limit_bytes=52 * 2**20),
+        compiler_params=pltpu.CompilerParams(vmem_limit_bytes=103 * 2**19),
         cost_estimate=pl.CostEstimate(
             flops=2 * NX * TOK * WIDTH * wide, bytes_accessed=3 * 10**6, transcendentals=0
         ),
@@ -200,10 +190,9 @@
     swap = pl.pallas_call(
         pack_kernel,
         out_shape=shape(NX, depth, NTP * COLS),
-        in_specs=[pl.BlockSpec(memory_space=pltpu.SMEM), pl.BlockSpec(memory_space=pl.ANY)],
-        scratch_shapes=[pltpu.VMEM(out_weight.shape, bf16), pltpu.SemaphoreType.DMA(())],
+        in_specs=[pl.BlockSpec(memory_space=pltpu.SMEM), pl.BlockSpec(memory_space=pltpu.VMEM)],
         name="pack",
-        compiler_params=pltpu.CompilerParams(vmem_limit_bytes=LARGE),
+        compiler_params=pltpu.CompilerParams(vmem_limit_bytes=32 * 2**20),
         cost_estimate=pl.CostEstimate(flops=0, bytes_accessed=3 * 10**5, transcendentals=0),
     )(core, out_weight)
     swap = lax.all_to_all(swap, "x", 0, 0, tiled=True)
@@ -212,7 +201,9 @@
         fresh_kernel, shape(CTX, PAIRS + 1, 2, N), 4 * 10**7, 10**6, "fresh", LARGE
     )(x_input, b_input, step, log_decay)
     send, swap = lax.optimization_barrier((send, swap))
-    weight = lax.all_gather(swap, "z", axis=0)
+    flat = swap.reshape(NX, 2, 8, NTP, COLS).transpose(2, 0, 1, 3, 4).reshape(8, NX * 2 * NTP * COLS)
+    weight = lax.all_gather(flat, "z", axis=0).reshape(NZ, 8, NX, 2, NTP, COLS)
+    weight = weight.transpose(0, 2, 3, 1, 4, 5).reshape(NZ, NX, depth, NTP * COLS)
 
     got = lax.all_to_all(send, ("x", "z"), 0, 0, tiled=True)
     inner, scale = call(

time: 138 us -> 138 us (level)
  no operation moved by 1% of the time
where the time goes in v10:
time: 138 us; the launch traced here: 137 us
  blocking collectives  66.6 us (48%)
  starting transfers between devices  22.3 us (16%)
  waiting for transfers between devices  22.2 us (16%)
  between operations  13.5 us (10%)
  Pallas kernels  10.6 us (8%)
  local copies, waits for them, and re-layouts  1.78 us (1%)
    all_to_all x1, blocking collectives, shards(): got = lax.all_to_all(send, ('x', 'z'), 0, 0, tiled=True)  36.5 us
    all_to_all x1, waiting for transfers between devices, shards(): states = lax.all_to_all(entering, ('x', 'z'), 0, 0, tiled=True)  19.7 us
    all_to_all x1, blocking collectives, shards(): lax.all_to_all(parts.reshape(NX * NY, TOK, COLS), ('x', 'y'), 0, 0, tiled...  16.3 us
    all_to_all x1, blocking collectives, shards(): everyone = lax.all_to_all(hidden, 'x', 0, 0, tiled=True)  13.9 us
    ppermute x1, starting transfers between devices, shards(): other = lax.ppermute(other, 'c', [(0, 1), (1, 0)])  8.75 us
    all_to_all x1, starting transfers between devices, shards(): states = lax.all_to_all(entering, ('x', 'z'), 0, 0, tiled=True)  8.7 us
    all_to_all x1, starting transfers between devices, shards(): swap = lax.all_to_all(swap, 'x', 0, 0, tiled=True)  4.84 us
    pallas_call x2, Pallas kernels, product(): pl.pallas_call(functools.partial(product_kernel, half), out_shape=shape(N...  3.76 us
  transfers between devices with their start and end apart: 4, of which 3 were waited for; matrix products, arithmetic and copies ran while one was open for 0% of the time, Pallas kernels for 5%

profile of v10, /device:TPU:1, one launch (start us, length us, event | category | flops | bytes accessed | tf_op | source)
XLA Modules:
  0.0 137.0 jit_solution(16400564271910289113)
XLA Ops:
  6.5 0.9 copy-done.1
  7.5 0.0 copy-start.5
  7.5 0.7 pack.1
  8.2 4.8 %all-to-all-start = ((bf16[4,16,1024]{2,1,0:T(8,128)(2,1)}), bf16[4,16,1024]{2,1,0:T(8,128)(2,1)S(1)}, u32[]{:S(2)}, u32[]{:S(2)}) async-start(bf16[4,16,1024]{2,1,0:T(8,128)(2,1)} %pack.1), calls=%async_computation | async-start | bytes 262144 | tf_op jit(solution)/shard_map/all_to_all | solution.py:198
  13.0 2.8 %fresh.1 = bf16[64,9,2,128]{3,2,1,0:T(2,128)(2,1)} custom-call(bf16[128,1024]{1,0:T(8,128)(2,1)} %x_ref.3, bf16[128,128]{1,0:T(8,128)(2,1)} %b_ref.3, f32[16,128]{1,0:T(8,128)} %step_ref.3, f32[16,128]{1,0:T(8,128)} %logs_ref.3), custom_call_target="tpu_custom_call" | custom-call | flops 40000000 | bytes 1000000 | tf_op jit(solution)/shard_map/fresh/pallas_call | solution.py:200
  15.9 2.0 %all-to-all-done = bf16[4,16,1024]{2,1,0:T(8,128)(2,1)S(1)} async-done(((bf16[4,16,1024]{2,1,0:T(8,128)(2,1)}), bf16[4,16,1024]{2,1,0:T(8,128)(2,1)S(1)}, u32[]{:S(2)}, u32[]{:S(2)}) %all-to-all-start) | async-done | bytes 131104 | tf_op jit(solution)/shard_map/all_to_all | solution.py:198
  17.9 0.7 copy-done.7
  18.5 0.0 all-gather.2.cloned.1.call-update
  18.6 36.5 %all_to_all.25.got_ref = bf16[64,9,2,128]{3,2,1,0:T(2,128)(2,1)S(1)} all-to-all(bf16[64,9,2,128]{3,2,1,0:T(2,128)(2,1)} %fresh.1), channel_id=1, replica_groups=mesh['x'=4,'z'=16,'y'=4,'c'=2] {'x','z'}, dimensions={0} | all-to-all | bytes 589824 | tf_op jit(solution)/shard_map/all_to_all | solution.py:208
  55.0 1.0 scan.1
  56.0 8.7 %all-to-all-start.2 = ((bf16[64,16,128]{2,1,0:T(8,128)(2,1)}), bf16[64,16,128]{2,1,0:T(8,128)(2,1)S(1)}, u32[]{:S(2)}, u32[]{:S(2)}) async-start(bf16[64,16,128]{2,1,0:T(8,128)(2,1)} %scan.1), calls=%async_computation.2 | async-start | bytes 524288 | tf_op jit(solution)/shard_map/all_to_all | solution.py:217
  64.7 0.1 broadcast_in_dim.9
  64.8 0.1 broadcast_in_dim_reshape.3.skip_ref
  64.9 1.2 inner.1
  66.0 19.7 %all-to-all-done.2.state_ref = bf16[64,16,128]{2,1,0:T(8,128)(2,1)S(1)} async-done(((bf16[64,16,128]{2,1,0:T(8,128)(2,1)}), bf16[64,16,128]{2,1,0:T(8,128)(2,1)S(1)}, u32[]{:S(2)}, u32[]{:S(2)}) %all-to-all-start.2) | async-done | bytes 262176 | tf_op jit(solution)/shard_map/all_to_all | solution.py:217
  85.8 0.4 hidden.1
  86.1 13.9 %all_to_all.26.hidden_ref = bf16[4,128,1024]{2,1,0:T(8,128)(2,1)S(1)} all-to-all(bf16[4,128,1024]{2,1,0:T(8,128)(2,1)S(1)} %hidden.1), channel_id=1, replica_groups=mesh['x'=4,'z'=16,'y'=4,'c'=2] {'x'}, dimensions={0} | all-to-all | bytes 2097152 | tf_op jit(solution)/shard_map/all_to_all | solution.py:222
  100.0 0.4 all-gather.2.cloned.1.call-done
  100.4 1.9 %other.1 = bf16[4,4,128,128]{3,2,1,0:T(8,128)(2,1)S(1)} custom-call(bf16[4,128,1024]{2,1,0:T(8,128)(2,1)S(1)} %all_to_all.26.hidden_ref, bf16[16,4,16,1024]{3,2,1,0:T(8,128)(2,1)} %bitcast.17), custom_call_target="tpu_custom_call" | custom-call | flops 536870912 | bytes 3000000 | tf_op jit(solution)/shard_map/other/pallas_call | solution.py:170
  102.3 8.8 %collective-permute-start = (bf16[4,4,128,128]{3,2,1,0:T(8,128)(2,1)S(1)}, bf16[4,4,128,128]{3,2,1,0:T(8,128)(2,1)S(1)}, u32[]{:S(2)}, u32[]{:S(2)}) collective-permute-start(bf16[4,4,128,128]{3,2,1,0:T(8,128)(2,1)S(1)} %other.1), channel_id=1, source_target_pairs={{0,1},{1,0},{2,3},{3,2},{4,5},{5,4},{6,7},{7,6},{8,9},{9,8},{10,11... | collective-permute-start | bytes 1572872 | tf_op jit(solution)/shard_map/ppermute | solution.py:224
  111.1 1.9 %mine.1.mine_ref = f32[4,4,128,128]{3,2,1,0:T(8,128)S(1)} custom-call(bf16[4,128,1024]{2,1,0:T(8,128)(2,1)S(1)} %all_to_all.26.hidden_ref, bf16[16,4,16,1024]{3,2,1,0:T(8,128)(2,1)} %bitcast.18), custom_call_target="tpu_custom_call" | custom-call | flops 536870912 | bytes 3000000 | tf_op jit(solution)/shard_map/mine/pallas_call | solution.py:170
  113.0 0.1 pair.1
  113.1 16.3 %all_to_all.27 = bf16[16,128,128]{2,1,0:T(8,128)(2,1)S(1)} all-to-all(bf16[16,128,128]{2,1,0:T(8,128)(2,1)S(1)} %bitcast.15), channel_id=1, replica_groups=mesh['x'=4,'z'=16,'y'=4,'c'=2] {'x','y'}, dimensions={0} | all-to-all | bytes 1048576 | tf_op jit(solution)/shard_map/all_to_all | solution.py:227
  129.4 0.7 sum.1
  (17 shorter events, 0.0 us)
Async XLA Ops:
  6.5 58.3 %copy-start = (bf16[128,1024]{1,0:T(8,128)(2,1)S(1)}, bf16[128,1024]{1,0:T(8,128)(2,1)}, u32[]{:S(2)}) copy-start(bf16[128,1024]{1,0:T(8,128)(2,1)} %x_ref.3) | copy-start | bytes 786436
  6.5 0.9 copy-start.1
  7.5 57.2 %copy-start.8 = (f32[16]{0:T(128)S(1)}, f32[16]{0:T(128)}, u32[]{:S(2)}) copy-start(f32[16]{0:T(128)} %param.13) | copy-start | bytes 196
  7.5 57.4 %copy-start.2 = (bf16[128,128]{1,0:T(8,128)(2,1)S(1)}, bf16[128,128]{1,0:T(8,128)(2,1)}, u32[]{:S(2)}) copy-start(bf16[128,128]{1,0:T(8,128)(2,1)} %c_ref.3) | copy-start | bytes 98308
  7.5 57.4 %copy-start.3 = (bf16[128,128]{1,0:T(8,128)(2,1)S(1)}, bf16[128,128]{1,0:T(8,128)(2,1)}, u32[]{:S(2)}) copy-start(bf16[128,128]{1,0:T(8,128)(2,1)} %b_ref.3) | copy-start | bytes 98308
  7.5 57.4 %copy-start.4 = (f32[16,128]{1,0:T(8,128)S(1)}, f32[16,128]{1,0:T(8,128)}, u32[]{:S(2)}) copy-start(f32[16,128]{1,0:T(8,128)} %step_ref.3) | copy-start | bytes 24580
  7.5 57.4 %copy-start.5 = (f32[16,128]{1,0:T(8,128)S(1)}, f32[16,128]{1,0:T(8,128)}, u32[]{:S(2)}) copy-start(f32[16,128]{1,0:T(8,128)} %logs_ref.3) | copy-start | bytes 24580
  7.5 78.2 %copy-start.6 = (f32[1024]{0:T(1024)S(1)}, f32[1024]{0:T(1024)}, u32[]{:S(2)}) copy-start(f32[1024]{0:T(1024)} %param.14) | copy-start | bytes 12292
  8.2 9.7 %all-to-all-start = ((bf16[4,16,1024]{2,1,0:T(8,128)(2,1)}), bf16[4,16,1024]{2,1,0:T(8,128)(2,1)S(1)}, u32[]{:S(2)}, u32[]{:S(2)}) async-start(bf16[4,16,1024]{2,1,0:T(8,128)(2,1)} %pack.1), calls=%async_computation | async-start | bytes 262144 | tf_op jit(solution)/shard_map/all_to_all | solution.py:198
  13.0 87.4 %all-gather.2.cloned.1.call-start = ((), (), s32[]{:S(2)}) async-start(), calls=%async_computation.5 | async-start | bytes 2228224 | tf_op jit(solution)/shard_map/all_gather | solution.py:205
  17.9 0.7 copy-start.7
  56.0 29.8 %all-to-all-start.2 = ((bf16[64,16,128]{2,1,0:T(8,128)(2,1)}), bf16[64,16,128]{2,1,0:T(8,128)(2,1)S(1)}, u32[]{:S(2)}, u32[]{:S(2)}) async-start(bf16[64,16,128]{2,1,0:T(8,128)(2,1)} %scan.1), calls=%async_computation.2 | async-start | bytes 524288 | tf_op jit(solution)/shard_map/all_to_all | solution.py:217
  102.3 10.7 %collective-permute-start = (bf16[4,4,128,128]{3,2,1,0:T(8,128)(2,1)S(1)}, bf16[4,4,128,128]{3,2,1,0:T(8,128)(2,1)S(1)}, u32[]{:S(2)}, u32[]{:S(2)}) collective-permute-start(bf16[4,4,128,128]{3,2,1,0:T(8,128)(2,1)S(1)} %other.1), channel_id=1, source_target_pairs={{0,1},{1,0},{2,3},{3,2},{4,5},{5,4},{6,7},{7,6},{8,9},{9,8},{10,11... | collective-permute-start | bytes 1572872 | tf_op jit(solution)/shard_map/ppermute | solution.py:224
Sparse Core Ops, SparseCore 0:
  18.7 81.7 all-gather.1

commit v11 on v10

--- a/solution.py
+++ b/solution.py
@@ -54,15 +54,13 @@
     return dot(per_head, owner, 0, 0, HIGH)
 
 
-def pack_kernel(core_ref, held_ref, out_ref):
-    first = core_ref[0] == 0
+def pack_kernel(weight_ref, out_ref):
     for x in range(NX):
-        for y in range(NY):
-            even, odd = (
-                held_ref[:, pl.ds(((y * NC + c) * NX + x) * COLS, COLS)] for c in range(NC)
-            )
-            out_ref[x, :, y * COLS : (y + 1) * COLS] = jnp.where(first, even, odd)
-            out_ref[x, :, (NY + y) * COLS : (NY + y + 1) * COLS] = jnp.where(first, odd, even)
+        for c in range(NC):
+            for y in range(NY):
+                begin = ((y * NC + c) * NX + x) * COLS
+                end = (c * NY + y) * COLS
+                out_ref[x, :, end : end + COLS] = weight_ref[:, begin : begin + COLS]
 
 
 def fresh_kernel(x_ref, b_ref, step_ref, logs_ref, out_ref):
@@ -123,12 +121,14 @@
         out_ref[k, :, :] = hidden
 
 
-def product_kernel(half, hidden_ref, weight_ref, out_ref, held_ref, total_ref, sems):
+def product_kernel(half, core_ref, hidden_ref, weight_ref, out_ref, held_ref, total_ref, sems):
     depth = WIDTH // NX
     wide = NY * COLS
+    core = 1 - core_ref[0] if half else core_ref[0]
+    begin = pl.multiple_of(core * wide, wide)
     copies = [
         pltpu.make_async_copy(
-            weight_ref.at[:, k, :, pl.ds(half * wide, wide)], held_ref.at[k], sems.at[k]
+            weight_ref.at[:, k, :, pl.ds(begin, wide)], held_ref.at[k], sems.at[k]
         )
         for k in range(NX)
     ]
@@ -165,12 +165,16 @@
     return jax.ShapeDtypeStruct(dims, dtype)
 
 
-def product(everyone, weight, half):
+def product(core, everyone, weight, half):
     depth, wide = weight.shape[2], NY * COLS
     return pl.pallas_call(
         functools.partial(product_kernel, half),
         out_shape=shape(NX, NY, TOK, COLS, dtype=bf16 if half else f32),
-        in_specs=[pl.BlockSpec(memory_space=pltpu.VMEM), pl.BlockSpec(memory_space=pl.ANY)],
+        in_specs=[
+            pl.BlockSpec(memory_space=pltpu.SMEM),
+            pl.BlockSpec(memory_space=pltpu.VMEM),
+            pl.BlockSpec(memory_space=pl.ANY),
+        ],
         scratch_shapes=[
             pltpu.VMEM((NX, NZ, depth, wide), bf16),
             pltpu.VMEM((NX, TOK, wide), f32),
@@ -181,7 +185,7 @@
         cost_estimate=pl.CostEstimate(
             flops=2 * NX * TOK * WIDTH * wide, bytes_accessed=3 * 10**6, transcendentals=0
         ),
-    )(everyone, weight)
+    )(core, everyone, weight)
 
 
 def shards(x_input, b_input, c_input, step, log_decay, skip, gain, out_weight):
@@ -190,11 +194,10 @@
     swap = pl.pallas_call(
         pack_kernel,
         out_shape=shape(NX, depth, NTP * COLS),
-        in_specs=[pl.BlockSpec(memory_space=pltpu.SMEM), pl.BlockSpec(memory_space=pltpu.VMEM)],
         name="pack",
         compiler_params=pltpu.CompilerParams(vmem_limit_bytes=32 * 2**20),
         cost_estimate=pl.CostEstimate(flops=0, bytes_accessed=3 * 10**5, transcendentals=0),
-    )(core, out_weight)
+    )(out_weight)
     swap = lax.all_to_all(swap, "x", 0, 0, tiled=True)
 
     send = call(
@@ -220,9 +223,9 @@
         inner, scale, c_input, states, gain[None]
     )
     everyone = lax.all_to_all(hidden, "x", 0, 0, tiled=True)
-    other = product(everyone, weight, 1)
+    other = product(core, everyone, weight, 1)
     other = lax.ppermute(other, "c", [(0, 1), (1, 0)])
-    mine = product(everyone, weight, 0)
+    mine = product(core, everyone, weight, 0)
     parts = call(pair_kernel, shape(NX, NY, TOK, COLS), 10**6, 2 * 10**6, "pair")(mine, other)
     parts = lax.all_to_all(parts.reshape(NX * NY, TOK, COLS), ("x", "y"), 0, 0, tiled=True)
     return call(sum_kernel, shape(TOK, NX * COLS), 10**6, 10**6, "sum")(

time: 138 us -> 138 us (level)
  blocking collectives: 66.6 us -> 52.8 us
  waiting for transfers between devices: 22.2 us -> 31.3 us
  starting transfers between devices: 22.3 us -> 26.2 us
    all_to_all x1 -> x0, blocking collectives: 13.9 us -> none  [shards(): everyone = lax.all_to_all(hidden, 'x', 0, 0, tiled=True)]
    all_to_all x0 -> x1, waiting for transfers between devices: none -> 9.75 us  [shards(): everyone = lax.all_to_all(hidden, 'x', 0, 0, tiled=True)]
    all_to_all x0 -> x1, starting transfers between devices: none -> 4.3 us  [shards(): everyone = lax.all_to_all(hidden, 'x', 0, 0, tiled=True)]
  transfers between devices with their start and end apart: 4 -> 5, of which waited for: 3 -> 3; matrix products, arithmetic and copies ran while one was open for 0% -> 0% of each run, Pallas kernels for 5% -> 6%
where the time goes in v11:
time: 138 us; the launch traced here: 137 us
  blocking collectives  52.8 us (38%)
  waiting for transfers between devices  31.3 us (23%)
  starting transfers between devices  26.2 us (19%)
  between operations  13.5 us (10%)
  Pallas kernels  11.5 us (8%)
  local copies, waits for them, and re-layouts  1.78 us (1%)
    all_to_all x1, blocking collectives, shards(): got = lax.all_to_all(send, ('x', 'z'), 0, 0, tiled=True)  36.5 us
    all_to_all x1, waiting for transfers between devices, shards(): states = lax.all_to_all(entering, ('x', 'z'), 0, 0, tiled=True)  19.5 us
    all_to_all x1, blocking collectives, shards(): lax.all_to_all(parts.reshape(NX * NY, TOK, COLS), ('x', 'y'), 0, 0, tiled...  16.3 us
    all_to_all x1, waiting for transfers between devices, shards(): everyone = lax.all_to_all(hidden, 'x', 0, 0, tiled=True)  9.75 us
    all_to_all x1, starting transfers between devices, shards(): states = lax.all_to_all(entering, ('x', 'z'), 0, 0, tiled=True)  8.68 us
    ppermute x1, starting transfers between devices, shards(): other = lax.ppermute(other, 'c', [(0, 1), (1, 0)])  8.41 us
    all_to_all x1, starting transfers between devices, shards(): swap = lax.all_to_all(swap, 'x', 0, 0, tiled=True)  4.84 us
    all_to_all x1, starting transfers between devices, shards(): everyone = lax.all_to_all(hidden, 'x', 0, 0, tiled=True)  4.3 us
  transfers between devices with their start and end apart: 5, of which 3 were waited for; matrix products, arithmetic and copies ran while one was open for 0% of the time, Pallas kernels for 6%

profile of v11, /device:TPU:1, one launch (start us, length us, event | category | flops | bytes accessed | tf_op | source)
XLA Modules:
  0.0 137.1 jit_solution(12228438849511571223)
XLA Ops:
  6.5 0.9 copy-done.1
  7.5 0.0 copy-start.5
  7.5 0.7 pack.1
  8.2 4.8 %all-to-all-start = ((bf16[4,16,1024]{2,1,0:T(8,128)(2,1)}), bf16[4,16,1024]{2,1,0:T(8,128)(2,1)S(1)}, u32[]{:S(2)}, u32[]{:S(2)}) async-start(bf16[4,16,1024]{2,1,0:T(8,128)(2,1)} %pack.1), calls=%async_computation | async-start | bytes 262144 | tf_op jit(solution)/shard_map/all_to_all | solution.py:201
  13.0 2.8 %fresh.1 = bf16[64,9,2,128]{3,2,1,0:T(2,128)(2,1)} custom-call(bf16[128,1024]{1,0:T(8,128)(2,1)} %x_ref.3, bf16[128,128]{1,0:T(8,128)(2,1)} %b_ref.3, f32[16,128]{1,0:T(8,128)} %step_ref.3, f32[16,128]{1,0:T(8,128)} %logs_ref.3), custom_call_target="tpu_custom_call" | custom-call | flops 40000000 | bytes 1000000 | tf_op jit(solution)/shard_map/fresh/pallas_call | solution.py:203
  15.9 2.0 %all-to-all-done = bf16[4,16,1024]{2,1,0:T(8,128)(2,1)S(1)} async-done(((bf16[4,16,1024]{2,1,0:T(8,128)(2,1)}), bf16[4,16,1024]{2,1,0:T(8,128)(2,1)S(1)}, u32[]{:S(2)}, u32[]{:S(2)}) %all-to-all-start) | async-done | bytes 131104 | tf_op jit(solution)/shard_map/all_to_all | solution.py:201
  17.9 0.7 copy-done.7
  18.5 0.0 all-gather.2.cloned.1.call-update
  18.5 36.5 %all_to_all.25.got_ref = bf16[64,9,2,128]{3,2,1,0:T(2,128)(2,1)S(1)} all-to-all(bf16[64,9,2,128]{3,2,1,0:T(2,128)(2,1)} %fresh.1), channel_id=1, replica_groups=mesh['x'=4,'z'=16,'y'=4,'c'=2] {'x','z'}, dimensions={0} | all-to-all | bytes 589824 | tf_op jit(solution)/shard_map/all_to_all | solution.py:211
  55.0 0.9 scan.1
  56.0 8.7 %all-to-all-start.2 = ((bf16[64,16,128]{2,1,0:T(8,128)(2,1)}), bf16[64,16,128]{2,1,0:T(8,128)(2,1)S(1)}, u32[]{:S(2)}, u32[]{:S(2)}) async-start(bf16[64,16,128]{2,1,0:T(8,128)(2,1)} %scan.1), calls=%async_computation.2 | async-start | bytes 524288 | tf_op jit(solution)/shard_map/all_to_all | solution.py:220
  64.7 0.1 broadcast_in_dim.10
  64.7 0.1 broadcast_in_dim_reshape.3.skip_ref
  64.9 1.2 inner.1
  66.0 19.5 %all-to-all-done.2.state_ref = bf16[64,16,128]{2,1,0:T(8,128)(2,1)S(1)} async-done(((bf16[64,16,128]{2,1,0:T(8,128)(2,1)}), bf16[64,16,128]{2,1,0:T(8,128)(2,1)S(1)}, u32[]{:S(2)}, u32[]{:S(2)}) %all-to-all-start.2) | async-done | bytes 262176 | tf_op jit(solution)/shard_map/all_to_all | solution.py:220
  85.6 1.3 hidden.1
  86.9 4.3 %all-to-all-start.3 = ((bf16[4,128,1024]{2,1,0:T(8,128)(2,1)}), bf16[4,128,1024]{2,1,0:T(8,128)(2,1)S(1)}, u32[]{:S(2)}, u32[]{:S(2)}) async-start(bf16[4,128,1024]{2,1,0:T(8,128)(2,1)} %hidden.1), calls=%async_computation.3 | async-start | bytes 2097152 | tf_op jit(solution)/shard_map/all_to_all | solution.py:225
  91.2 9.7 %all-to-all-done.3.hidden_ref = bf16[4,128,1024]{2,1,0:T(8,128)(2,1)S(1)} async-done(((bf16[4,128,1024]{2,1,0:T(8,128)(2,1)}), bf16[4,128,1024]{2,1,0:T(8,128)(2,1)S(1)}, u32[]{:S(2)}, u32[]{:S(2)}) %all-to-all-start.3) | async-done | bytes 1048608 | tf_op jit(solution)/shard_map/all_to_all | solution.py:225
  100.9 1.9 %other.1 = bf16[4,4,128,128]{3,2,1,0:T(8,128)(2,1)S(1)} custom-call(s32[1]{0:T(128)} %bitcast.core_ref, bf16[4,128,1024]{2,1,0:T(8,128)(2,1)S(1)} %all-to-all-done.3.hidden_ref, bf16[16,4,16,1024]{3,2,1,0:T(8,128)(2,1)} %bitcast.17), custom_call_target="tpu_custom_call" | custom-call | flops 536870912 | bytes 3000000 | tf_op jit(solution)/shard_map/other/pallas_call | solution.py:170
  102.8 8.4 %collective-permute-start = (bf16[4,4,128,128]{3,2,1,0:T(8,128)(2,1)S(1)}, bf16[4,4,128,128]{3,2,1,0:T(8,128)(2,1)S(1)}, u32[]{:S(2)}, u32[]{:S(2)}) collective-permute-start(bf16[4,4,128,128]{3,2,1,0:T(8,128)(2,1)S(1)} %other.1), channel_id=1, source_target_pairs={{0,1},{1,0},{2,3},{3,2},{4,5},{5,4},{6,7},{7,6},{8,9},{9,8},{10,11... | collective-permute-start | bytes 1572872 | tf_op jit(solution)/shard_map/ppermute | solution.py:227
  111.2 1.9 %mine.1.mine_ref = f32[4,4,128,128]{3,2,1,0:T(8,128)S(1)} custom-call(s32[1]{0:T(128)} %bitcast.core_ref, bf16[4,128,1024]{2,1,0:T(8,128)(2,1)S(1)} %all-to-all-done.3.hidden_ref, bf16[16,4,16,1024]{3,2,1,0:T(8,128)(2,1)} %bitcast.18), custom_call_target="tpu_custom_call" | custom-call | flops 536870912 | bytes 3000000 | tf_op jit(solution)/shard_map/mine/pallas_call | solution.py:170
  113.2 0.1 pair.1
  113.2 16.3 %all_to_all.26 = bf16[16,128,128]{2,1,0:T(8,128)(2,1)S(1)} all-to-all(bf16[16,128,128]{2,1,0:T(8,128)(2,1)S(1)} %bitcast.15), channel_id=1, replica_groups=mesh['x'=4,'z'=16,'y'=4,'c'=2] {'x','y'}, dimensions={0} | all-to-all | bytes 1048576 | tf_op jit(solution)/shard_map/all_to_all | solution.py:230
  129.6 0.7 sum.1
  (18 shorter events, 0.0 us)
Async XLA Ops:
  6.5 58.3 %copy-start = (bf16[128,1024]{1,0:T(8,128)(2,1)S(1)}, bf16[128,1024]{1,0:T(8,128)(2,1)}, u32[]{:S(2)}) copy-start(bf16[128,1024]{1,0:T(8,128)(2,1)} %x_ref.3) | copy-start | bytes 786436
  6.5 0.9 copy-start.1
  7.5 57.2 %copy-start.8 = (f32[16]{0:T(128)S(1)}, f32[16]{0:T(128)}, u32[]{:S(2)}) copy-start(f32[16]{0:T(128)} %param.13) | copy-start | bytes 196
  7.5 57.3 %copy-start.2 = (bf16[128,128]{1,0:T(8,128)(2,1)S(1)}, bf16[128,128]{1,0:T(8,128)(2,1)}, u32[]{:S(2)}) copy-start(bf16[128,128]{1,0:T(8,128)(2,1)} %c_ref.3) | copy-start | bytes 98308
  7.5 57.3 %copy-start.3 = (bf16[128,128]{1,0:T(8,128)(2,1)S(1)}, bf16[128,128]{1,0:T(8,128)(2,1)}, u32[]{:S(2)}) copy-start(bf16[128,128]{1,0:T(8,128)(2,1)} %b_ref.3) | copy-start | bytes 98308
  7.5 57.4 %copy-start.4 = (f32[16,128]{1,0:T(8,128)S(1)}, f32[16,128]{1,0:T(8,128)}, u32[]{:S(2)}) copy-start(f32[16,128]{1,0:T(8,128)} %step_ref.3) | copy-start | bytes 24580
  7.5 57.4 %copy-start.5 = (f32[16,128]{1,0:T(8,128)S(1)}, f32[16,128]{1,0:T(8,128)}, u32[]{:S(2)}) copy-start(f32[16,128]{1,0:T(8,128)} %logs_ref.3) | copy-start | bytes 24580
  7.5 78.0 %copy-start.6 = (f32[1024]{0:T(1024)S(1)}, f32[1024]{0:T(1024)}, u32[]{:S(2)}) copy-start(f32[1024]{0:T(1024)} %param.14) | copy-start | bytes 12292
  8.2 9.7 %all-to-all-start = ((bf16[4,16,1024]{2,1,0:T(8,128)(2,1)}), bf16[4,16,1024]{2,1,0:T(8,128)(2,1)S(1)}, u32[]{:S(2)}, u32[]{:S(2)}) async-start(bf16[4,16,1024]{2,1,0:T(8,128)(2,1)} %pack.1), calls=%async_computation | async-start | bytes 262144 | tf_op jit(solution)/shard_map/all_to_all | solution.py:201
  13.0 87.9 %all-gather.2.cloned.1.call-start = ((), (), s32[]{:S(2)}) async-start(), calls=%async_computation.5 | async-start | bytes 2228224 | tf_op jit(solution)/shard_map/all_gather | solution.py:208
  17.9 0.7 copy-start.7
  56.0 29.6 %all-to-all-start.2 = ((bf16[64,16,128]{2,1,0:T(8,128)(2,1)}), bf16[64,16,128]{2,1,0:T(8,128)(2,1)S(1)}, u32[]{:S(2)}, u32[]{:S(2)}) async-start(bf16[64,16,128]{2,1,0:T(8,128)(2,1)} %scan.1), calls=%async_computation.2 | async-start | bytes 524288 | tf_op jit(solution)/shard_map/all_to_all | solution.py:220
  86.9 14.0 %all-to-all-start.3 = ((bf16[4,128,1024]{2,1,0:T(8,128)(2,1)}), bf16[4,128,1024]{2,1,0:T(8,128)(2,1)S(1)}, u32[]{:S(2)}, u32[]{:S(2)}) async-start(bf16[4,128,1024]{2,1,0:T(8,128)(2,1)} %hidden.1), calls=%async_computation.3 | async-start | bytes 2097152 | tf_op jit(solution)/shard_map/all_to_all | solution.py:225
  102.8 10.3 %collective-permute-start = (bf16[4,4,128,128]{3,2,1,0:T(8,128)(2,1)S(1)}, bf16[4,4,128,128]{3,2,1,0:T(8,128)(2,1)S(1)}, u32[]{:S(2)}, u32[]{:S(2)}) collective-permute-start(bf16[4,4,128,128]{3,2,1,0:T(8,128)(2,1)S(1)} %other.1), channel_id=1, source_target_pairs={{0,1},{1,0},{2,3},{3,2},{4,5},{5,4},{6,7},{7,6},{8,9},{9,8},{10,11... | collective-permute-start | bytes 1572872 | tf_op jit(solution)/shard_map/ppermute | solution.py:227
Sparse Core Ops, SparseCore 0:
  18.7 81.8 all-gather.1

commit v12 on v10

--- a/solution.py
+++ b/solution.py
@@ -85,11 +85,11 @@
 
 def scan_kernel(got_ref, out_ref):
     state = jnp.zeros((CHUNK, N), f32)
+    pieces = got_ref[:, PAIRS, :, :].astype(f32)
+    decays = jnp.exp(pieces[:, 0, :] + pieces[:, 1, :])
     for k in range(CTX):
         out_ref[k, :, :] = state.astype(bf16)
-        pieces = got_ref[k, PAIRS, :, :].astype(f32)
-        decay = jnp.exp(pieces[0:1] + pieces[1:2])
-        state = decay * state + got_ref[k, :PAIRS, :, :].reshape(CHUNK, N).astype(f32)
+        state = decays[k : k + 1] * state + got_ref[k, :PAIRS, :, :].reshape(CHUNK, N).astype(f32)
 
 
 def inner_kernel(x_ref, b_ref, c_ref, step_ref, logs_ref, skip_ref, out_ref, scale_ref):

time: 138 us -> 138 us (level)
  no operation moved by 1% of the time
where the time goes in v12:
time: 138 us; the launch traced here: 137 us
  blocking collectives  66.6 us (48%)
  starting transfers between devices  22.3 us (16%)
  waiting for transfers between devices  22.2 us (16%)
  between operations  13.5 us (10%)
  Pallas kernels  10.6 us (8%)
  local copies, waits for them, and re-layouts  1.78 us (1%)
    all_to_all x1, blocking collectives, shards(): got = lax.all_to_all(send, ('x', 'z'), 0, 0, tiled=True)  36.5 us
    all_to_all x1, waiting for transfers between devices, shards(): states = lax.all_to_all(entering, ('x', 'z'), 0, 0, tiled=True)  19.7 us
    all_to_all x1, blocking collectives, shards(): lax.all_to_all(parts.reshape(NX * NY, TOK, COLS), ('x', 'y'), 0, 0, tiled...  16.3 us
    all_to_all x1, blocking collectives, shards(): everyone = lax.all_to_all(hidden, 'x', 0, 0, tiled=True)  13.9 us
    ppermute x1, starting transfers between devices, shards(): other = lax.ppermute(other, 'c', [(0, 1), (1, 0)])  8.75 us
    all_to_all x1, starting transfers between devices, shards(): states = lax.all_to_all(entering, ('x', 'z'), 0, 0, tiled=True)  8.7 us
    all_to_all x1, starting transfers between devices, shards(): swap = lax.all_to_all(swap, 'x', 0, 0, tiled=True)  4.84 us
    pallas_call x2, Pallas kernels, product(): pl.pallas_call(functools.partial(product_kernel, half), out_shape=shape(N...  3.76 us
  transfers between devices with their start and end apart: 4, of which 3 were waited for; matrix products, arithmetic and copies ran while one was open for 0% of the time, Pallas kernels for 5%

profile of v12, /device:TPU:1, one launch (start us, length us, event | category | flops | bytes accessed | tf_op | source)
XLA Modules:
  0.0 137.0 jit_solution(16400564271910289113)
XLA Ops:
  6.5 0.9 copy-done.1
  7.5 0.0 copy-start.5
  7.5 0.7 pack.1
  8.2 4.8 %all-to-all-start = ((bf16[4,16,1024]{2,1,0:T(8,128)(2,1)}), bf16[4,16,1024]{2,1,0:T(8,128)(2,1)S(1)}, u32[]{:S(2)}, u32[]{:S(2)}) async-start(bf16[4,16,1024]{2,1,0:T(8,128)(2,1)} %pack.1), calls=%async_computation | async-start | bytes 262144 | tf_op jit(solution)/shard_map/all_to_all | solution.py:198
  13.0 2.8 %fresh.1 = bf16[64,9,2,128]{3,2,1,0:T(2,128)(2,1)} custom-call(bf16[128,1024]{1,0:T(8,128)(2,1)} %x_ref.3, bf16[128,128]{1,0:T(8,128)(2,1)} %b_ref.3, f32[16,128]{1,0:T(8,128)} %step_ref.3, f32[16,128]{1,0:T(8,128)} %logs_ref.3), custom_call_target="tpu_custom_call" | custom-call | flops 40000000 | bytes 1000000 | tf_op jit(solution)/shard_map/fresh/pallas_call | solution.py:200
  15.9 2.0 %all-to-all-done = bf16[4,16,1024]{2,1,0:T(8,128)(2,1)S(1)} async-done(((bf16[4,16,1024]{2,1,0:T(8,128)(2,1)}), bf16[4,16,1024]{2,1,0:T(8,128)(2,1)S(1)}, u32[]{:S(2)}, u32[]{:S(2)}) %all-to-all-start) | async-done | bytes 131104 | tf_op jit(solution)/shard_map/all_to_all | solution.py:198
  17.9 0.7 copy-done.7
  18.5 0.0 all-gather.2.cloned.1.call-update
  18.6 36.5 %all_to_all.25.got_ref = bf16[64,9,2,128]{3,2,1,0:T(2,128)(2,1)S(1)} all-to-all(bf16[64,9,2,128]{3,2,1,0:T(2,128)(2,1)} %fresh.1), channel_id=1, replica_groups=mesh['x'=4,'z'=16,'y'=4,'c'=2] {'x','z'}, dimensions={0} | all-to-all | bytes 589824 | tf_op jit(solution)/shard_map/all_to_all | solution.py:208
  55.0 1.0 scan.1
  56.0 8.7 %all-to-all-start.2 = ((bf16[64,16,128]{2,1,0:T(8,128)(2,1)}), bf16[64,16,128]{2,1,0:T(8,128)(2,1)S(1)}, u32[]{:S(2)}, u32[]{:S(2)}) async-start(bf16[64,16,128]{2,1,0:T(8,128)(2,1)} %scan.1), calls=%async_computation.2 | async-start | bytes 524288 | tf_op jit(solution)/shard_map/all_to_all | solution.py:217
  64.7 0.1 broadcast_in_dim.9
  64.8 0.1 broadcast_in_dim_reshape.3.skip_ref
  64.9 1.2 inner.1
  66.0 19.7 %all-to-all-done.2.state_ref = bf16[64,16,128]{2,1,0:T(8,128)(2,1)S(1)} async-done(((bf16[64,16,128]{2,1,0:T(8,128)(2,1)}), bf16[64,16,128]{2,1,0:T(8,128)(2,1)S(1)}, u32[]{:S(2)}, u32[]{:S(2)}) %all-to-all-start.2) | async-done | bytes 262176 | tf_op jit(solution)/shard_map/all_to_all | solution.py:217
  85.8 0.4 hidden.1
  86.1 13.9 %all_to_all.26.hidden_ref = bf16[4,128,1024]{2,1,0:T(8,128)(2,1)S(1)} all-to-all(bf16[4,128,1024]{2,1,0:T(8,128)(2,1)S(1)} %hidden.1), channel_id=1, replica_groups=mesh['x'=4,'z'=16,'y'=4,'c'=2] {'x'}, dimensions={0} | all-to-all | bytes 2097152 | tf_op jit(solution)/shard_map/all_to_all | solution.py:222
  100.0 0.4 all-gather.2.cloned.1.call-done
  100.4 1.9 %other.1 = bf16[4,4,128,128]{3,2,1,0:T(8,128)(2,1)S(1)} custom-call(bf16[4,128,1024]{2,1,0:T(8,128)(2,1)S(1)} %all_to_all.26.hidden_ref, bf16[16,4,16,1024]{3,2,1,0:T(8,128)(2,1)} %bitcast.17), custom_call_target="tpu_custom_call" | custom-call | flops 536870912 | bytes 3000000 | tf_op jit(solution)/shard_map/other/pallas_call | solution.py:170
  102.3 8.8 %collective-permute-start = (bf16[4,4,128,128]{3,2,1,0:T(8,128)(2,1)S(1)}, bf16[4,4,128,128]{3,2,1,0:T(8,128)(2,1)S(1)}, u32[]{:S(2)}, u32[]{:S(2)}) collective-permute-start(bf16[4,4,128,128]{3,2,1,0:T(8,128)(2,1)S(1)} %other.1), channel_id=1, source_target_pairs={{0,1},{1,0},{2,3},{3,2},{4,5},{5,4},{6,7},{7,6},{8,9},{9,8},{10,11... | collective-permute-start | bytes 1572872 | tf_op jit(solution)/shard_map/ppermute | solution.py:224
  111.1 1.9 %mine.1.mine_ref = f32[4,4,128,128]{3,2,1,0:T(8,128)S(1)} custom-call(bf16[4,128,1024]{2,1,0:T(8,128)(2,1)S(1)} %all_to_all.26.hidden_ref, bf16[16,4,16,1024]{3,2,1,0:T(8,128)(2,1)} %bitcast.18), custom_call_target="tpu_custom_call" | custom-call | flops 536870912 | bytes 3000000 | tf_op jit(solution)/shard_map/mine/pallas_call | solution.py:170
  113.0 0.1 pair.1
  113.1 16.3 %all_to_all.27 = bf16[16,128,128]{2,1,0:T(8,128)(2,1)S(1)} all-to-all(bf16[16,128,128]{2,1,0:T(8,128)(2,1)S(1)} %bitcast.15), channel_id=1, replica_groups=mesh['x'=4,'z'=16,'y'=4,'c'=2] {'x','y'}, dimensions={0} | all-to-all | bytes 1048576 | tf_op jit(solution)/shard_map/all_to_all | solution.py:227
  129.4 0.7 sum.1
  (17 shorter events, 0.0 us)
Async XLA Ops:
  6.5 58.3 %copy-start = (bf16[128,1024]{1,0:T(8,128)(2,1)S(1)}, bf16[128,1024]{1,0:T(8,128)(2,1)}, u32[]{:S(2)}) copy-start(bf16[128,1024]{1,0:T(8,128)(2,1)} %x_ref.3) | copy-start | bytes 786436
  6.5 0.9 copy-start.1
  7.5 57.2 %copy-start.8 = (f32[16]{0:T(128)S(1)}, f32[16]{0:T(128)}, u32[]{:S(2)}) copy-start(f32[16]{0:T(128)} %param.13) | copy-start | bytes 196
  7.5 57.4 %copy-start.2 = (bf16[128,128]{1,0:T(8,128)(2,1)S(1)}, bf16[128,128]{1,0:T(8,128)(2,1)}, u32[]{:S(2)}) copy-start(bf16[128,128]{1,0:T(8,128)(2,1)} %c_ref.3) | copy-start | bytes 98308
  7.5 57.4 %copy-start.3 = (bf16[128,128]{1,0:T(8,128)(2,1)S(1)}, bf16[128,128]{1,0:T(8,128)(2,1)}, u32[]{:S(2)}) copy-start(bf16[128,128]{1,0:T(8,128)(2,1)} %b_ref.3) | copy-start | bytes 98308
  7.5 57.4 %copy-start.4 = (f32[16,128]{1,0:T(8,128)S(1)}, f32[16,128]{1,0:T(8,128)}, u32[]{:S(2)}) copy-start(f32[16,128]{1,0:T(8,128)} %step_ref.3) | copy-start | bytes 24580
  7.5 57.4 %copy-start.5 = (f32[16,128]{1,0:T(8,128)S(1)}, f32[16,128]{1,0:T(8,128)}, u32[]{:S(2)}) copy-start(f32[16,128]{1,0:T(8,128)} %logs_ref.3) | copy-start | bytes 24580
  7.5 78.2 %copy-start.6 = (f32[1024]{0:T(1024)S(1)}, f32[1024]{0:T(1024)}, u32[]{:S(2)}) copy-start(f32[1024]{0:T(1024)} %param.14) | copy-start | bytes 12292
  8.2 9.7 %all-to-all-start = ((bf16[4,16,1024]{2,1,0:T(8,128)(2,1)}), bf16[4,16,1024]{2,1,0:T(8,128)(2,1)S(1)}, u32[]{:S(2)}, u32[]{:S(2)}) async-start(bf16[4,16,1024]{2,1,0:T(8,128)(2,1)} %pack.1), calls=%async_computation | async-start | bytes 262144 | tf_op jit(solution)/shard_map/all_to_all | solution.py:198
  13.0 87.4 %all-gather.2.cloned.1.call-start = ((), (), s32[]{:S(2)}) async-start(), calls=%async_computation.5 | async-start | bytes 2228224 | tf_op jit(solution)/shard_map/all_gather | solution.py:205
  17.9 0.7 copy-start.7
  56.0 29.8 %all-to-all-start.2 = ((bf16[64,16,128]{2,1,0:T(8,128)(2,1)}), bf16[64,16,128]{2,1,0:T(8,128)(2,1)S(1)}, u32[]{:S(2)}, u32[]{:S(2)}) async-start(bf16[64,16,128]{2,1,0:T(8,128)(2,1)} %scan.1), calls=%async_computation.2 | async-start | bytes 524288 | tf_op jit(solution)/shard_map/all_to_all | solution.py:217
  102.3 10.7 %collective-permute-start = (bf16[4,4,128,128]{3,2,1,0:T(8,128)(2,1)S(1)}, bf16[4,4,128,128]{3,2,1,0:T(8,128)(2,1)S(1)}, u32[]{:S(2)}, u32[]{:S(2)}) collective-permute-start(bf16[4,4,128,128]{3,2,1,0:T(8,128)(2,1)S(1)} %other.1), channel_id=1, source_target_pairs={{0,1},{1,0},{2,3},{3,2},{4,5},{5,4},{6,7},{7,6},{8,9},{9,8},{10,11... | collective-permute-start | bytes 1572872 | tf_op jit(solution)/shard_map/ppermute | solution.py:224
Sparse Core Ops, SparseCore 0:
  18.7 81.7 all-gather.1
